TPU v7x, 128 devices: a whole 4x4x4 slice. The times are simulated.
128 devices in a mesh: dp: 32 (over x, y, core), tensor: 4 (over z).
Axes of the slice: x: 4, y: 4, z: 4, core: 2. Of those that a mesh axis runs over, the one named last changes fastest.
Arguments:
- residual: bfloat16 [512, 7168], P('dp'), may hold values from -6 to 6
- query_latent: bfloat16 [512, 128, 512], P('dp', 'tensor'), may hold values from -64 to 64
- query_rope: bfloat16 [512, 128, 64], P('dp', 'tensor'), may hold values from -6 to 6
- cache_latent: bfloat16 [512, 1024, 512], P('dp'), may hold values from -4 to 4
- cache_rope: bfloat16 [512, 64, 1024], P('dp'), may hold values from -6 to 6
- lengths: int32 [512], P('dp'), may hold values from 256 to 1024, as said below
- value_up: bfloat16 [128, 512, 128], P('tensor'), may hold values from -0.25 to 0.25
- out_proj: bfloat16 [16384, 7168], P('tensor', 'dp'), may hold values from -0.5 to 0.5
- gate_proj: bfloat16 [32, 7168, 1024], P('dp', None, 'tensor'), may hold values from -0.0625 to 0.0625
- up_proj: bfloat16 [32, 7168, 1024], P('dp', None, 'tensor'), may hold values from -0.0625 to 0.0625
- down_proj: bfloat16 [32, 1024, 7168], P('dp', 'tensor'), may hold values from -0.1875 to 0.1875
- groups: int32 [512, 4], P('dp'), may hold values from 0 to 7, as said below
- expert_picks: int32 [512, 8], P('dp'), may hold values from 0 to 15, as said below
- gate_levels: int32 [512, 8], P('dp'), may hold values from 1 to 255
Outputs:
- layer_out: bfloat16 [512, 7168], P('dp')
Inputs may be any that keep to these rules, and one draw needn't show every extreme that they name: Row r attends to cache positions 0 to lengths[r] - 1; in every draw some row has length 1024. Each row names 4 different groups; among the rows of one index of dp no group is named by more than 8 rows. `expert_picks`: each row's 8 entries differ, so its experts differ. Among the rows of one index of dp no expert is named by more than 8 rows; in every draw one expert is named by exactly 8 rows of every index of dp.
All inputs are finite; a program needn't handle non-finite values.
Results may differ from a plain program's by a relative error of at most 0.02.
Values may be sent and summed in bfloat16 or wider, within the bound.
No kernel may reach another device: no remote copies, remote signals or barrier semaphores. Data moves between devices by JAX's collectives and lax.ppermute only.
A program may use at most 128 MiB of HBM per device.

v0:
```python
import jax
import jax.numpy as jnp
from jax import lax
from jax.sharding import PartitionSpec as P

TOPG = 4


score_scale = 192.0 ** (-0.5)
route_scale = 2.5
far_below = -1e30


def attend_rows(query_latent, query_rope, cache_latent, cache_rope, lengths):
    positions = cache_latent.shape[1]
    latent_term = jnp.einsum(
        "bhl,bsl->bhs", query_latent, cache_latent, preferred_element_type=jnp.float32
    )
    rope_term = jnp.einsum(
        "bhi,bis->bhs", query_rope, cache_rope, preferred_element_type=jnp.float32
    )
    scores = (latent_term + rope_term) * score_scale
    visible = jnp.arange(positions)[None, None, :] < lengths[:, None, None]
    scores = jnp.where(visible, scores, far_below)
    highest = jnp.max(scores, axis=2, keepdims=True)
    raised = jnp.exp(scores - highest)
    weights = (raised / jnp.sum(raised, axis=2, keepdims=True)).astype(jnp.bfloat16)
    mixture = jnp.einsum("bhs,bsl->bhl", weights, cache_latent, preferred_element_type=jnp.float32)
    return mixture.astype(jnp.bfloat16)


def route_tables(groups, expert_picks, gate_levels, owners):
    group_count = min(8, owners // 2)
    per_group = owners // group_count
    slot_group = expert_picks // per_group
    slot_range = jnp.arange(groups.shape[1], dtype=jnp.int32)
    picked_group = jnp.sum(
        jnp.where(slot_group[:, :, None] == slot_range[None, None, :], groups[:, None, :], 0),
        axis=2,
    )
    expert_ids = picked_group * per_group + expert_picks % per_group
    levels = gate_levels.astype(jnp.float32)
    gates = route_scale * levels / jnp.sum(levels, axis=1, keepdims=True)
    expert_range = jnp.arange(owners, dtype=jnp.int32)
    matches = expert_ids[:, :, None] == expert_range[None, None, :]
    coefficients = jnp.sum(jnp.where(matches, gates[:, :, None], 0.0), axis=1)
    selected = jnp.any(matches, axis=1)
    level_for = jnp.sum(jnp.where(matches, gate_levels[:, :, None], 0), axis=1)
    return (coefficients, selected, level_for)


def slot_table(member, capacity):
    counts = member.astype(jnp.int32)
    ranking = jnp.cumsum(counts, axis=0) - counts
    placed = member[:, :, None] & (
        ranking[:, :, None] == jnp.arange(capacity, dtype=jnp.int32)[None, None, :]
    )
    return jnp.transpose(placed, (1, 2, 0)).astype(jnp.float32)


def expert_block(arrivals, gate_weight, up_weight, down_weight):
    gated = jnp.einsum("sid,df->sif", arrivals, gate_weight, preferred_element_type=jnp.float32)
    upward = jnp.einsum("sid,df->sif", arrivals, up_weight, preferred_element_type=jnp.float32)
    activation = (jax.nn.silu(gated) * upward).astype(jnp.bfloat16)
    produced = jnp.einsum(
        "sif,fd->sid", activation, down_weight, preferred_element_type=jnp.float32
    )
    return lax.psum(produced.astype(jnp.bfloat16), "tensor")


def local(
    residual,
    query_latent,
    query_rope,
    cache_latent,
    cache_rope,
    lengths,
    value_up,
    out_proj,
    gate_proj,
    up_proj,
    down_proj,
    groups,
    expert_picks,
    gate_levels,
):
    row_count, model_width = residual.shape
    owners = lax.axis_size("dp")
    group_count = min(8, owners // 2)
    capacity = min(row_count, TOPG * ((row_count + group_count - 1) // group_count))
    latent_mix = attend_rows(query_latent, query_rope, cache_latent, cache_rope, lengths)
    head_out = jnp.einsum(
        "bhl,hlv->bhv", latent_mix, value_up, preferred_element_type=jnp.float32
    ).astype(jnp.bfloat16)
    head_out = head_out.reshape(row_count, -1)
    column_terms = jnp.dot(
        lax.all_gather(head_out, "dp", axis=0, tiled=True),
        out_proj,
        preferred_element_type=jnp.float32,
    )
    summed_terms = lax.psum(column_terms, "tensor")
    attention = lax.all_to_all(
        summed_terms.astype(jnp.bfloat16), "dp", split_axis=0, concat_axis=1, tiled=True
    )
    hidden = (residual.astype(jnp.float32) + attention.astype(jnp.float32)).astype(jnp.bfloat16)
    coefficients, selected, level_for = route_tables(groups, expert_picks, gate_levels, owners)
    gate_weight = gate_proj[0]
    up_weight = up_proj[0]
    down_weight = down_proj[0]
    slot_place = slot_table(selected, capacity)
    outgoing = jnp.einsum(
        "ecr,rd->ecd", slot_place.astype(jnp.bfloat16), hidden, preferred_element_type=jnp.float32
    ).astype(jnp.bfloat16)
    produced = expert_block(
        lax.all_to_all(outgoing, "dp", split_axis=0, concat_axis=0, tiled=True),
        gate_weight,
        up_weight,
        down_weight,
    )
    returned = lax.all_to_all(produced, "dp", split_axis=0, concat_axis=0, tiled=True)
    weighting = slot_place * jnp.transpose(coefficients)[:, None, :]
    routed = jnp.einsum(
        "ecr,ecd->rd", weighting, returned.astype(jnp.float32), precision=lax.Precision.HIGHEST
    )
    return (hidden.astype(jnp.float32) + routed).astype(jnp.bfloat16)


def solution(mesh):
    return jax.shard_map(
        local,
        mesh=mesh,
        in_specs=(
            P("dp", None),
            P("dp", "tensor", None),
            P("dp", "tensor", None),
            P("dp", None, None),
            P("dp", None, None),
            P("dp"),
            P("tensor", None, None),
            P("tensor", "dp"),
            P("dp", None, "tensor"),
            P("dp", None, "tensor"),
            P("dp", "tensor", None),
            P("dp", None),
            P("dp", None),
            P("dp", None),
        ),
        out_specs=P("dp", None),
        check_vma=False,
    )
```

profile of v0, /device:TPU:0, one launch (start us, length us, event | category | flops | bytes accessed | tf_op | source)
XLA Modules:
  0.0 337.3 jit_solution(5564416044865030700)
XLA Ops:
  6.5 0.9 iota_compare_fusion.2
  7.4 0.7 copy-done
  8.1 2.7 fusion.34
  10.8 11.3 %multiply_select_fusion = f32[16,32,1024]{2,1,0:T(8,128)S(1)} fusion(f32[16,32,1024]{2,1,0:T(8,128)} %fusion.34, bf16[16,32,512]{2,1,0:T(8,128)(2,1)S(1)} %copy-done.3, bf16[16,1024,512]{2,1,0:T(8,128)(2,1)} %param.17, pred[16,1024]{1,0:T(8,128)(4,1)S(1)} %iota_compare_fusion.2), kind=kOutput, calls=%fused_computation.14 | convolution fusion | flops 538443776 | bytes 21512192 | tf_op jit(solution)/shard_map/bhl,bsl->bhs/dot_general | solution.py:16
  22.2 0.5 fusion.33
  22.6 8.8 %convolution_convert_fusion.2 = bf16[16,32,512]{2,1,0:T(8,128)(2,1)S(1)} fusion(bf16[16,1024,512]{2,1,0:T(8,128)(2,1)} %param.17, f32[16,32]{1,0:T(8,128)S(1)} %fusion.33, f32[16,32,1024]{2,1,0:T(8,128)S(1)} %multiply_select_fusion), kind=kOutput, calls=%fused_computation.15 | convolution fusion | flops 538707456 | bytes 19400704 | tf_op jit(solution)/shard_map/bhs,bsl->bhl/dot_general | solution.py:28
  31.5 3.1 fusion.15
  34.5 0.7 copy.59
  35.4 0.1 fusion.21
  35.5 48.3 %all-gather.2.cloned.1.call-done = bf16[512,4096]{1,0:T(8,128)(2,1)} async-done(((bf16[16,4096]{1,0:T(8,128)(2,1)}), bf16[512,4096]{1,0:T(8,128)(2,1)}) %all-gather.2.cloned.1.call-update) | async-done | bytes 4194320 | tf_op jit(solution)/shard_map/all_gather | solution.py:97
  83.8 4.2 %fusion.35 = f32[512,224]{0,1:T(8,128)S(1)} fusion(bf16[512,4096]{1,0:T(8,128)(2,1)} %all-gather.2.cloned.1.call-done, bf16[4096,224]{0,1:T(8,128)(2,1)} %param.21), kind=kOutput, calls=%fused_computation.57 | convolution fusion | flops 939524096 | bytes 6488064 | tf_op jit(solution)/shard_map/dot_general | solution.py:96
  88.0 22.5 %all-reduce.4 = bf16[512,224]{0,1:T(8,128)(2,1)S(1)} all-reduce(f32[512,224]{0,1:T(8,128)S(1)} %fusion.35), channel_id=1, replica_groups=mesh['dp'=32,'tensor'=4] {'tensor'}, use_global_device_ids=true, to_apply=%region_2.3 | all-reduce | flops 114688 | bytes 688128 | tf_op jit(solution)/shard_map/psum | solution.py:101
  110.5 0.8 copy.43
  111.3 5.2 %all-to-all-start = ((bf16[32,16,224]{2,1,0:T(8,128)(2,1)}), bf16[32,16,224]{2,1,0:T(8,128)(2,1)S(1)}, u32[]{:S(2)}, u32[]{:S(2)}) async-start(bf16[32,16,224]{2,1,0:T(8,128)(2,1)} %bitcast.1), calls=%async_computation | async-start | bytes 524288 | tf_op jit(solution)/shard_map/all_to_all | solution.py:102
  116.7 0.1 copy.47
  116.8 8.8 %all-to-all-done = bf16[32,16,224]{2,1,0:T(8,128)(2,1)S(1)} async-done(((bf16[32,16,224]{2,1,0:T(8,128)(2,1)}), bf16[32,16,224]{2,1,0:T(8,128)(2,1)S(1)}, u32[]{:S(2)}, u32[]{:S(2)}) %all-to-all-start) | async-done | bytes 229408 | tf_op jit(solution)/shard_map/all_to_all | solution.py:102
  125.6 0.3 copy.44
  125.9 0.3 reshape.51
  126.2 1.1 convolution_convert_fusion.1
  127.3 48.6 %all_to_all.23 = bf16[32,8,7168]{2,1,0:T(8,128)(2,1)S(1)} all-to-all(bf16[32,8,7168]{2,1,0:T(8,128)(2,1)S(1)} %convolution_convert_fusion.1), channel_id=1, replica_groups=mesh['dp'=32,'tensor'=4] {'dp'}, dimensions={0} | all-to-all | bytes 7340032 | tf_op jit(solution)/shard_map/all_to_all | solution.py:115
  176.0 1.1 fusion.6
  177.1 0.9 copy-done.9
  178.0 1.1 fusion.12
  179.1 0.9 copy-done.2
  180.0 3.0 convolution_convert_fusion
  183.0 81.3 %all-reduce.3.cloned.1.call-done = bf16[32,8,7168]{2,0,1:T(8,128)(2,1)} async-done(((bf16[32,8,7168]{2,0,1:T(8,128)(2,1)}), bf16[32,8,7168]{2,0,1:T(8,128)(2,1)}) %all-reduce.3.cloned.1.call-update) | async-done | bytes 3670032 | tf_op jit(solution)/shard_map/psum | solution.py:68
  264.3 5.9 %copy.49 = bf16[32,8,7168]{2,1,0:T(8,128)(2,1)} copy(bf16[32,8,7168]{2,0,1:T(8,128)(2,1)} %all-reduce.3.cloned.1.call-done) | data formatting | bytes 7340032 | tf_op jit(solution)/shard_map/psum | solution.py:68
  270.2 7.3 %all-to-all-start.2 = ((bf16[32,8,7168]{2,1,0:T(8,128)(2,1)}), bf16[32,8,7168]{2,1,0:T(8,128)(2,1)}, u32[]{:S(2)}, u32[]{:S(2)}) async-start(bf16[32,8,7168]{2,1,0:T(8,128)(2,1)} %copy.49), calls=%async_computation.2 | async-start | bytes 7340032 | tf_op jit(solution)/shard_map/all_to_all | solution.py:120
  277.6 0.1 copy.46
  277.7 0.1 select_reduce_fusion
  277.8 46.3 %all-to-all-done.2 = bf16[32,8,7168]{2,1,0:T(8,128)(2,1)} async-done(((bf16[32,8,7168]{2,1,0:T(8,128)(2,1)}), bf16[32,8,7168]{2,1,0:T(8,128)(2,1)}, u32[]{:S(2)}, u32[]{:S(2)}) %all-to-all-start.2) | async-done | bytes 3670048 | tf_op jit(solution)/shard_map/all_to_all | solution.py:120
  324.1 6.4 %fusion.2 = bf16[16,7168]{1,0:T(8,128)(2,1)} fusion(bf16[32,8,7168]{2,1,0:T(8,128)(2,1)} %all-to-all-done.2, f32[32,16]{0,1:T(8,128)S(1)} %bitcast.55, s32[32,16]{0,1:T(8,128)S(1)} %bitcast_subtract_fusion, pred[32,16]{0,1:T(8,128)(4,1)S(1)} %bitcast.54, f32[16,7168]{1,0:T(8,128)S(1)} %reshape.51, bf16[16,7168]{1,0:T(8,128)(2,1)S(1)} %copy-done.4), kind=kOutput, calls=%fused_computation.5 | convolution fusion | flops 353021952 | bytes 4592128 | tf_op jit(solution)/shard_map/ecr,ecd->rd/dot_general | solution.py:122
  (32 shorter events, 0.4 us)
Async XLA Ops:
  6.5 1.6 copy-start
  6.5 4.3 %copy-start.3 = (bf16[16,32,512]{2,1,0:T(8,128)(2,1)S(1)}, bf16[16,32,512]{2,1,0:T(8,128)(2,1)}, u32[]{:S(2)}) copy-start(bf16[16,32,512]{2,1,0:T(8,128)(2,1)} %param.15) | copy-start | bytes 1572868
  6.5 77.2 %all-gather.2.cloned.1.call-start = ((), (), s32[]{:S(2)}) async-start(), calls=%async_computation.3 | async-start | bytes 4325376 | tf_op jit(solution)/shard_map/all_gather | solution.py:97
  31.4 3.8 %copy-start.5 = (s32[16,8]{0,1:T(8,128)S(1)}, s32[16,8]{0,1:T(8,128)}, u32[]{:S(2)}) copy-start(s32[16,8]{0,1:T(8,128)} %param.26) | copy-start | bytes 1540
  31.4 3.8 %copy-start.7 = (s32[16,4]{0,1:T(4,128)S(1)}, s32[16,4]{0,1:T(4,128)}, u32[]{:S(2)}) copy-start(s32[16,4]{0,1:T(4,128)} %param.25) | copy-start | bytes 772
  88.0 38.2 %copy-start.4 = (bf16[16,7168]{1,0:T(8,128)(2,1)S(1)}, bf16[16,7168]{1,0:T(8,128)(2,1)}, u32[]{:S(2)}) copy-start(bf16[16,7168]{1,0:T(8,128)(2,1)} %param.14) | copy-start | bytes 688132
  111.3 14.2 %all-to-all-start = ((bf16[32,16,224]{2,1,0:T(8,128)(2,1)}), bf16[32,16,224]{2,1,0:T(8,128)(2,1)S(1)}, u32[]{:S(2)}, u32[]{:S(2)}) async-start(bf16[32,16,224]{2,1,0:T(8,128)(2,1)} %bitcast.1), calls=%async_computation | async-start | bytes 524288 | tf_op jit(solution)/shard_map/all_to_all | solution.py:102
  116.6 147.7 %all-reduce.3.cloned.1.call-start = ((), (), s32[]{:S(2)}) async-start(), calls=%async_computation.4 | async-start | bytes 7340032 | tf_op jit(solution)/shard_map/psum | solution.py:68
  127.3 48.6 %copy-start.8 = (bf16[1,7168,256]{2,1,0:T(8,128)(2,1)S(1)}, bf16[1,7168,256]{2,1,0:T(8,128)(2,1)}, u32[]{:S(2)}) copy-start(bf16[1,7168,256]{2,1,0:T(8,128)(2,1)} %param.22) | copy-start | bytes 11010052
  175.9 2.0 copy-start.9
  178.0 2.0 copy-start.2
  270.2 7.4 %copy-start.6 = (s32[16,8]{0,1:T(8,128)S(1)}, s32[16,8]{0,1:T(8,128)}, u32[]{:S(2)}) copy-start(s32[16,8]{0,1:T(8,128)} %param.27) | copy-start | bytes 1540
  270.2 53.9 %all-to-all-start.2 = ((bf16[32,8,7168]{2,1,0:T(8,128)(2,1)}), bf16[32,8,7168]{2,1,0:T(8,128)(2,1)}, u32[]{:S(2)}, u32[]{:S(2)}) async-start(bf16[32,8,7168]{2,1,0:T(8,128)(2,1)} %copy.49), calls=%async_computation.2 | async-start | bytes 7340032 | tf_op jit(solution)/shard_map/all_to_all | solution.py:120
  277.6 52.9 %copy-start.1 = (bf16[16,64,1024]{2,1,0:T(8,128)(2,1)S(1)}, bf16[16,64,1024]{2,1,0:T(8,128)(2,1)}, u32[]{:S(2)}) copy-start(bf16[16,64,1024]{2,1,0:T(8,128)(2,1)} %param.18) | copy-start | bytes 6291460
Sparse Core Ops, SparseCore 0:
  35.3 48.3 all-gather.1
  183.1 81.1 all-reduce.2
where the time goes:
time: 338 us; the launch traced here: 337 us
  waiting for transfers between devices  185 us (55%)
  blocking collectives  71.1 us (21%)
  matrix products  42.7 us (13%)
  between operations  13.6 us (4%)
  starting transfers between devices  12.6 us (4%)
  local copies, waits for them, and re-layouts  10.8 us (3%)
    psum x1, waiting for transfers between devices, expert_block(): return lax.psum(produced.astype(jnp.bfloat16), 'tensor')  81.3 us
    all_to_all x1, blocking collectives, local(): lax.all_to_all(outgoing, 'dp', split_axis=0, concat_axis=0, tiled=True)  48.6 us
    all_gather x1, waiting for transfers between devices, local(): lax.all_gather(head_out, 'dp', axis=0, tiled=True)  48.3 us
    all_to_all x1, waiting for transfers between devices, local(): lax.all_to_all(produced, 'dp', split_axis=0, concat_axis=0, tiled=True)  46.3 us
    psum x1, blocking collectives, local(): summed_terms = lax.psum(column_terms, 'tensor')  22.5 us
    dot_general x1, matrix products, attend_rows(): jnp.einsum('bhl,bsl->bhs', query_latent, cache_latent, preferred_element_...  11.3 us
    dot_general x1, matrix products, attend_rows(): jnp.einsum('bhs,bsl->bhl', weights, cache_latent, preferred_element_type=...  8.79 us
    all_to_all x1, waiting for transfers between devices, local(): lax.all_to_all(summed_terms.astype(jnp.bfloat16), 'dp', split_axis=0, con...  8.75 us
  transfers between devices with their start and end apart: 4, of which 4 were waited for; matrix products, arithmetic and copies ran while one was open for 0% of the time, Pallas kernels for 0%

commit v1 on v0

v1 whole, which is shorter than its diff:
```python
import jax
import jax.numpy as jnp
from jax import lax
from jax.experimental import pallas as pl
from jax.experimental.pallas import tpu as pltpu
from jax.sharding import PartitionSpec as P

SIDE = 4
CORES = 2
CHIPS = SIDE * SIDE
PLANES = 4
TOPG = 4
GROUPS = 8
EPG = 4
CAP = 8

score_scale = 192.0 ** (-0.5)
route_scale = 2.5
far_below = -1e30

f32 = jnp.float32
bf16 = jnp.bfloat16


def dp_index(x, y, c):
    return (x * SIDE + y) * CORES + c


def shift_pairs(dx, dy, dc):
    pairs = []
    for x in range(SIDE):
        for y in range(SIDE):
            for c in range(CORES):
                pairs.append(
                    (dp_index(x, y, c), dp_index((x + dx) % SIDE, (y + dy) % SIDE, (c + dc) % CORES))
                )
    return pairs


def move_x(value, by):
    return lax.ppermute(value, "dp", shift_pairs(by, 0, 0))


def move_y(value, by):
    return lax.ppermute(value, "dp", shift_pairs(0, by, 0))


def move_core(value):
    return lax.ppermute(value, "dp", shift_pairs(0, 0, 1))


def move_z(value, by):
    return lax.ppermute(value, "tensor", [(z, (z + by) % PLANES) for z in range(PLANES)])


def chip_exchange(value):
    groups = [[dp_index(x, y, c) for x in range(SIDE) for y in range(SIDE)] for c in range(CORES)]
    return lax.all_to_all(
        value, "dp", split_axis=0, concat_axis=0, axis_index_groups=groups, tiled=True
    )


ROWS_STEP = 2


def attend_kernel(lengths, q_ref, qr_ref, k_ref, r_ref, vu_hbm, out_ref, mix_ref, vu_ref, sem):
    step = pl.program_id(0)
    copy = pltpu.make_async_copy(vu_hbm, vu_ref, sem)

    @pl.when(step == 0)
    def _():
        copy.start()

    heads = q_ref.shape[1]
    for i in range(ROWS_STEP):
        row = step * ROWS_STEP + i
        keys = k_ref[i]
        scores = lax.dot_general(
            q_ref[i], keys, (((1,), (1,)), ((), ())), preferred_element_type=f32
        )
        scores = scores + jnp.dot(qr_ref[i], r_ref[i], preferred_element_type=f32)
        scores = scores * score_scale
        place = lax.broadcasted_iota(jnp.int32, scores.shape, 1)
        scores = jnp.where(place < lengths[row], scores, far_below)
        highest = jnp.max(scores, axis=1, keepdims=True)
        raised = jnp.exp(scores - highest)
        weights = (raised / jnp.sum(raised, axis=1, keepdims=True)).astype(bf16)
        mix = jnp.dot(weights, keys, preferred_element_type=f32)
        at = pl.ds(pl.multiple_of(row * heads, heads), heads)
        for j in range(mix_ref.shape[0]):
            mix_ref[j, at, :] = mix[:, j * 128 : (j + 1) * 128]

    @pl.when(step == pl.num_programs(0) - 1)
    def _():
        copy.wait()
        rows = out_ref.shape[0]
        width = vu_ref.shape[2]
        for h in range(heads):
            left = [mix_ref[j, pl.ds(h, rows, stride=heads), :] for j in range(mix_ref.shape[0])]
            left = jnp.concatenate(left, axis=1).astype(bf16)
            out_ref[:, h * width : (h + 1) * width] = jnp.dot(
                left, vu_ref[h], preferred_element_type=f32
            ).astype(bf16)


def attend(query_latent, query_rope, cache_latent, cache_rope, lengths, value_up):
    rows, heads, lat = query_latent.shape
    rope = query_rope.shape[2]
    positions = cache_latent.shape[1]
    width = value_up.shape[2]
    return pl.pallas_call(
        attend_kernel,
        grid_spec=pltpu.PrefetchScalarGridSpec(
            num_scalar_prefetch=1,
            grid=(rows // ROWS_STEP,),
            in_specs=[
                pl.BlockSpec((ROWS_STEP, heads, lat), lambda i, n: (i, 0, 0)),
                pl.BlockSpec((ROWS_STEP, heads, rope), lambda i, n: (i, 0, 0)),
                pl.BlockSpec((ROWS_STEP, positions, lat), lambda i, n: (i, 0, 0)),
                pl.BlockSpec((ROWS_STEP, rope, positions), lambda i, n: (i, 0, 0)),
                pl.BlockSpec(memory_space=pl.ANY),
            ],
            out_specs=pl.BlockSpec((rows, heads * width), lambda i, n: (0, 0)),
            scratch_shapes=[
                pltpu.VMEM((lat // 128, rows * heads, 128), f32),
                pltpu.VMEM((heads, lat, width), bf16),
                pltpu.SemaphoreType.DMA,
            ],
        ),
        out_shape=jax.ShapeDtypeStruct((rows, heads * width), bf16),
        compiler_params=pltpu.CompilerParams(vmem_limit_bytes=32 * 1024 * 1024),
        cost_estimate=pl.CostEstimate(
            flops=4 * rows * heads * positions * lat,
            bytes_accessed=2 * rows * positions * (lat + rope),
            transcendentals=rows * heads * positions,
        ),
        name="attend",
    )(lengths, query_latent, query_rope, cache_latent, cache_rope, value_up)


def route_info(groups, expert_picks, gate_levels):
    rows = groups.shape[0]
    group_range = jnp.arange(GROUPS, dtype=jnp.int32)
    member = jnp.any(groups[:, :, None] == group_range[None, None, :], axis=1).astype(jnp.int32)
    below = jnp.arange(rows)[:, None] >= jnp.arange(rows)[None, :]
    counted = jnp.sum(jnp.where(below[:, :, None], member[None, :, :], 0), axis=1)
    place = counted * member
    places = jnp.repeat(place, 16, axis=1)
    slot_range = jnp.arange(TOPG, dtype=jnp.int32)
    picked = jnp.sum(
        jnp.where((expert_picks // EPG)[:, :, None] == slot_range, groups[:, None, :], 0), axis=2
    )
    expert_ids = picked * EPG + expert_picks % EPG
    experts = jnp.arange(GROUPS * EPG, dtype=jnp.int32)
    level = jnp.sum(
        jnp.where(expert_ids[:, :, None] == experts, gate_levels[:, :, None], 0), axis=1
    )
    home = (groups[:, :1] == group_range[None, :]).astype(jnp.int32)
    levels = jnp.concatenate(
        [level, home, jnp.zeros((rows, 128 - GROUPS * EPG - GROUPS), jnp.int32)], axis=1
    )
    return place, places.astype(bf16), levels.astype(bf16)


def select_kernel(table, p0_ref, p1_ref, p2_ref, p3_ref, res_ref, places_ref, out_ref):
    core = table[CHIPS]
    rows = res_ref.shape[2]
    lane = lax.broadcasted_iota(jnp.int32, (2 * rows, 128), 1)
    wanted = (lane % CAP + 1).astype(f32)
    second = lax.broadcasted_iota(jnp.int32, (2 * rows, 128), 0) >= rows
    right_half = (lane % (2 * CAP) >= CAP) == second

    def of(ref, parity, chip):
        return ref[parity ^ core, table[chip]]

    for pair in range(CHIPS // 2):
        for parity in range(CORES):
            parts = []
            marks = []
            for chip in (2 * pair, 2 * pair + 1):
                even = of(p0_ref, parity, chip).astype(f32) + of(p2_ref, parity, chip).astype(f32)
                odd = of(p1_ref, parity, chip).astype(f32) + of(p3_ref, parity, chip).astype(f32)
                attention = (even + odd).astype(bf16).astype(f32)
                parts.append((res_ref[chip, parity].astype(f32) + attention).astype(bf16))
                marks.append(of(places_ref, parity, chip).astype(f32))
            hidden = jnp.concatenate(parts, axis=0)
            mark = jnp.concatenate(marks, axis=0)
            pick = jnp.where((mark == wanted) & right_half, 1.0, 0.0).astype(bf16)
            chosen = lax.dot_general(
                pick, hidden, (((0,), (0,)), ((), ())), preferred_element_type=f32
            ).astype(bf16)
            at = parity * CHIPS * CAP + pair * 2 * CAP
            for group in range(GROUPS):
                block = chosen[group * 2 * CAP : (group + 1) * 2 * CAP]
                out_ref[2 * group, at : at + 2 * CAP, :] = block
                out_ref[2 * group + 1, at : at + 2 * CAP, :] = block


def select(table, parts, residual, places):
    columns = residual.shape[-1]
    slots = CHIPS * CORES * CAP
    whole = pl.BlockSpec(memory_space=pltpu.VMEM)
    return pl.pallas_call(
        select_kernel,
        in_specs=[pl.BlockSpec(memory_space=pltpu.SMEM)] + [whole] * 6,
        out_specs=whole,
        out_shape=jax.ShapeDtypeStruct((CHIPS, slots, columns), bf16),
        compiler_params=pltpu.CompilerParams(vmem_limit_bytes=32 * 1024 * 1024),
        cost_estimate=pl.CostEstimate(flops=10**9, bytes_accessed=6 * 10**6, transcendentals=0),
        name="select",
    )(table, *parts, residual, places)


def up_kernel(scalars, x_ref, gw_ref, uw_ref, *rest):
    if len(rest) == 1:
        (acc_ref,) = rest
        before = None
    else:
        before, acc_ref = rest
    step = pl.program_id(0)

    @pl.when(step == 0)
    def _():
        if before is None:
            acc_ref[...] = jnp.zeros_like(acc_ref)
        else:
            acc_ref[...] = before[...]

    acc_ref[0] += jnp.dot(x_ref[0], gw_ref[0, 0], preferred_element_type=f32)
    acc_ref[1] += jnp.dot(x_ref[0], uw_ref[0, 0], preferred_element_type=f32)


def up(scalars, which, x, gate_weight, up_weight, before=None):
    chips, slots, columns = x.shape
    units = gate_weight.shape[-1]
    weight = pl.BlockSpec((1, 1, columns, units), lambda i, s: (i, s[which], 0, 0))
    acc = pl.BlockSpec((2, slots, units), lambda i, s: (0, 0, 0))
    return pl.pallas_call(
        up_kernel,
        grid_spec=pltpu.PrefetchScalarGridSpec(
            num_scalar_prefetch=1,
            grid=(chips,),
            in_specs=[pl.BlockSpec((1, slots, columns), lambda i, s: (i, 0, 0)), weight, weight]
            + ([] if before is None else [acc]),
            out_specs=acc,
        ),
        out_shape=jax.ShapeDtypeStruct((2, slots, units), f32),
        compiler_params=pltpu.CompilerParams(vmem_limit_bytes=24 * 1024 * 1024),
        cost_estimate=pl.CostEstimate(
            flops=4 * chips * slots * columns * units, bytes_accessed=10**7, transcendentals=0
        ),
        name="up",
    )(scalars, x, gate_weight, up_weight, *([] if before is None else [before]))


def down_kernel(scalars, acc_ref, w_ref, coef_ref, home_ref, own_ref, other_ref, *rest):
    if len(rest) == 2:
        received, out_ref = None, rest[0]
        act_ref = rest[1]
    else:
        received, out_ref, act_ref = rest
    step = pl.program_id(0)

    @pl.when(step == 0)
    def _():
        gated = acc_ref[0]
        act_ref[...] = (gated / (1.0 + jnp.exp(-gated)) * acc_ref[1]).astype(bf16)

    produced = jnp.dot(act_ref[...], w_ref[...], preferred_element_type=f32) * coef_ref[...]
    core = scalars[0]
    parts = []
    for chip in range(own_ref.shape[0]):
        mine = own_ref[chip].astype(f32)
        theirs = other_ref[chip].astype(f32)
        flip = core == 1
        parts.append(jnp.where(flip, theirs, mine))
        parts.append(jnp.where(flip, mine, theirs))
    hidden = jnp.concatenate(parts, axis=1)
    produced = produced + hidden * home_ref[...]
    if received is not None:
        produced = produced + received[...].astype(f32)
    out_ref[...] = produced.astype(bf16)


def down(scalars, which, acc, down_weight, coef, home, own, other, received=None):
    units, width = down_weight.shape
    chips, slots, columns = own.shape
    half = slots // CORES
    chips_step = 2
    block = chips_step * CORES * columns
    x_spec = pl.BlockSpec((chips_step, half, columns), lambda i, s: (i, s[which], 0))
    out_spec = pl.BlockSpec((half, block), lambda i, s: (0, i))
    column = pl.BlockSpec((half, 1), lambda i, s: (s[which], 0))
    return pl.pallas_call(
        down_kernel,
        grid_spec=pltpu.PrefetchScalarGridSpec(
            num_scalar_prefetch=1,
            grid=(width // block,),
            in_specs=[
                pl.BlockSpec((2, half, units), lambda i, s: (0, s[which], 0)),
                pl.BlockSpec((units, block), lambda i, s: (0, i)),
                column,
                column,
                x_spec,
                x_spec,
            ]
            + ([] if received is None else [out_spec]),
            out_specs=out_spec,
            scratch_shapes=[pltpu.VMEM((half, units), bf16)],
        ),
        out_shape=jax.ShapeDtypeStruct((half, width), bf16),
        compiler_params=pltpu.CompilerParams(vmem_limit_bytes=24 * 1024 * 1024),
        cost_estimate=pl.CostEstimate(
            flops=2 * half * units * width, bytes_accessed=8 * 10**6, transcendentals=half * units
        ),
        name="down",
    )(scalars, acc, down_weight, coef, home, own, other, *([] if received is None else [received]))


def around(value, move):
    return jnp.stack([value, move(value, 1), move(value, 3), move(value, 2)])


ORDER = (0, 1, 3, 2)


def local(
    residual,
    query_latent,
    query_rope,
    cache_latent,
    cache_rope,
    lengths,
    value_up,
    out_proj,
    gate_proj,
    up_proj,
    down_proj,
    groups,
    expert_picks,
    gate_levels,
):
    rows, model = residual.shape
    columns = out_proj.shape[1]
    dp = lax.axis_index("dp")
    z = lax.axis_index("tensor")
    core = dp % CORES
    chip = dp // CORES
    here_x, here_y = chip // SIDE, chip % SIDE

    spread = residual.reshape(rows, CHIPS * CORES, columns).transpose(1, 0, 2)
    residual_columns = lax.all_to_all(spread, "dp", split_axis=0, concat_axis=0, tiled=True)
    residual_columns = residual_columns.reshape(CHIPS, CORES, rows, columns)

    place, places, levels = route_info(groups, expert_picks, gate_levels)
    head_out = attend(query_latent, query_rope, cache_latent, cache_rope, lengths, value_up)

    half = head_out.shape[1] // 2
    first = jnp.concatenate([head_out[:, :half], places], axis=1)
    second = jnp.concatenate([head_out[:, half:], levels], axis=1)
    first = around(around(first, move_x), move_y)
    second = around(around(second, move_y), move_x)
    wide = half + 128
    first = first.reshape(CHIPS * rows, wide)
    second = second.reshape(CHIPS * rows, wide)
    first_other = move_core(first)
    second_other = move_core(second)

    def project(block, weight):
        return jnp.dot(block[:, :half], weight, preferred_element_type=f32)

    def terms(one, two):
        a = project(one, out_proj[:half]).reshape(SIDE, SIDE, rows, columns)
        b = project(two, out_proj[half:]).reshape(SIDE, SIDE, rows, columns)
        return (a + b.transpose(1, 0, 2, 3)).astype(bf16).reshape(CHIPS, rows, columns)

    partial = jnp.stack([terms(first, second), terms(first_other, second_other)])
    parts = [partial, move_z(partial, 1), move_z(partial, 2), move_z(partial, 3)]

    spot = jnp.array([ORDER.index(k) for k in range(SIDE)], jnp.int32)
    far = jnp.arange(SIDE, dtype=jnp.int32)
    x_spot = jnp.take(spot, (here_x - far) % SIDE)
    y_spot = jnp.take(spot, (here_y - far) % SIDE)
    first_place = (y_spot[None, :] * SIDE + x_spot[:, None]).reshape(CHIPS)
    second_place = (x_spot[:, None] * SIDE + y_spot[None, :]).reshape(CHIPS)
    table = jnp.concatenate([first_place, core[None]]).astype(jnp.int32)

    places_all = jnp.stack([first[:, half:], first_other[:, half:]]).reshape(CORES, CHIPS, rows, 128)
    outgoing = select(table, parts, residual_columns, places_all)
    own = chip_exchange(outgoing)
    other = move_core(own)

    group = dp // EPG
    levels_all = jnp.stack([second[:, half:], second_other[:, half:]]).astype(f32)
    levels_all = levels_all.reshape(CORES, CHIPS, rows, 128)
    marks = places_all.astype(f32)

    def in_order(value, at):
        to = (jnp.arange(CHIPS)[None, :] == at[:, None]).astype(f32)
        value = jnp.einsum("ap,cpr->car", to, value, precision=lax.Precision.HIGHEST)
        return jnp.where(core == 0, value, value[::-1])

    sums = jnp.sum(levels_all[..., : GROUPS * EPG], axis=-1)
    mine = lax.dynamic_index_in_dim(levels_all, dp, 3, keepdims=False)
    gates = in_order(route_scale * mine / sums, second_place)
    homes = in_order(
        lax.dynamic_index_in_dim(levels_all, GROUPS * EPG + group, 3, keepdims=False), second_place
    )
    ranks = in_order(lax.dynamic_index_in_dim(marks, group * 16, 3, keepdims=False), first_place)
    hits = ranks[..., None, :] == jnp.arange(1, CAP + 1, dtype=f32)[:, None]
    slots = CORES * CHIPS * CAP
    coef = jnp.sum(jnp.where(hits, gates[..., None, :], 0.0), axis=-1).reshape(slots, 1)
    first_chip = (z == 0) & (dp % EPG == 0)
    home = jnp.sum(jnp.where(hits, homes[..., None, :], 0.0), axis=-1).reshape(slots, 1)
    home = jnp.where(first_chip, home, 0.0)

    gate_weight = gate_proj.reshape(CHIPS, CORES, columns, -1)
    up_weight = up_proj.reshape(CHIPS, CORES, columns, -1)
    scalars = jnp.stack([core, 1 - core]).astype(jnp.int32)
    acc = up(scalars, 0, own, gate_weight, up_weight)
    acc = up(scalars, 1, other, gate_weight, up_weight, acc)
    for_other = down(scalars, 1, acc, down_proj[0], coef, home, own, other)
    returning = down(scalars, 0, acc, down_proj[0], coef, home, own, other, move_core(for_other))

    returned = chip_exchange(returning.reshape(CHIPS, CAP, model)).reshape(CHIPS * CAP, model)
    slot = jnp.arange(1, CAP + 1, dtype=jnp.int32)
    weighting = jnp.repeat(place, 2, axis=1)[:, :, None] == slot[None, None, :]
    weighting = weighting.astype(bf16).reshape(rows, CHIPS * CAP)
    mixed = jnp.dot(weighting, returned, preferred_element_type=f32).astype(bf16)
    even = mixed.astype(f32) + move_z(mixed, 2).astype(f32)
    odd = move_z(mixed, 1).astype(f32) + move_z(mixed, 3).astype(f32)
    return (even + odd).astype(bf16)


def solution(mesh):
    return jax.shard_map(
        local,
        mesh=mesh,
        in_specs=(
            P("dp", None),
            P("dp", "tensor", None),
            P("dp", "tensor", None),
            P("dp", None, None),
            P("dp", None, None),
            P("dp"),
            P("tensor", None, None),
            P("tensor", "dp"),
            P("dp", None, "tensor"),
            P("dp", None, "tensor"),
            P("dp", "tensor", None),
            P("dp", None),
            P("dp", None),
            P("dp", None),
        ),
        out_specs=P("dp", None),
        check_vma=False,
    )
```

time: 338 us -> 209 us (0.62)
  waiting for transfers between devices: 185 us -> 83.6 us
  blocking collectives: 71.1 us -> 0 us
  matrix products: 42.7 us -> 3.59 us
  starting transfers between devices: 12.6 us -> 48.2 us
  Pallas kernels: 0 us -> 34 us
  local copies, waits for them, and re-layouts: 10.8 us -> 34.4 us
  between operations: 13.6 us -> 0.61 us
    psum x1 -> x0, waiting for transfers between devices: 81.3 us -> none  [expert_block(): return lax.psum(produced.astype(jnp.bfloat16), 'tensor')]
    all_to_all x1 -> x0, blocking collectives: 48.6 us -> none  [local(): lax.all_to_all(outgoing, 'dp', split_axis=0, concat_axis=0, tiled=True)]
    all_gather x1 -> x0, waiting for transfers between devices: 48.3 us -> none  [local(): lax.all_gather(head_out, 'dp', axis=0, tiled=True)]
    dot_general x10 -> x8, matrix products: 42.7 us -> 3.59 us  [the longest x4 1.87 us: project(): return jnp.dot(block[:, :half], weight, preferred_element_type=f32)]
    ppermute x0 -> x22, starting transfers between devices: none -> 34.1 us  [the longest x6 11.7 us: move_z(): lax.ppermute(value, 'tensor', [(z, (z + by) % PLANES) for z in range(PLAN...]
    pallas_call x0 -> x6, Pallas kernels: none -> 34 us  [the longest x1 16.7 us: attend(): pl.pallas_call(attend_kernel, grid_spec=pltpu.PrefetchScalarGridSpec(num_...]
    ppermute x0 -> x22, waiting for transfers between devices: none -> 32 us  [the longest x6 17.6 us: move_z(): lax.ppermute(value, 'tensor', [(z, (z + by) % PLANES) for z in range(PLAN...]
    psum x1 -> x0, blocking collectives: 22.5 us -> none  [local(): summed_terms = lax.psum(column_terms, 'tensor')]
  transfers between devices with their start and end apart: 4 -> 25, of which waited for: 4 -> 14; matrix products, arithmetic and copies ran while one was open for 0% -> 7% of each run, Pallas kernels for 0% -> 2%
where the time goes in v1:
time: 209 us; the launch traced here: 208 us
  waiting for transfers between devices  83.6 us (40%)
  starting transfers between devices  48.2 us (23%)
  local copies, waits for them, and re-layouts  34.4 us (16%)
  Pallas kernels  34 us (16%)
  other arithmetic  3.92 us (2%)
  matrix products  3.59 us (2%)
    all_to_all x2, waiting for transfers between devices, chip_exchange(): lax.all_to_all(value, 'dp', split_axis=0, concat_axis=0, axis_index_group...  51.6 us
    unnamed x55, local copies, waits for them, and re-layouts  18.6 us
    ppermute x6, waiting for transfers between devices, move_z(): lax.ppermute(value, 'tensor', [(z, (z + by) % PLANES) for z in range(PLAN...  17.6 us
    pallas_call x1, Pallas kernels, attend(): pl.pallas_call(attend_kernel, grid_spec=pltpu.PrefetchScalarGridSpec(num_...  16.7 us
    ppermute x6, starting transfers between devices, move_z(): lax.ppermute(value, 'tensor', [(z, (z + by) % PLANES) for z in range(PLAN...  11.7 us
    ppermute x6, starting transfers between devices, move_x(): return lax.ppermute(value, 'dp', shift_pairs(by, 0, 0))  11.5 us
    ppermute x6, starting transfers between devices, move_y(): return lax.ppermute(value, 'dp', shift_pairs(0, by, 0))  10.1 us
    all_to_all x2, starting transfers between devices, chip_exchange(): lax.all_to_all(value, 'dp', split_axis=0, concat_axis=0, axis_index_group...  9.23 us
  transfers between devices with their start and end apart: 25, of which 14 were waited for; matrix products, arithmetic and copies ran while one was open for 7% of the time, Pallas kernels for 2%

profile of v1, /device:TPU:0, one launch (start us, length us, event | category | flops | bytes accessed | tf_op | source)
XLA Modules:
  0.0 208.2 jit_solution(13335250955047071214)
XLA Ops:
  0.0 2.2 %copy-done.8 = bf16[32,512,128]{2,1,0:T(8,128)(2,1)S(1)} copy-done((bf16[32,512,128]{2,1,0:T(8,128)(2,1)S(1)}, bf16[32,512,128]{2,1,0:T(8,128)(2,1)}, u32[]{:S(2)}) %copy-start.8) | copy-done | bytes 4194328
  6.4 16.7 %attend.1 = bf16[16,4096]{1,0:T(8,128)(2,1)S(1)} custom-call(s32[16]{0:T(128)S(1)} %copy-done.12, bf16[16,32,512]{2,1,0:T(8,128)(2,1)S(1)} %copy-done.10, bf16[16,32,64]{2,1,0:T(8,128)(2,1)S(1)} %copy-done.11, bf16[16,1024,512]{2,1,0:T(8,128)(2,1)} %k_ref.1, bf16[16,64,1024]{2,1,0:T(8,128)(2,1)S(1)} %copy-done.9, bf16[32,512,128]{2,1,0:T(8,128)(2,1)S(1)} %copy-done.8), custom_call_target="tpu_custom_call" | custom-call | flops 1073741824 | bytes 18874368 | tf_op jit(solution)/shard_map/attend/pallas_call | solution.py:111
  34.1 4.8 %all-to-all-start = ((bf16[32,16,224]{2,1,0:T(8,128)(2,1)}), bf16[32,16,224]{2,1,0:T(8,128)(2,1)S(1)}, u32[]{:S(2)}, u32[]{:S(2)}) async-start(bf16[32,16,224]{2,1,0:T(8,128)(2,1)} %bitcast.75), calls=%async_computation | async-start | bytes 524288 | tf_op jit(solution)/shard_map/all_to_all | solution.py:352
  40.4 3.4 %collective-permute-start.8 = (bf16[16,2176]{1,0:T(8,128)(2,1)S(1)}, bf16[16,2176]{1,0:T(8,128)(2,1)S(1)}, u32[]{:S(2)}, u32[]{:S(2)}) collective-permute-start(bf16[16,2176]{1,0:T(8,128)(2,1)S(1)} %concatenate.17), channel_id=1, source_target_pairs={{0,16},{4,20},{8,24},{12,28},{16,0},{20,4},{24,8},{28,12},{32,48},... | collective-permute-start | bytes 208904 | tf_op jit(solution)/shard_map/ppermute | solution.py:45
  49.4 2.6 %collective-permute-start.10 = (bf16[4,16,2176]{2,1,0:T(8,128)(2,1)S(1)}, bf16[4,16,2176]{2,1,0:T(8,128)(2,1)S(1)}, u32[]{:S(2)}, u32[]{:S(2)}) collective-permute-start(bf16[4,16,2176]{2,1,0:T(8,128)(2,1)S(1)} %get-tuple-element.15), channel_id=1, source_target_pairs={{0,96},{4,100},{8,104},{12,108},{16,112},{20,116},{24,120},{28,124... | collective-permute-start | bytes 835592 | tf_op jit(solution)/shard_map/ppermute | solution.py:41
  51.9 3.0 %collective-permute-done.5 = bf16[4,16,2176]{2,1,0:T(8,128)(2,1)S(1)} collective-permute-done((bf16[4,16,2176]{2,1,0:T(8,128)(2,1)S(1)}, bf16[4,16,2176]{2,1,0:T(8,128)(2,1)S(1)}, u32[]{:S(2)}, u32[]{:S(2)}) %collective-permute-start.5) | collective-permute-done | bytes 278560 | tf_op jit(solution)/shard_map/ppermute | solution.py:45
  54.9 3.0 %collective-permute-start.11 = (bf16[4,16,2176]{2,1,0:T(8,128)(2,1)S(1)}, bf16[4,16,2176]{2,1,0:T(8,128)(2,1)S(1)}, u32[]{:S(2)}, u32[]{:S(2)}) collective-permute-start(bf16[4,16,2176]{2,1,0:T(8,128)(2,1)S(1)} %get-tuple-element.15), channel_id=1, source_target_pairs={{0,64},{4,68},{8,72},{12,76},{16,80},{20,84},{24,88},{28,92},{32,9... | collective-permute-start | bytes 835592 | tf_op jit(solution)/shard_map/ppermute | solution.py:41
  57.9 2.4 %collective-permute-done.3 = bf16[4,16,2176]{2,1,0:T(8,128)(2,1)S(1)} collective-permute-done((bf16[4,16,2176]{2,1,0:T(8,128)(2,1)S(1)}, bf16[4,16,2176]{2,1,0:T(8,128)(2,1)S(1)}, u32[]{:S(2)}, u32[]{:S(2)}) %collective-permute-start.3) | collective-permute-done | bytes 278560 | tf_op jit(solution)/shard_map/ppermute | solution.py:45
  60.6 2.1 %collective-permute-done.10 = bf16[4,16,2176]{2,1,0:T(8,128)(2,1)S(1)} collective-permute-done((bf16[4,16,2176]{2,1,0:T(8,128)(2,1)S(1)}, bf16[4,16,2176]{2,1,0:T(8,128)(2,1)S(1)}, u32[]{:S(2)}, u32[]{:S(2)}) %collective-permute-start.10) | collective-permute-done | bytes 278560 | tf_op jit(solution)/shard_map/ppermute | solution.py:41
  68.5 2.0 collective-permute-start.14
  70.5 3.6 %collective-permute-start.15 = (bf16[2,16,16,224]{3,2,1,0:T(8,128)(2,1)S(1)}, bf16[2,16,16,224]{3,2,1,0:T(8,128)(2,1)S(1)}, u32[]{:S(2)}, u32[]{:S(2)}) collective-permute-start(bf16[2,16,16,224]{3,2,1,0:T(8,128)(2,1)S(1)} %pad_maximum_fusion.4.p0_ref), channel_id=1, source_target_pairs={{0,2},{1,3},{2,0},{3,1},{4,6},{5,7},{6,4},{7,5},{8,10},{9,11},{10,... | collective-permute-start | bytes 688136 | tf_op jit(solution)/shard_map/ppermute | solution.py:53
  76.8 2.4 %collective-permute-done.14.p1_ref = bf16[2,16,16,224]{3,2,1,0:T(8,128)(2,1)S(1)} collective-permute-done((bf16[2,16,16,224]{3,2,1,0:T(8,128)(2,1)S(1)}, bf16[2,16,16,224]{3,2,1,0:T(8,128)(2,1)S(1)}, u32[]{:S(2)}, u32[]{:S(2)}) %collective-permute-start.14) | collective-permute-done | bytes 229408 | tf_op jit(solution)/shard_map/ppermute | solution.py:53
  79.2 6.8 %collective-permute-done.15.p2_ref = bf16[2,16,16,224]{3,2,1,0:T(8,128)(2,1)S(1)} collective-permute-done((bf16[2,16,16,224]{3,2,1,0:T(8,128)(2,1)S(1)}, bf16[2,16,16,224]{3,2,1,0:T(8,128)(2,1)S(1)}, u32[]{:S(2)}, u32[]{:S(2)}) %collective-permute-start.15) | collective-permute-done | bytes 229408 | tf_op jit(solution)/shard_map/ppermute | solution.py:53
  87.0 2.3 %copy.130 = bf16[16,256,224]{1,2,0:T(8,128)(2,1)} copy(bf16[16,256,224]{2,1,0:T(8,128)(2,1)S(1)} %select.30) | data formatting | bytes 3670016 | tf_op jit(solution)/shard_map/select/pallas_call | solution.py:203
  89.3 5.5 %all-to-all-start.1 = ((bf16[16,256,224]{1,2,0:T(8,128)(2,1)}), bf16[16,256,224]{1,2,0:T(8,128)(2,1)}, u32[]{:S(2)}, u32[]{:S(2)}) async-start(bf16[16,256,224]{1,2,0:T(8,128)(2,1)} %copy.130), calls=%async_computation.1 | async-start | bytes 3670016 | tf_op jit(solution)/shard_map/all_to_all | solution.py:58
  97.3 23.9 %all-to-all-done.1 = bf16[16,256,224]{1,2,0:T(8,128)(2,1)} async-done(((bf16[16,256,224]{1,2,0:T(8,128)(2,1)}), bf16[16,256,224]{1,2,0:T(8,128)(2,1)}, u32[]{:S(2)}, u32[]{:S(2)}) %all-to-all-start.1) | async-done | bytes 1835040 | tf_op jit(solution)/shard_map/all_to_all | solution.py:58
  123.2 2.8 %copy.131.x_ref.own_ref = bf16[16,256,224]{2,1,0:T(8,128)(2,1)S(1)} copy(bf16[16,256,224]{1,2,0:T(8,128)(2,1)} %all-to-all-done.1) | data formatting | bytes 3670016 | tf_op jit(solution)/shard_map/all_to_all | solution.py:58
  126.1 2.0 copy-done.2
  128.1 2.0 copy-done.4
  130.1 4.4 %up.2.rest_0_ = f32[2,256,256]{2,1,0:T(8,128)S(1)} custom-call(s32[2]{0:T(128)S(1)} %pad_add_fusion.scalars, bf16[16,256,224]{2,1,0:T(8,128)(2,1)S(1)} %copy.131.x_ref.own_ref, bf16[16,2,224,256]{3,2,1,0:T(8,128)(2,1)S(1)} %bitcast.76, bf16[16,2,224,256]{3,2,1,0:T(8,128)(2,1)S(1)} %bitcast.78), custom_call_target="tpu_custom_call" | custom-call | flops 939524096 | bytes 10000000 | tf_op jit(solution)/shard_map/up/pallas_call | solution.py:238
  134.5 3.8 %copy.132.x_ref.other_ref = bf16[16,256,224]{2,1,0:T(8,128)(2,1)} copy(bf16[16,256,224]{1,2,0:T(8,128)(2,1)} %collective-permute-done.17) | data formatting | bytes 3670016 | tf_op jit(solution)/shard_map/ppermute | solution.py:49
  139.9 2.0 copy-done.3
  142.0 2.0 copy-done.5
  144.0 4.4 %up.3.acc_ref = f32[2,256,256]{2,1,0:T(8,128)S(1)} custom-call(s32[2]{0:T(128)S(1)} %pad_add_fusion.scalars, bf16[16,256,224]{2,1,0:T(8,128)(2,1)S(1)} %copy-done, bf16[16,2,224,256]{3,2,1,0:T(8,128)(2,1)S(1)} %bitcast.77, bf16[16,2,224,256]{3,2,1,0:T(8,128)(2,1)S(1)} %bitcast.79, f32[2,256,256]{2,1,0:T(8,128)S(1)} %up.2.rest_0_), custom_call_target="tpu_custom_call" | custom-call | flops 939524096 | bytes 10000000 | tf_op jit(solution)/shard_map/up/pallas_call | solution.py:238
  148.4 3.6 %down.2 = bf16[128,7168]{1,0:T(8,128)(2,1)S(1)} custom-call(s32[2]{0:T(128)S(1)} %pad_add_fusion.scalars, f32[2,256,256]{2,1,0:T(8,128)S(1)} %up.3.acc_ref, bf16[256,7168]{1,0:T(8,128)(2,1)S(1)} %bitcast.80, f32[256,1]{1,0:T(8,128)S(1)} %reshape.183.coef_ref, f32[256,1]{1,0:T(8,128)S(1)} %select_n.139.home_ref, ...), custom_call_target="tpu_custom_call" | custom-call | flops 469762048 | bytes 8000000 | tf_op jit(solution)/shard_map/down/pallas_call | solution.py:294
  152.6 3.4 %collective-permute-done.18.rest_0_ = bf16[128,7168]{1,0:T(8,128)(2,1)S(1)} collective-permute-done((bf16[128,7168]{1,0:T(8,128)(2,1)S(1)}, bf16[128,7168]{1,0:T(8,128)(2,1)S(1)}, u32[]{:S(2)}, u32[]{:S(2)}) %collective-permute-start.18) | collective-permute-done | bytes 1835040 | tf_op jit(solution)/shard_map/ppermute | solution.py:49
  156.0 3.9 %down.3 = bf16[128,7168]{1,0:T(8,128)(2,1)S(1)} custom-call(s32[2]{0:T(128)S(1)} %pad_add_fusion.scalars, f32[2,256,256]{2,1,0:T(8,128)S(1)} %up.3.acc_ref, bf16[256,7168]{1,0:T(8,128)(2,1)S(1)} %bitcast.81, f32[256,1]{1,0:T(8,128)S(1)} %reshape.183.coef_ref, f32[256,1]{1,0:T(8,128)S(1)} %select_n.139.home_ref, ...), custom_call_target="tpu_custom_call" | custom-call | flops 469762048 | bytes 8000000 | tf_op jit(solution)/shard_map/down/pallas_call | solution.py:294
  161.2 3.7 %all-to-all-start.2 = ((bf16[16,8,7168]{2,1,0:T(8,128)(2,1)}), bf16[16,8,7168]{2,1,0:T(8,128)(2,1)S(1)}, u32[]{:S(2)}, u32[]{:S(2)}) async-start(bf16[16,8,7168]{2,1,0:T(8,128)(2,1)} %bitcast.82), calls=%async_computation.2 | async-start | bytes 3670016 | tf_op jit(solution)/shard_map/all_to_all | solution.py:58
  165.0 27.7 %all-to-all-done.2 = bf16[16,8,7168]{2,1,0:T(8,128)(2,1)S(1)} async-done(((bf16[16,8,7168]{2,1,0:T(8,128)(2,1)}), bf16[16,8,7168]{2,1,0:T(8,128)(2,1)S(1)}, u32[]{:S(2)}, u32[]{:S(2)}) %all-to-all-start.2) | async-done | bytes 1835040 | tf_op jit(solution)/shard_map/all_to_all | solution.py:58
  195.7 2.2 %collective-permute-start.20 = (bf16[16,7168]{1,0:T(8,128)(2,1)S(1)}, bf16[16,7168]{1,0:T(8,128)(2,1)S(1)}, u32[]{:S(2)}, u32[]{:S(2)}) collective-permute-start(bf16[16,7168]{1,0:T(8,128)(2,1)S(1)} %fusion), channel_id=1, source_target_pairs={{0,1},{1,2},{2,3},{3,0},{4,5},{5,6},{6,7},{7,4},{8,9},{9,10},{10,1... | collective-permute-start | bytes 688136 | tf_op jit(solution)/shard_map/ppermute | solution.py:53
  199.0 5.0 %collective-permute-done.19 = bf16[16,7168]{1,0:T(8,128)(2,1)S(1)} collective-permute-done((bf16[16,7168]{1,0:T(8,128)(2,1)S(1)}, bf16[16,7168]{1,0:T(8,128)(2,1)S(1)}, u32[]{:S(2)}, u32[]{:S(2)}) %collective-permute-start.19) | collective-permute-done | bytes 229408 | tf_op jit(solution)/shard_map/ppermute | solution.py:53
  204.0 2.8 %collective-permute-done.20 = bf16[16,7168]{1,0:T(8,128)(2,1)S(1)} collective-permute-done((bf16[16,7168]{1,0:T(8,128)(2,1)S(1)}, bf16[16,7168]{1,0:T(8,128)(2,1)S(1)}, u32[]{:S(2)}, u32[]{:S(2)}) %collective-permute-start.20) | collective-permute-done | bytes 229408 | tf_op jit(solution)/shard_map/ppermute | solution.py:53
  (160 shorter events, 45.2 us)
Async XLA Ops:
  6.4 16.8 %copy-start.20 = (s32[16,8]{0,1:T(8,128)S(1)}, s32[16,8]{0,1:T(8,128)}, u32[]{:S(2)}) copy-start(s32[16,8]{0,1:T(8,128)} %param.29) | copy-start | bytes 1540
  6.4 16.8 %copy-start.21 = (s32[16,4]{0,1:T(4,128)S(1)}, s32[16,4]{0,1:T(4,128)}, u32[]{:S(2)}) copy-start(s32[16,4]{0,1:T(4,128)} %param.28) | copy-start | bytes 772
  6.4 16.9 %copy-start.22 = (s32[16,8]{0,1:T(8,128)S(1)}, s32[16,8]{0,1:T(8,128)}, u32[]{:S(2)}) copy-start(s32[16,8]{0,1:T(8,128)} %param.30) | copy-start | bytes 1540
  6.4 26.5 %copy-start.19 = (bf16[16,7168]{1,0:T(8,128)(2,1)S(1)}, bf16[16,7168]{1,0:T(8,128)(2,1)}, u32[]{:S(2)}) copy-start(bf16[16,7168]{1,0:T(8,128)(2,1)} %param.17) | copy-start | bytes 688132
  23.1 15.9 %copy-start.13 = (s32[4]{0:T(128)S(1)}, s32[4]{0:T(128)}, u32[]{:S(2)}) copy-start(s32[4]{0:T(128)} %constant.137.clone2.2) | copy-start | bytes 52
  23.7 22.2 %collective-permute-start.6 = (bf16[16,2176]{1,0:T(8,128)(2,1)S(1)}, bf16[16,2176]{1,0:T(8,128)(2,1)S(1)}, u32[]{:S(2)}, u32[]{:S(2)}) collective-permute-start(bf16[16,2176]{1,0:T(8,128)(2,1)S(1)} %concatenate.17), channel_id=1, source_target_pairs={{0,8},{4,12},{8,16},{12,20},{16,24},{20,28},{24,0},{28,4},{32,40},... | collective-permute-start | bytes 208904 | tf_op jit(solution)/shard_map/ppermute | solution.py:45
  25.4 22.0 %collective-permute-start.7 = (bf16[16,2176]{1,0:T(8,128)(2,1)S(1)}, bf16[16,2176]{1,0:T(8,128)(2,1)S(1)}, u32[]{:S(2)}, u32[]{:S(2)}) collective-permute-start(bf16[16,2176]{1,0:T(8,128)(2,1)S(1)} %concatenate.17), channel_id=1, source_target_pairs={{0,24},{4,28},{8,0},{12,4},{16,8},{20,12},{24,16},{28,20},{32,56},... | collective-permute-start | bytes 208904 | tf_op jit(solution)/shard_map/ppermute | solution.py:45
  27.7 12.7 %collective-permute-start = (bf16[16,2176]{1,0:T(8,128)(2,1)S(1)}, bf16[16,2176]{1,0:T(8,128)(2,1)S(1)}, u32[]{:S(2)}, u32[]{:S(2)}) collective-permute-start(bf16[16,2176]{1,0:T(8,128)(2,1)S(1)} %get-tuple-element.21), channel_id=1, source_target_pairs={{0,32},{4,36},{8,40},{12,44},{16,48},{20,52},{24,56},{28,60},{32,6... | collective-permute-start | bytes 208904 | tf_op jit(solution)/shard_map/ppermute | solution.py:41
  29.3 14.4 %collective-permute-start.1 = (bf16[16,2176]{1,0:T(8,128)(2,1)S(1)}, bf16[16,2176]{1,0:T(8,128)(2,1)S(1)}, u32[]{:S(2)}, u32[]{:S(2)}) collective-permute-start(bf16[16,2176]{1,0:T(8,128)(2,1)S(1)} %get-tuple-element.21), channel_id=1, source_target_pairs={{0,96},{4,100},{8,104},{12,108},{16,112},{20,116},{24,120},{28,124... | collective-permute-start | bytes 208904 | tf_op jit(solution)/shard_map/ppermute | solution.py:41
  31.0 12.7 %collective-permute-start.2 = (bf16[16,2176]{1,0:T(8,128)(2,1)S(1)}, bf16[16,2176]{1,0:T(8,128)(2,1)S(1)}, u32[]{:S(2)}, u32[]{:S(2)}) collective-permute-start(bf16[16,2176]{1,0:T(8,128)(2,1)S(1)} %get-tuple-element.21), channel_id=1, source_target_pairs={{0,64},{4,68},{8,72},{12,76},{16,80},{20,84},{24,88},{28,92},{32,9... | collective-permute-start | bytes 208904 | tf_op jit(solution)/shard_map/ppermute | solution.py:41
  34.1 42.7 %all-to-all-start = ((bf16[32,16,224]{2,1,0:T(8,128)(2,1)}), bf16[32,16,224]{2,1,0:T(8,128)(2,1)S(1)}, u32[]{:S(2)}, u32[]{:S(2)}) async-start(bf16[32,16,224]{2,1,0:T(8,128)(2,1)} %bitcast.75), calls=%async_computation | async-start | bytes 524288 | tf_op jit(solution)/shard_map/all_to_all | solution.py:352
  40.4 8.2 %collective-permute-start.8 = (bf16[16,2176]{1,0:T(8,128)(2,1)S(1)}, bf16[16,2176]{1,0:T(8,128)(2,1)S(1)}, u32[]{:S(2)}, u32[]{:S(2)}) collective-permute-start(bf16[16,2176]{1,0:T(8,128)(2,1)S(1)} %concatenate.17), channel_id=1, source_target_pairs={{0,16},{4,20},{8,24},{12,28},{16,0},{20,4},{24,8},{28,12},{32,48},... | collective-permute-start | bytes 208904 | tf_op jit(solution)/shard_map/ppermute | solution.py:45
  43.8 11.1 %collective-permute-start.5 = (bf16[4,16,2176]{2,1,0:T(8,128)(2,1)S(1)}, bf16[4,16,2176]{2,1,0:T(8,128)(2,1)S(1)}, u32[]{:S(2)}, u32[]{:S(2)}) collective-permute-start(bf16[4,16,2176]{2,1,0:T(8,128)(2,1)S(1)} %get-tuple-element.17), channel_id=1, source_target_pairs={{0,16},{4,20},{8,24},{12,28},{16,0},{20,4},{24,8},{28,12},{32,48},... | collective-permute-start | bytes 835592 | tf_op jit(solution)/shard_map/ppermute | solution.py:45
  44.1 16.2 %collective-permute-start.3 = (bf16[4,16,2176]{2,1,0:T(8,128)(2,1)S(1)}, bf16[4,16,2176]{2,1,0:T(8,128)(2,1)S(1)}, u32[]{:S(2)}, u32[]{:S(2)}) collective-permute-start(bf16[4,16,2176]{2,1,0:T(8,128)(2,1)S(1)} %get-tuple-element.17), channel_id=1, source_target_pairs={{0,8},{4,12},{8,16},{12,20},{16,24},{20,28},{24,0},{28,4},{32,40},... | collective-permute-start | bytes 835592 | tf_op jit(solution)/shard_map/ppermute | solution.py:45
  45.9 14.4 %collective-permute-start.4 = (bf16[4,16,2176]{2,1,0:T(8,128)(2,1)S(1)}, bf16[4,16,2176]{2,1,0:T(8,128)(2,1)S(1)}, u32[]{:S(2)}, u32[]{:S(2)}) collective-permute-start(bf16[4,16,2176]{2,1,0:T(8,128)(2,1)S(1)} %get-tuple-element.17), channel_id=1, source_target_pairs={{0,24},{4,28},{8,0},{12,4},{16,8},{20,12},{24,16},{28,20},{32,56},... | collective-permute-start | bytes 835592 | tf_op jit(solution)/shard_map/ppermute | solution.py:45
  48.6 12.0 %collective-permute-start.9 = (bf16[4,16,2176]{2,1,0:T(8,128)(2,1)S(1)}, bf16[4,16,2176]{2,1,0:T(8,128)(2,1)S(1)}, u32[]{:S(2)}, u32[]{:S(2)}) collective-permute-start(bf16[4,16,2176]{2,1,0:T(8,128)(2,1)S(1)} %get-tuple-element.15), channel_id=1, source_target_pairs={{0,32},{4,36},{8,40},{12,44},{16,48},{20,52},{24,56},{28,60},{32,6... | collective-permute-start | bytes 835592 | tf_op jit(solution)/shard_map/ppermute | solution.py:41
  49.4 13.4 %collective-permute-start.10 = (bf16[4,16,2176]{2,1,0:T(8,128)(2,1)S(1)}, bf16[4,16,2176]{2,1,0:T(8,128)(2,1)S(1)}, u32[]{:S(2)}, u32[]{:S(2)}) collective-permute-start(bf16[4,16,2176]{2,1,0:T(8,128)(2,1)S(1)} %get-tuple-element.15), channel_id=1, source_target_pairs={{0,96},{4,100},{8,104},{12,108},{16,112},{20,116},{24,120},{28,124... | collective-permute-start | bytes 835592 | tf_op jit(solution)/shard_map/ppermute | solution.py:41
  54.9 9.5 %collective-permute-start.11 = (bf16[4,16,2176]{2,1,0:T(8,128)(2,1)S(1)}, bf16[4,16,2176]{2,1,0:T(8,128)(2,1)S(1)}, u32[]{:S(2)}, u32[]{:S(2)}) collective-permute-start(bf16[4,16,2176]{2,1,0:T(8,128)(2,1)S(1)} %get-tuple-element.15), channel_id=1, source_target_pairs={{0,64},{4,68},{8,72},{12,76},{16,80},{20,84},{24,88},{28,92},{32,9... | collective-permute-start | bytes 835592 | tf_op jit(solution)/shard_map/ppermute | solution.py:41
  60.4 5.9 %collective-permute-start.12 = (bf16[256,2176]{1,0:T(8,128)(2,1)S(1)}, bf16[256,2176]{1,0:T(8,128)(2,1)S(1)}, u32[]{:S(2)}, u32[]{:S(2)}) collective-permute-start(bf16[256,2176]{1,0:T(8,128)(2,1)S(1)} %bitcast.87), channel_id=1, source_target_pairs={{0,4},{4,0},{8,12},{12,8},{16,20},{20,16},{24,28},{28,24},{32,36},... | collective-permute-start | bytes 3342344 | tf_op jit(solution)/shard_map/ppermute | solution.py:49
  64.6 2.8 %collective-permute-start.13 = (bf16[256,2176]{1,0:T(8,128)(2,1)S(1)}, bf16[256,2176]{1,0:T(8,128)(2,1)S(1)}, u32[]{:S(2)}, u32[]{:S(2)}) collective-permute-start(bf16[256,2176]{1,0:T(8,128)(2,1)S(1)} %bitcast.84), channel_id=1, source_target_pairs={{0,4},{4,0},{8,12},{12,8},{16,20},{20,16},{24,28},{28,24},{32,36},... | collective-permute-start | bytes 3342344 | tf_op jit(solution)/shard_map/ppermute | solution.py:49
  68.5 10.7 %collective-permute-start.14 = (bf16[2,16,16,224]{3,2,1,0:T(8,128)(2,1)S(1)}, bf16[2,16,16,224]{3,2,1,0:T(8,128)(2,1)S(1)}, u32[]{:S(2)}, u32[]{:S(2)}) collective-permute-start(bf16[2,16,16,224]{3,2,1,0:T(8,128)(2,1)S(1)} %pad_maximum_fusion.4.p0_ref), channel_id=1, source_target_pairs={{0,1},{1,2},{2,3},{3,0},{4,5},{5,6},{6,7},{7,4},{8,9},{9,10},{10,1... | collective-permute-start | bytes 688136 | tf_op jit(solution)/shard_map/ppermute | solution.py:53
  70.5 15.5 %collective-permute-start.15 = (bf16[2,16,16,224]{3,2,1,0:T(8,128)(2,1)S(1)}, bf16[2,16,16,224]{3,2,1,0:T(8,128)(2,1)S(1)}, u32[]{:S(2)}, u32[]{:S(2)}) collective-permute-start(bf16[2,16,16,224]{3,2,1,0:T(8,128)(2,1)S(1)} %pad_maximum_fusion.4.p0_ref), channel_id=1, source_target_pairs={{0,2},{1,3},{2,0},{3,1},{4,6},{5,7},{6,4},{7,5},{8,10},{9,11},{10,... | collective-permute-start | bytes 688136 | tf_op jit(solution)/shard_map/ppermute | solution.py:53
  74.1 11.9 %collective-permute-start.16 = (bf16[2,16,16,224]{3,2,1,0:T(8,128)(2,1)S(1)}, bf16[2,16,16,224]{3,2,1,0:T(8,128)(2,1)S(1)}, u32[]{:S(2)}, u32[]{:S(2)}) collective-permute-start(bf16[2,16,16,224]{3,2,1,0:T(8,128)(2,1)S(1)} %pad_maximum_fusion.4.p0_ref), channel_id=1, source_target_pairs={{0,3},{1,0},{2,1},{3,2},{4,7},{5,4},{6,5},{7,6},{8,11},{9,8},{10,9... | collective-permute-start | bytes 688136 | tf_op jit(solution)/shard_map/ppermute | solution.py:53
  89.3 31.8 %all-to-all-start.1 = ((bf16[16,256,224]{1,2,0:T(8,128)(2,1)}), bf16[16,256,224]{1,2,0:T(8,128)(2,1)}, u32[]{:S(2)}, u32[]{:S(2)}) async-start(bf16[16,256,224]{1,2,0:T(8,128)(2,1)} %copy.130), calls=%async_computation.1 | async-start | bytes 3670016 | tf_op jit(solution)/shard_map/all_to_all | solution.py:58
  94.8 27.3 %copy-start.16 = (bf16[256,128]{1,0:T(8,128)(2,1)S(1)}, bf16[256,128]{1,0:T(8,128)(2,1)}, u32[]{:S(2)}) copy-start(bf16[256,128]{1,0:T(8,128)(2,1)} %copy-done.15) | copy-start | bytes 196612
  94.9 27.3 %copy-start.18 = (bf16[256,128]{1,0:T(8,128)(2,1)S(1)}, bf16[256,128]{1,0:T(8,128)(2,1)}, u32[]{:S(2)}) copy-start(bf16[256,128]{1,0:T(8,128)(2,1)} %copy-done.17) | copy-start | bytes 196612
  121.1 13.4 %collective-permute-start.17 = (bf16[16,256,224]{1,2,0:T(8,128)(2,1)}, bf16[16,256,224]{1,2,0:T(8,128)(2,1)}, u32[]{:S(2)}, u32[]{:S(2)}) collective-permute-start(bf16[16,256,224]{1,2,0:T(8,128)(2,1)} %all-to-all-done.1), channel_id=1, source_target_pairs={{0,4},{4,0},{8,12},{12,8},{16,20},{20,16},{24,28},{28,24},{32,36},... | collective-permute-start | bytes 5505032 | tf_op jit(solution)/shard_map/ppermute | solution.py:49
  152.0 4.0 %collective-permute-start.18 = (bf16[128,7168]{1,0:T(8,128)(2,1)S(1)}, bf16[128,7168]{1,0:T(8,128)(2,1)S(1)}, u32[]{:S(2)}, u32[]{:S(2)}) collective-permute-start(bf16[128,7168]{1,0:T(8,128)(2,1)S(1)} %down.2), channel_id=1, source_target_pairs={{0,4},{4,0},{8,12},{12,8},{16,20},{20,16},{24,28},{28,24},{32,36},... | collective-permute-start | bytes 5505032 | tf_op jit(solution)/shard_map/ppermute | solution.py:49
  161.2 31.6 %all-to-all-start.2 = ((bf16[16,8,7168]{2,1,0:T(8,128)(2,1)}), bf16[16,8,7168]{2,1,0:T(8,128)(2,1)S(1)}, u32[]{:S(2)}, u32[]{:S(2)}) async-start(bf16[16,8,7168]{2,1,0:T(8,128)(2,1)} %bitcast.82), calls=%async_computation.2 | async-start | bytes 3670016 | tf_op jit(solution)/shard_map/all_to_all | solution.py:58
  193.9 10.1 %collective-permute-start.19 = (bf16[16,7168]{1,0:T(8,128)(2,1)S(1)}, bf16[16,7168]{1,0:T(8,128)(2,1)S(1)}, u32[]{:S(2)}, u32[]{:S(2)}) collective-permute-start(bf16[16,7168]{1,0:T(8,128)(2,1)S(1)} %fusion), channel_id=1, source_target_pairs={{0,2},{1,3},{2,0},{3,1},{4,6},{5,7},{6,4},{7,5},{8,10},{9,11},{10,... | collective-permute-start | bytes 688136 | tf_op jit(solution)/shard_map/ppermute | solution.py:53
  195.7 11.0 %collective-permute-start.20 = (bf16[16,7168]{1,0:T(8,128)(2,1)S(1)}, bf16[16,7168]{1,0:T(8,128)(2,1)S(1)}, u32[]{:S(2)}, u32[]{:S(2)}) collective-permute-start(bf16[16,7168]{1,0:T(8,128)(2,1)S(1)} %fusion), channel_id=1, source_target_pairs={{0,1},{1,2},{2,3},{3,0},{4,5},{5,6},{6,7},{7,4},{8,9},{9,10},{10,1... | collective-permute-start | bytes 688136 | tf_op jit(solution)/shard_map/ppermute | solution.py:53
  198.0 9.4 %collective-permute-start.21 = (bf16[16,7168]{1,0:T(8,128)(2,1)S(1)}, bf16[16,7168]{1,0:T(8,128)(2,1)S(1)}, u32[]{:S(2)}, u32[]{:S(2)}) collective-permute-start(bf16[16,7168]{1,0:T(8,128)(2,1)S(1)} %fusion), channel_id=1, source_target_pairs={{0,3},{1,0},{2,1},{3,2},{4,7},{5,4},{6,5},{7,6},{8,11},{9,8},{10,9... | collective-permute-start | bytes 688136 | tf_op jit(solution)/shard_map/ppermute | solution.py:53
  (20 other events, 49.8 us)

commit v2 on v0

v2 whole, which is shorter than its diff:
```python
import jax
import jax.numpy as jnp
from jax import lax
from jax.experimental import pallas as pl
from jax.experimental.pallas import tpu as pltpu
from jax.sharding import PartitionSpec as P

SIDE = 4
CORES = 2
CHIPS = SIDE * SIDE
PLANES = 4
TOPG = 4
GROUPS = 8
EPG = 4
CAP = 8
QUARTER = 4
PART = QUARTER * CAP

score_scale = 192.0 ** (-0.5)
route_scale = 2.5
far_below = -1e30

f32 = jnp.float32
bf16 = jnp.bfloat16
VMEM = 28 * 1024 * 1024


def distant(value):
    return pltpu.with_memory_space_constraint(value, pltpu.HBM)


def dp_index(x, y, c):
    return (x * SIDE + y) * CORES + c


def place_pairs(place):
    return [
        (dp_index(x, y, c), dp_index(*place(x, y, c)))
        for x in range(SIDE)
        for y in range(SIDE)
        for c in range(CORES)
    ]


def move_core(value):
    return lax.ppermute(value, "dp", place_pairs(lambda x, y, c: (x, y, 1 - c)))


def move_ring(value, by, x_core):
    def place(x, y, c):
        return ((x + by) % SIDE, y, c) if c == x_core else (x, (y + by) % SIDE, c)

    return lax.ppermute(value, "dp", place_pairs(place))


def move_z(value, by):
    return lax.ppermute(value, "tensor", [(z, (z + by) % PLANES) for z in range(PLANES)])


def sum_z(low, high):
    def add(block, mask):
        pairs = [(z, z ^ mask) for z in range(PLANES)]
        moved = lax.ppermute(block, "tensor", pairs)
        return (block.astype(f32) + moved.astype(f32)).astype(bf16)

    low, high = add(low, 1), add(high, 3)
    low, high = add(low, 3), add(high, 1)
    return low, high


def chip_exchange(value):
    groups = [[dp_index(x, y, c) for x in range(SIDE) for y in range(SIDE)] for c in range(CORES)]
    return lax.all_to_all(
        value, "dp", split_axis=0, concat_axis=0, axis_index_groups=groups, tiled=True
    )


CHUNK = 256
DEPTH = 6


def this_core():
    return lax.axis_index("dp") % CORES


def upright(ref):
    rows = ref.shape[1]
    same = lax.broadcasted_iota(jnp.int32, (rows, rows), 0) == lax.broadcasted_iota(
        jnp.int32, (rows, rows), 1
    )
    turned = lax.dot_general(
        jnp.where(same, 1.0, 0.0).astype(bf16),
        ref[...].astype(f32).astype(bf16),
        (((1,), (1,)), ((), ())),
        preferred_element_type=f32,
    )
    return turned.astype(jnp.int32)


def route_tables(groups, picks, levels):
    rows = groups.shape[0]
    lane = lax.broadcasted_iota(jnp.int32, (rows, 128), 1)
    member = lane < 0
    for t in range(TOPG):
        member = member | (lane // 16 == groups[:, t : t + 1])
    below = lax.broadcasted_iota(jnp.int32, (rows, rows), 0) >= lax.broadcasted_iota(
        jnp.int32, (rows, rows), 1
    )
    counted = jnp.dot(
        jnp.where(below, 1.0, 0.0).astype(bf16),
        jnp.where(member, 1.0, 0.0).astype(bf16),
        preferred_element_type=f32,
    )
    places = jnp.where(member, counted, 0.0)
    table = jnp.where(lane - GROUPS * EPG == groups[:, :1], 1, 0)
    for k in range(picks.shape[1]):
        pick = picks[:, k : k + 1]
        group = jnp.zeros_like(pick)
        for t in range(TOPG):
            group = jnp.where(pick // EPG == t, groups[:, t : t + 1], group)
        table = jnp.where(lane == group * EPG + pick % EPG, levels[:, k : k + 1], table)
    return places.astype(bf16), table.astype(f32).astype(bf16)


def attend_kernel(
    lengths, q_ref, qr_ref, k_hbm, r_hbm, vu_hbm, groups_ref, picks_ref, levels_ref,
    kept_ref, given_ref, places_ref, k_ref, r_ref, mix_ref, vu_ref, k_sems, r_sems, vu_sem,
):
    rows, heads, lat = q_ref.shape
    positions = k_hbm.shape[1]
    chunks = positions // CHUNK
    width = vu_ref.shape[2]
    core = this_core()
    vu_copy = pltpu.make_async_copy(vu_hbm, vu_ref, vu_sem)

    def held(row):
        return (lengths[row] + CHUNK - 1) // CHUNK

    def copies(row, slot, chunk):
        at = pl.ds(chunk * CHUNK, CHUNK)
        return (
            pltpu.make_async_copy(
                k_hbm.at[row, at, :], k_ref.at[slot, at, :], k_sems.at[slot, chunk]
            ),
            pltpu.make_async_copy(
                r_hbm.at[row, :, at], r_ref.at[slot, :, at], r_sems.at[slot, chunk]
            ),
        )

    def each(row, slot, act):
        for chunk in range(chunks):

            @pl.when(chunk < held(row))
            def _():
                for copy in copies(row, slot, chunk):
                    act(copy)

    for row in range(DEPTH):
        each(row, row, lambda copy: copy.start())
    vu_copy.start()

    places, levels = route_tables(upright(groups_ref), upright(picks_ref), upright(levels_ref))
    places_ref[...] = places
    half = heads * width // 2
    first = core == 0
    kept_ref[:, half:] = jnp.where(first, places.astype(f32), levels.astype(f32)).astype(bf16)
    given_ref[:, half:] = jnp.where(first, levels.astype(f32), places.astype(f32)).astype(bf16)

    def step(row, carry):
        slot = lax.rem(row, DEPTH)
        each(row, slot, lambda copy: copy.wait())
        for count in range(1, chunks + 1):

            @pl.when(held(row) == count)
            def _():
                seen = count * CHUNK
                keys = k_ref[slot, :seen, :]
                scores = lax.dot_general(
                    q_ref[row], keys, (((1,), (1,)), ((), ())), preferred_element_type=f32
                )
                scores = scores + jnp.dot(
                    qr_ref[row], r_ref[slot, :, :seen], preferred_element_type=f32
                )
                scores = scores * score_scale
                place = lax.broadcasted_iota(jnp.int32, scores.shape, 1)
                scores = jnp.where(place < lengths[row], scores, far_below)
                highest = jnp.max(scores, axis=1, keepdims=True)
                raised = jnp.exp(scores - highest)
                weights = (raised / jnp.sum(raised, axis=1, keepdims=True)).astype(bf16)
                mix = jnp.dot(weights, keys, preferred_element_type=f32)
                at = pl.ds(pl.multiple_of(row * heads, heads), heads)
                for j in range(mix_ref.shape[0]):
                    mix_ref[j, at, :] = mix[:, j * 128 : (j + 1) * 128]

        @pl.when(row + DEPTH < rows)
        def _():
            each(row + DEPTH, slot, lambda copy: copy.start())

        return carry

    lax.fori_loop(0, rows, step, 0)
    vu_copy.wait()
    for side, ref in ((core, kept_ref), (1 - core, given_ref)):
        for i in range(heads // 2):
            h = side * (heads // 2) + i
            left = [mix_ref[j, pl.ds(h, rows, stride=heads), :] for j in range(mix_ref.shape[0])]
            left = jnp.concatenate(left, axis=1).astype(bf16)
            ref[:, i * width : (i + 1) * width] = jnp.dot(
                left, vu_ref[h], preferred_element_type=f32
            ).astype(bf16)


def attend(query_latent, query_rope, cache_latent, cache_rope, lengths, value_up, routing):
    rows, heads, lat = query_latent.shape
    rope = query_rope.shape[2]
    positions = cache_latent.shape[1]
    width = value_up.shape[2]
    whole = pl.BlockSpec(memory_space=pltpu.VMEM)
    small = pl.BlockSpec(memory_space=pltpu.SMEM)
    far = pl.BlockSpec(memory_space=pltpu.HBM)
    return pl.pallas_call(
        attend_kernel,
        in_specs=[small, whole, whole, far, far, far, whole, whole, whole],
        out_specs=(whole,) * 3,
        out_shape=(
            jax.ShapeDtypeStruct((rows, heads * width // 2 + 128), bf16),
            jax.ShapeDtypeStruct((rows, heads * width // 2 + 128), bf16),
            jax.ShapeDtypeStruct((rows, 128), bf16),
        ),
        scratch_shapes=[
            pltpu.VMEM((DEPTH, positions, lat), bf16),
            pltpu.VMEM((DEPTH, rope, positions), bf16),
            pltpu.VMEM((lat // 128, rows * heads, 128), f32),
            pltpu.VMEM((heads, lat, width), bf16),
            pltpu.SemaphoreType.DMA((DEPTH, positions // CHUNK)),
            pltpu.SemaphoreType.DMA((DEPTH, positions // CHUNK)),
            pltpu.SemaphoreType.DMA,
        ],
        compiler_params=pltpu.CompilerParams(vmem_limit_bytes=VMEM),
        cost_estimate=pl.CostEstimate(
            flops=4 * rows * heads * positions * lat,
            bytes_accessed=2 * rows * positions * (lat + rope),
            transcendentals=rows * heads * positions,
        ),
        name="attend",
    )(
        lengths, query_latent, query_rope, distant(cache_latent), distant(cache_rope), distant(value_up),
        *routing,
    )


def project_kernel(*refs):
    count = 2 * SIDE
    blocks_hbm, w_hbm = refs[:count], refs[count]
    low_ref, high_ref, places_ref, levels_ref = refs[count + 1 : count + 5]
    b_ref, w_ref, b_sems, w_sems = refs[count + 5 :]
    core = this_core()
    half = w_ref.shape[2]
    lanes = [pl.ds(pl.multiple_of(side * half, half), half) for side in (core, 1 - core)]
    w_copies = [
        pltpu.make_async_copy(w_hbm.at[:, lanes[n]], w_ref.at[n], w_sems.at[n]) for n in range(2)
    ]
    copies = [
        pltpu.make_async_copy(blocks_hbm[n], b_ref.at[n], b_sems.at[n]) for n in range(count)
    ]
    w_copies[0].start()
    for copy in copies[:SIDE]:
        copy.start()
    w_copies[1].start()
    for copy in copies[SIDE:]:
        copy.start()
    made = []
    for n in range(count):
        if n % SIDE == 0:
            w_copies[n // SIDE].wait()
        copies[n].wait()
        made.append(
            lax.dot_general(
                b_ref[n, :, :half], w_ref[n // SIDE], (((1,), (1,)), ((), ())),
                preferred_element_type=f32,
            )
        )
    rows = made[0].shape[0] // SIDE
    first = core == 0
    for i in range(SIDE):
        for j in range(SIDE):
            at, across = slice(j * rows, (j + 1) * rows), slice(i * rows, (i + 1) * rows)
            total = (made[i][at] + made[SIDE + j][across]).astype(bf16)
            (low_ref if i < 2 else high_ref)[i % 2 * SIDE + j] = total
            mine = b_ref[i, at, half:].astype(f32)
            theirs = b_ref[SIDE + j, across, half:].astype(f32)
            places_ref[i * SIDE + j] = jnp.where(first, mine, theirs).astype(bf16)
            levels_ref[i * SIDE + j] = jnp.where(first, theirs, mine).astype(bf16)


def project(blocks, swapped, out_proj):
    wide = blocks[0].shape[1]
    rows = blocks[0].shape[0] // SIDE
    columns = out_proj.shape[1]
    whole = pl.BlockSpec(memory_space=pltpu.VMEM)
    far = pl.BlockSpec(memory_space=pltpu.HBM)
    sums = jax.ShapeDtypeStruct((CHIPS // 2, rows, columns), bf16)
    table = jax.ShapeDtypeStruct((CHIPS, rows, 128), bf16)
    return pl.pallas_call(
        project_kernel,
        in_specs=[far] * (2 * SIDE + 1),
        out_specs=(whole,) * 4,
        out_shape=(sums, sums, table, table),
        scratch_shapes=[
            pltpu.VMEM((2 * SIDE, SIDE * rows, wide), bf16),
            pltpu.VMEM((2, columns, out_proj.shape[0] // 2), bf16),
            pltpu.SemaphoreType.DMA((2 * SIDE,)),
            pltpu.SemaphoreType.DMA((2,)),
        ],
        compiler_params=pltpu.CompilerParams(vmem_limit_bytes=VMEM),
        cost_estimate=pl.CostEstimate(flops=10**9, bytes_accessed=7 * 10**6, transcendentals=0),
        name="project",
    )(*blocks, *swapped, distant(out_proj.T))


def slot_masks(mark, rows):
    lane = lax.broadcasted_iota(jnp.int32, (2 * rows, 128), 1)
    wanted = (lane % CAP + 1).astype(f32)
    second = lax.broadcasted_iota(jnp.int32, (2 * rows, 128), 0) >= rows
    right_half = (lane % (2 * CAP) >= CAP) == second
    return jnp.where((mark == wanted) & right_half, 1.0, 0.0).astype(bf16)


def gate_kernel(table, places_ref, levels_ref, out_ref, made_ref):
    dp = lax.axis_index("dp")
    group = dp // EPG
    rows = places_ref.shape[1] // CORES
    lane = lax.broadcasted_iota(jnp.int32, (2 * rows, 128), 1)
    for quarter in range(CHIPS // QUARTER):
        for parity in range(CORES):
            for pair in range(QUARTER // 2):
                chips = (quarter * QUARTER + 2 * pair, quarter * QUARTER + 2 * pair + 1)
                at = slice(parity * rows, (parity + 1) * rows)
                mark = jnp.concatenate([places_ref[table[chip], at].astype(f32) for chip in chips])
                level = jnp.concatenate([levels_ref[table[chip], at].astype(f32) for chip in chips])
                total = jnp.sum(jnp.where(lane < GROUPS * EPG, level, 0.0), axis=1, keepdims=True)
                mine = jnp.sum(jnp.where(lane == dp, level, 0.0), axis=1, keepdims=True)
                home = jnp.sum(
                    jnp.where(lane == GROUPS * EPG + group, level, 0.0), axis=1, keepdims=True
                )
                gate = route_scale * mine / total
                high = gate.astype(bf16).astype(f32)
                values = jnp.where(lane == 0, high, jnp.where(lane == 1, gate - high, 0.0))
                values = jnp.where(lane == 2, home, values).astype(bf16)
                made_ref[...] = lax.dot_general(
                    slot_masks(mark, rows), values, (((0,), (0,)), ((), ())),
                    preferred_element_type=f32,
                )
                to = quarter * CORES * PART + parity * PART + pair * 2 * CAP
                out_ref[to : to + 2 * CAP] = made_ref[
                    pl.ds(pl.multiple_of(group * 2 * CAP, 2 * CAP), 2 * CAP)
                ]


def gate_table(table, places, levels):
    whole = pl.BlockSpec(memory_space=pltpu.VMEM)
    return pl.pallas_call(
        gate_kernel,
        in_specs=[pl.BlockSpec(memory_space=pltpu.SMEM), whole, whole],
        out_specs=whole,
        out_shape=jax.ShapeDtypeStruct((CHIPS * CORES * CAP, 128), f32),
        scratch_shapes=[pltpu.VMEM((128, 128), f32)],
        compiler_params=pltpu.CompilerParams(vmem_limit_bytes=VMEM),
        cost_estimate=pl.CostEstimate(flops=10**8, bytes_accessed=10**6, transcendentals=0),
        name="gate_table",
    )(table, places, levels)


def select_kernel(table, low_ref, high_ref, res_ref, places_ref, out_ref):
    rows = res_ref.shape[2]

    def attention_of(parity, chip):
        place = table[chip]
        side = CHIPS // 2
        inside = place % side
        at = slice(parity * rows, (parity + 1) * rows)
        return jnp.where(place < side, low_ref[inside, at].astype(f32), high_ref[inside, at].astype(f32))

    for parity in range(CORES):
        for pair in range(QUARTER // 2):
            quarters = []
            for quarter in range(CHIPS // QUARTER):
                parts = []
                marks = []
                for chip in (quarter * QUARTER + 2 * pair, quarter * QUARTER + 2 * pair + 1):
                    attention = attention_of(parity, chip)
                    parts.append((res_ref[chip, parity].astype(f32) + attention).astype(bf16))
                    at = slice(parity * rows, (parity + 1) * rows)
                    marks.append(places_ref[table[chip], at].astype(f32))
                hidden = jnp.concatenate(parts, axis=0)
                mark = jnp.concatenate(marks, axis=0)
                pick = slot_masks(mark, rows)
                quarters.append(
                    lax.dot_general(
                        pick, hidden, (((0,), (0,)), ((), ())), preferred_element_type=f32
                    )
                )
            chosen = jnp.concatenate(quarters, axis=1).astype(bf16)
            at = parity * PART + pair * 2 * CAP
            for group in range(GROUPS):
                block = chosen[group * 2 * CAP : (group + 1) * 2 * CAP]
                out_ref[2 * group, at : at + 2 * CAP, :] = block
                out_ref[2 * group + 1, at : at + 2 * CAP, :] = block


def select(table, parts, residual, places):
    columns = residual.shape[-1]
    whole = pl.BlockSpec(memory_space=pltpu.VMEM)
    return pl.pallas_call(
        select_kernel,
        in_specs=[pl.BlockSpec(memory_space=pltpu.SMEM)] + [whole] * 4,
        out_specs=whole,
        out_shape=jax.ShapeDtypeStruct(
            (CHIPS, CORES * PART, CHIPS // QUARTER * columns), bf16
        ),
        compiler_params=pltpu.CompilerParams(vmem_limit_bytes=VMEM),
        cost_estimate=pl.CostEstimate(flops=10**9, bytes_accessed=6 * 10**6, transcendentals=0),
        name="select",
    )(table, *parts, residual, places)


def unpacked(block, columns):
    parts = [block[:, q * columns : (q + 1) * columns] for q in range(CHIPS // QUARTER)]
    return jnp.concatenate(parts, axis=0)


def raise_up(x_ref, gw_hbm, uw_hbm, w_ref, sems, core, acc):
    columns, units = gw_hbm.shape[2:]
    span = CHIPS // QUARTER
    copies = []
    for part in range(QUARTER):
        chips = pl.ds(part * span, span)
        for n, source in enumerate((gw_hbm, uw_hbm)):
            lanes = slice(n * units, (n + 1) * units)
            copies.append(
                pltpu.make_async_copy(
                    source.at[chips, core], w_ref.at[chips, :, lanes], sems.at[part, n]
                )
            )
    for copy in copies:
        copy.start()
    for chip in range(CHIPS):
        if chip % span == 0:
            copies[chip // span * 2].wait()
            copies[chip // span * 2 + 1].wait()
        acc = acc + jnp.dot(unpacked(x_ref[chip], columns), w_ref[chip], preferred_element_type=f32)
    return acc


def up_kernel(x_ref, gw_hbm, uw_hbm, acc_ref, w_ref, sems):
    zero = jnp.zeros(acc_ref.shape, f32)
    acc_ref[...] = raise_up(x_ref, gw_hbm, uw_hbm, w_ref, sems, this_core(), zero)


def act_kernel(acc_ref, x_ref, gw_hbm, uw_hbm, act_ref, w_ref, sems):
    acc = raise_up(x_ref, gw_hbm, uw_hbm, w_ref, sems, 1 - this_core(), acc_ref[...])
    units = acc.shape[1] // 2
    gated = acc[:, :units]
    act_ref[...] = (gated / (1.0 + jnp.exp(-gated)) * acc[:, units:]).astype(bf16)


def up(x, gate_weight, up_weight, before=None):
    columns, units = gate_weight.shape[2:]
    slots = x.shape[1] * CHIPS // QUARTER
    whole = pl.BlockSpec(memory_space=pltpu.VMEM)
    far = pl.BlockSpec(memory_space=pltpu.HBM)
    operands = (x,) if before is None else (before, x)
    return pl.pallas_call(
        up_kernel if before is None else act_kernel,
        in_specs=[whole] * len(operands) + [far, far],
        out_specs=whole,
        out_shape=(
            jax.ShapeDtypeStruct((slots, 2 * units), f32)
            if before is None
            else jax.ShapeDtypeStruct((slots, units), bf16)
        ),
        scratch_shapes=[
            pltpu.VMEM((CHIPS, columns, 2 * units), bf16),
            pltpu.SemaphoreType.DMA((QUARTER, 2)),
        ],
        compiler_params=pltpu.CompilerParams(vmem_limit_bytes=VMEM),
        cost_estimate=pl.CostEstimate(
            flops=4 * CHIPS * slots * columns * units, bytes_accessed=6 * 10**6, transcendentals=0
        ),
        name="up",
    )(*operands, distant(gate_weight), distant(up_weight))


def cut_kernel(w_hbm, *refs):
    outs, held, sems = refs[:3], refs[3], refs[4]
    z = lax.axis_index("tensor")
    width = outs[0].shape[1]
    copies = []
    for n, by in enumerate((1, 3, 2)):
        lanes = pl.ds(pl.multiple_of((z + by) % PLANES * width, width), width)
        copies.append(pltpu.make_async_copy(w_hbm.at[:, lanes], held.at[n], sems.at[0, n]))
    for copy in copies:
        copy.start()
    leaving = []
    for n, copy in enumerate(copies):
        copy.wait()
        leaving.append(pltpu.make_async_copy(held.at[n], outs[n], sems.at[1, n]))
        leaving[n].start()
    for copy in leaving:
        copy.wait()


def cut(down_weight):
    units, width = down_weight.shape
    far = pl.BlockSpec(memory_space=pltpu.HBM)
    return pl.pallas_call(
        cut_kernel,
        in_specs=[far],
        out_specs=(far,) * 3,
        out_shape=(jax.ShapeDtypeStruct((units, width // PLANES), bf16),) * 3,
        scratch_shapes=[
            pltpu.VMEM((3, units, width // PLANES), bf16),
            pltpu.SemaphoreType.DMA((2, 3)),
        ],
        compiler_params=pltpu.CompilerParams(vmem_limit_bytes=VMEM),
        cost_estimate=pl.CostEstimate(flops=0, bytes_accessed=6 * 10**6, transcendentals=0),
        name="cut",
    )(distant(down_weight))


def down_kernel(a0, a1, a2, a3, own_hbm, w1, w2, w3, gates_ref, out_ref, w_ref, sems):
    acts = (a0, a1, a2, a3)
    z = lax.axis_index("tensor")
    units = a0.shape[1]
    width = out_ref.shape[1]
    lanes = pl.ds(pl.multiple_of(z * width, width), width)
    copies = [
        pltpu.make_async_copy(source, w_ref.at[n * units : (n + 1) * units], sems.at[n])
        for n, source in enumerate((own_hbm.at[:, lanes], w1, w2, w3))
    ]
    for copy in copies:
        copy.start()
    gate = gates_ref[:, 0:1] + gates_ref[:, 1:2]
    left = jnp.concatenate([act[...] for act in acts], axis=1)
    for copy in copies:
        copy.wait()
    block = 256
    for at in range(0, width, block):
        made = jnp.dot(left, w_ref[:, at : at + block], preferred_element_type=f32)
        out_ref[:, at : at + block] = (made * gate).astype(bf16)


def down(acts, own_weight, weights, gates):
    slots = acts[0].shape[0]
    units, width = weights[0].shape
    whole = pl.BlockSpec(memory_space=pltpu.VMEM)
    far = pl.BlockSpec(memory_space=pltpu.HBM)
    return pl.pallas_call(
        down_kernel,
        in_specs=[whole] * 4 + [far] * 4 + [whole],
        out_specs=whole,
        out_shape=jax.ShapeDtypeStruct((slots, width), bf16),
        scratch_shapes=[
            pltpu.VMEM((PLANES * units, width), bf16),
            pltpu.SemaphoreType.DMA((PLANES,)),
        ],
        compiler_params=pltpu.CompilerParams(vmem_limit_bytes=VMEM),
        cost_estimate=pl.CostEstimate(
            flops=8 * slots * units * width, bytes_accessed=6 * 10**6, transcendentals=0
        ),
        name="down",
    )(*acts, distant(own_weight), *[distant(weight) for weight in weights], gates)


def join_kernel(y_ref, received_ref, own_hbm, other_hbm, gates_ref, out_ref, x_ref, sems):
    half, width = out_ref.shape
    columns = own_hbm.shape[2] // (CHIPS // QUARTER)
    dp, z = lax.axis_index("dp"), lax.axis_index("tensor")
    core = dp % CORES
    step_here = dp // CORES % 2
    chips = QUARTER // 2
    near = pl.ds(z * QUARTER + step_here * chips, chips)
    rows = pl.ds(pl.multiple_of(core * PART, PART), PART)
    copies = [
        pltpu.make_async_copy(source.at[near, rows], x_ref.at[n], sems.at[n])
        for n, source in enumerate((own_hbm, other_hbm))
    ]
    for copy in copies:
        copy.start()
    both, homes = [], []
    for q in range(CHIPS // QUARTER):
        at = pl.ds(pl.multiple_of(q * CORES * PART + core * PART, PART), PART)
        both.append(y_ref[at, :].astype(f32) + received_ref[q * PART : (q + 1) * PART, :].astype(f32))
        homes.append(gates_ref[at, 2:3])
    total = jnp.concatenate(both, axis=0)
    home = jnp.concatenate(homes, axis=0)
    out_ref[...] = total.astype(bf16)
    for copy in copies:
        copy.wait()
    block = chips * CORES * columns
    flip = core == 1
    parts = []
    for chip in range(chips):
        mine = unpacked(x_ref[0, chip].astype(f32), columns)
        theirs = unpacked(x_ref[1, chip].astype(f32), columns)
        parts.append(jnp.where(flip, theirs, mine))
        parts.append(jnp.where(flip, mine, theirs))
    hidden = jnp.concatenate(parts, axis=1) * home
    for step in range(width // block):

        @pl.when(step_here == step)
        def _():
            at = slice(step * block, (step + 1) * block)
            out_ref[:, at] = (total[:, at] + hidden).astype(bf16)


def join(y, received, own, other, gates):
    whole = pl.BlockSpec(memory_space=pltpu.VMEM)
    far = pl.BlockSpec(memory_space=pltpu.HBM)
    return pl.pallas_call(
        join_kernel,
        in_specs=[whole, whole, far, far, whole],
        out_specs=whole,
        out_shape=jax.ShapeDtypeStruct(received.shape, bf16),
        scratch_shapes=[
            pltpu.VMEM((2, QUARTER // 2, PART, own.shape[2]), bf16),
            pltpu.SemaphoreType.DMA((2,)),
        ],
        compiler_params=pltpu.CompilerParams(vmem_limit_bytes=VMEM),
        cost_estimate=pl.CostEstimate(flops=10**6, bytes_accessed=2 * 10**6, transcendentals=0),
        name="join",
    )(y, received, own, other, gates)


def around(value, x_core):
    return [value] + [move_ring(value, by, x_core) for by in (1, 3, 2)]


def local(
    residual,
    query_latent,
    query_rope,
    cache_latent,
    cache_rope,
    lengths,
    value_up,
    out_proj,
    gate_proj,
    up_proj,
    down_proj,
    groups,
    expert_picks,
    gate_levels,
):
    rows, model = residual.shape
    columns = out_proj.shape[1]
    dp = lax.axis_index("dp")
    z = lax.axis_index("tensor")
    core = dp % CORES
    chip = dp // CORES
    here_x, here_y = chip // SIDE, chip % SIDE

    quarter = model // PLANES
    sent = cut(down_proj[0])
    downs = [move_z(part, by) for part, by in zip(sent, (1, 3, 2))]

    kept, given, places_here = attend(
        query_latent, query_rope, cache_latent, cache_rope, lengths, value_up,
        (groups.T, expert_picks.T, gate_levels.T),
    )
    weighting = places_here == (jnp.arange(128) % CAP + 1).astype(bf16)
    weighting = weighting.astype(bf16)

    given = move_core(given)
    flat = jnp.where(
        core == 0, jnp.concatenate([kept, given], axis=0), jnp.concatenate([given, kept], axis=0)
    )
    blocks = jnp.concatenate(around(flat, 0), axis=0)

    spread = residual.reshape(rows, CHIPS * CORES, columns).transpose(1, 0, 2)
    spread, blocks, downs[:2] = lax.optimization_barrier((spread, blocks, downs[:2]))
    residual_columns = lax.all_to_all(spread, "dp", split_axis=0, concat_axis=0, tiled=True)
    residual_columns = residual_columns.reshape(CHIPS, CORES, rows, columns)

    blocks = around(blocks, 1)
    blocks[3], downs[2], residual_columns = lax.optimization_barrier(
        (blocks[3], downs[2], residual_columns)
    )
    swapped = [move_core(block) for block in blocks]
    low, high, places_all, levels_all = project(blocks, swapped, out_proj)
    low, high = sum_z(low, high)

    far = jnp.arange(SIDE, dtype=jnp.int32)
    x_far = (here_x - far) % SIDE
    y_far = (here_y - far) % SIDE
    x_spot = (x_far ^ (x_far >> 1))[:, None]
    y_spot = (y_far ^ (y_far >> 1))[None, :]
    table = jnp.where(core == 0, y_spot * SIDE + x_spot, x_spot * SIDE + y_spot)
    table = table.reshape(CHIPS).astype(jnp.int32)
    gates = gate_table(table, places_all, levels_all)
    outgoing = select(table, (low, high), residual_columns, places_all)
    outgoing, gates = lax.optimization_barrier((outgoing, gates))

    own = chip_exchange(outgoing)
    other = move_core(own)
    gate_weight = gate_proj.reshape(CHIPS, CORES, columns, -1)
    up_weight = up_proj.reshape(CHIPS, CORES, columns, -1)
    acc = up(own, gate_weight, up_weight)
    act = up(other, gate_weight, up_weight, acc)
    acts = [act] + [move_z(act, by) for by in (1, 3, 2)]
    made = down(acts, down_proj[0], downs, gates)
    pieces = made.reshape(CHIPS // QUARTER, CORES, PART, quarter)
    theirs = lax.dynamic_index_in_dim(pieces, 1 - core, 1, keepdims=False)
    received = move_core(theirs.reshape(CHIPS * CAP, quarter))
    returning = join(made, received, own, other, gates)
    returning = returning.reshape(CHIPS, CAP, quarter)
    returning, weighting = lax.optimization_barrier((returning, weighting))

    returned = chip_exchange(returning).reshape(CHIPS * CAP, quarter)
    mixed = jnp.dot(weighting, returned, preferred_element_type=f32).astype(bf16)
    turned = jnp.stack([mixed] + [move_z(mixed, by) for by in (1, 3, 2)])
    back = (z - jnp.arange(PLANES)) % PLANES
    spot = back ^ (back >> 1)
    return jnp.concatenate(
        [lax.dynamic_index_in_dim(turned, spot[k], 0, keepdims=False) for k in range(PLANES)], axis=1
    )


def solution(mesh):
    return jax.shard_map(
        local,
        mesh=mesh,
        in_specs=(
            P("dp", None),
            P("dp", "tensor", None),
            P("dp", "tensor", None),
            P("dp", None, None),
            P("dp", None, None),
            P("dp"),
            P("tensor", None, None),
            P("tensor", "dp"),
            P("dp", None, "tensor"),
            P("dp", None, "tensor"),
            P("dp", "tensor", None),
            P("dp", None),
            P("dp", None),
            P("dp", None),
        ),
        out_specs=P("dp", None),
        check_vma=False,
    )
```

time: 338 us -> 166 us (0.49)
  waiting for transfers between devices: 185 us -> 31.9 us
  matrix products: 42.7 us -> 0.17 us
  Pallas kernels: 0 us -> 38.9 us
  blocking collectives: 71.1 us -> 42.5 us
  starting transfers between devices: 12.6 us -> 34.6 us
  between operations: 13.6 us -> 7.9 us
  local copies, waits for them, and re-layouts: 10.8 us -> 5.88 us
    psum x1 -> x0, waiting for transfers between devices: 81.3 us -> none  [expert_block(): return lax.psum(produced.astype(jnp.bfloat16), 'tensor')]
    all_to_all x2 -> x1, waiting for transfers between devices: 55.1 us -> 2.01 us  [local(): lax.all_to_all(spread, 'dp', split_axis=0, concat_axis=0, tiled=True)]
    all_gather x1 -> x0, waiting for transfers between devices: 48.3 us -> none  [local(): lax.all_gather(head_out, 'dp', axis=0, tiled=True)]
    dot_general x10 -> x1, matrix products: 42.7 us -> 0.17 us  [local(): jnp.dot(weighting, returned, preferred_element_type=f32).astype(bf16)]
    pallas_call x0 -> x9, Pallas kernels: none -> 38.9 us  [the longest x1 16.7 us: attend(): pl.pallas_call(attend_kernel, in_specs=[small, whole, whole, far, far, fa...]
    ppermute x0 -> x26, starting transfers between devices: none -> 30 us  [the longest x9 12.8 us: move_z(): lax.ppermute(value, 'tensor', [(z, (z + by) % PLANES) for z in range(PLAN...]
    ppermute x0 -> x26, waiting for transfers between devices: none -> 29.9 us  [the longest x9 15.2 us: move_z(): lax.ppermute(value, 'tensor', [(z, (z + by) % PLANES) for z in range(PLAN...]
    psum x1 -> x0, blocking collectives: 22.5 us -> none  [local(): summed_terms = lax.psum(column_terms, 'tensor')]
  transfers between devices with their start and end apart: 4 -> 27, of which waited for: 4 -> 16; matrix products, arithmetic and copies ran while one was open for 0% -> 3% of each run, Pallas kernels for 0% -> 12%
where the time goes in v2:
time: 166 us; the launch traced here: 165 us
  blocking collectives  42.5 us (26%)
  Pallas kernels  38.9 us (23%)
  starting transfers between devices  34.6 us (21%)
  waiting for transfers between devices  31.9 us (19%)
  between operations  7.9 us (5%)
  local copies, waits for them, and re-layouts  5.88 us (4%)
  other arithmetic  3.03 us (2%)
    all_to_all x2, blocking collectives, chip_exchange(): lax.all_to_all(value, 'dp', split_axis=0, concat_axis=0, axis_index_group...  42.5 us
    pallas_call x1, Pallas kernels, attend(): pl.pallas_call(attend_kernel, in_specs=[small, whole, whole, far, far, fa...  16.7 us
    ppermute x9, waiting for transfers between devices, move_z(): lax.ppermute(value, 'tensor', [(z, (z + by) % PLANES) for z in range(PLAN...  15.2 us
    ppermute x9, starting transfers between devices, move_z(): lax.ppermute(value, 'tensor', [(z, (z + by) % PLANES) for z in range(PLAN...  12.8 us
    ppermute x6, starting transfers between devices, move_ring(): return lax.ppermute(value, 'dp', place_pairs(place))  10 us
    pallas_call x1, Pallas kernels, project(): pl.pallas_call(project_kernel, in_specs=[far] * (2 * SIDE + 1), out_specs...  7.07 us
    ppermute x7, waiting for transfers between devices, move_core(): return lax.ppermute(value, 'dp', place_pairs(lambda x, y, c: (x, y, 1 - c)))  6.66 us
    pallas_call x2, Pallas kernels, up(): pl.pallas_call(up_kernel if before is None else act_kernel, in_specs=[who...  6.28 us
  transfers between devices with their start and end apart: 27, of which 16 were waited for; matrix products, arithmetic and copies ran while one was open for 3% of the time, Pallas kernels for 12%

profile of v2, /device:TPU:0, one launch (start us, length us, event | category | flops | bytes accessed | tf_op | source)
XLA Modules:
  0.0 164.9 jit_solution(2516589407070290688)
XLA Ops:
  0.0 2.8 %cut.1 = (bf16[256,1792]{1,0:T(8,128)(2,1)S(1)}, bf16[256,1792]{1,0:T(8,128)(2,1)S(1)}, bf16[256,1792]{1,0:T(8,128)(2,1)}) custom-call(bf16[256,7168]{1,0:T(8,128)(2,1)} %bitcast.42), custom_call_target="tpu_custom_call" | custom-call | bytes 6000000 | tf_op jit(solution)/shard_map/cut/pallas_call | solution.py:516
  2.8 2.1 %collective-permute-start.4 = (bf16[256,1792]{1,0:T(8,128)(2,1)S(1)}, bf16[256,1792]{1,0:T(8,128)(2,1)S(1)}, u32[]{:S(2)}, u32[]{:S(2)}) collective-permute-start(bf16[256,1792]{1,0:T(8,128)(2,1)S(1)} %get-tuple-element.28), channel_id=1, source_target_pairs={{0,1},{1,2},{2,3},{3,0},{4,5},{5,6},{6,7},{7,4},{8,9},{9,10},{10,1... | collective-permute-start | bytes 2752520 | tf_op jit(solution)/shard_map/ppermute | solution.py:57
  4.9 2.2 %collective-permute-start.5 = (bf16[256,1792]{1,0:T(8,128)(2,1)S(1)}, bf16[256,1792]{1,0:T(8,128)(2,1)}, u32[]{:S(2)}, u32[]{:S(2)}) collective-permute-start(bf16[256,1792]{1,0:T(8,128)(2,1)S(1)} %get-tuple-element.29), channel_id=1, source_target_pairs={{0,3},{1,0},{2,1},{3,2},{4,7},{5,4},{6,5},{7,6},{8,11},{9,8},{10,9... | collective-permute-start | bytes 2752520 | tf_op jit(solution)/shard_map/ppermute | solution.py:57
  7.2 16.7 %attend.1 = (bf16[16,2176]{1,0:T(8,128)(2,1)S(1)}, bf16[16,2176]{1,0:T(8,128)(2,1)S(1)}, bf16[16,128]{1,0:T(8,128)(2,1)S(1)}) custom-call(s32[16]{0:T(128)S(1)} %copy-done.13, bf16[16,32,512]{2,1,0:T(8,128)(2,1)S(1)} %copy-done.2, bf16[16,32,64]{2,1,0:T(8,128)(2,1)S(1)} %copy-done.5, bf16[16,1024,512]{2,1,0:T(8,128)(2,1)} %k_hbm.1, ...), custom_call_target="tpu_custom_call" | custom-call | flops 1073741824 | bytes 18874368 | tf_op jit(solution)/shard_map/attend/pallas_call | solution.py:221
  23.9 1.5 collective-permute-start
  26.3 2.5 %collective-permute-start.3 = (bf16[32,2176]{1,0:T(8,128)(2,1)S(1)}, bf16[32,2176]{1,0:T(8,128)(2,1)}, u32[]{:S(2)}, u32[]{:S(2)}) collective-permute-start(bf16[32,2176]{1,0:T(8,128)(2,1)S(1)} %maximum_select_fusion), channel_id=1, source_target_pairs={{0,64},{4,20},{8,72},{12,28},{16,80},{20,4},{24,88},{28,12},{32,96... | collective-permute-start | bytes 417800 | tf_op jit(solution)/shard_map/ppermute | solution.py:53
  28.8 1.2 collective-permute-start.2
  30.8 2.2 %collective-permute-done.3 = bf16[32,2176]{1,0:T(8,128)(2,1)} collective-permute-done((bf16[32,2176]{1,0:T(8,128)(2,1)S(1)}, bf16[32,2176]{1,0:T(8,128)(2,1)}, u32[]{:S(2)}, u32[]{:S(2)}) %collective-permute-start.3) | collective-permute-done | bytes 139296 | tf_op jit(solution)/shard_map/ppermute | solution.py:53
  33.0 1.5 collective-permute-start.9
  36.3 1.1 pad_maximum_fusion.refs_0_
  37.4 2.3 %collective-permute-start.8 = (bf16[128,2176]{1,0:T(8,128)(2,1)S(1)}, bf16[128,2176]{1,0:T(8,128)(2,1)S(1)}, u32[]{:S(2)}, u32[]{:S(2)}) collective-permute-start(bf16[128,2176]{1,0:T(8,128)(2,1)S(1)} %pad_maximum_fusion.refs_0_), channel_id=1, source_target_pairs={{0,16},{4,68},{8,24},{12,76},{16,0},{20,84},{24,8},{28,92},{32,48}... | collective-permute-start | bytes 1671176 | tf_op jit(solution)/shard_map/ppermute | solution.py:53
  39.7 2.8 %collective-permute-start.6 = (bf16[128,2176]{1,0:T(8,128)(2,1)S(1)}, bf16[128,2176]{1,0:T(8,128)(2,1)S(1)}, u32[]{:S(2)}, u32[]{:S(2)}) collective-permute-start(bf16[128,2176]{1,0:T(8,128)(2,1)S(1)} %pad_maximum_fusion.refs_0_), channel_id=1, source_target_pairs={{0,8},{4,36},{8,16},{12,44},{16,24},{20,52},{24,0},{28,60},{32,40}... | collective-permute-start | bytes 1671176 | tf_op jit(solution)/shard_map/ppermute | solution.py:53
  42.9 4.5 %all-to-all-start = ((bf16[32,16,224]{2,1,0:T(8,128)(2,1)}), bf16[32,16,224]{2,1,0:T(8,128)(2,1)S(1)}, u32[]{:S(2)}, u32[]{:S(2)}) async-start(bf16[32,16,224]{2,1,0:T(8,128)(2,1)} %bitcast.35), calls=%async_computation | async-start | bytes 524288 | tf_op jit(solution)/shard_map/all_to_all | solution.py:682
  47.9 8.8 %collective-permute-done.9.w3 = bf16[256,1792]{1,0:T(8,128)(2,1)} collective-permute-done((bf16[256,1792]{1,0:T(8,128)(2,1)}, bf16[256,1792]{1,0:T(8,128)(2,1)}, u32[]{:S(2)}, u32[]{:S(2)}) %collective-permute-start.9) | collective-permute-done | bytes 917536 | tf_op jit(solution)/shard_map/ppermute | solution.py:57
  56.6 2.0 %all-to-all-done = bf16[32,16,224]{2,1,0:T(8,128)(2,1)S(1)} async-done(((bf16[32,16,224]{2,1,0:T(8,128)(2,1)}), bf16[32,16,224]{2,1,0:T(8,128)(2,1)S(1)}, u32[]{:S(2)}, u32[]{:S(2)}) %all-to-all-start) | async-done | bytes 229408 | tf_op jit(solution)/shard_map/all_to_all | solution.py:682
  60.0 1.3 collective-permute-done.11.refs_5_
  63.0 7.1 %project.1 = (bf16[8,32,224]{2,1,0:T(8,128)(2,1)}, bf16[8,32,224]{2,1,0:T(8,128)(2,1)S(1)}, bf16[16,32,128]{2,1,0:T(8,128)(2,1)S(1)}, bf16[16,32,128]{2,1,0:T(8,128)(2,1)S(1)}) custom-call(bf16[128,2176]{1,0:T(8,128)(2,1)S(1)} %pad_maximum_fusion.refs_0_, bf16[128,2176]{1,0:T(8,128)(2,1)S(1)} %collective-permute-done.6.refs_1_, ...), custom_call_target="tpu_custom_call" | custom-call | flops 1000000000 | bytes 7000000 | tf_op jit(solution)/shard_map/project/pallas_call | solution.py:304
  71.5 2.4 %collective-permute-start.16 = (bf16[8,32,224]{2,1,0:T(8,128)(2,1)S(1)}, bf16[8,32,224]{2,1,0:T(8,128)(2,1)S(1)}, u32[]{:S(2)}, u32[]{:S(2)}) collective-permute-start(bf16[8,32,224]{2,1,0:T(8,128)(2,1)S(1)} %get-tuple-element.35), channel_id=1, source_target_pairs={{0,3},{1,2},{2,1},{3,0},{4,7},{5,6},{6,5},{7,4},{8,11},{9,10},{10,... | collective-permute-start | bytes 344072 | tf_op jit(solution)/shard_map/ppermute | solution.py:63
  75.7 1.1 gate_table.1.gates_ref
  78.1 2.0 %collective-permute-start.15 = (bf16[8,32,224]{2,1,0:T(8,128)(2,1)S(1)}, bf16[8,32,224]{2,1,0:T(8,128)(2,1)S(1)}, u32[]{:S(2)}, u32[]{:S(2)}) collective-permute-start(bf16[8,32,224]{2,1,0:T(8,128)(2,1)S(1)} %add_convert_fusion.3), channel_id=1, source_target_pairs={{0,3},{1,2},{2,1},{3,0},{4,7},{5,6},{6,5},{7,4},{8,11},{9,10},{10,... | collective-permute-start | bytes 344072 | tf_op jit(solution)/shard_map/ppermute | solution.py:63
  80.4 3.9 %collective-permute-done.15 = bf16[8,32,224]{2,1,0:T(8,128)(2,1)S(1)} collective-permute-done((bf16[8,32,224]{2,1,0:T(8,128)(2,1)S(1)}, bf16[8,32,224]{2,1,0:T(8,128)(2,1)S(1)}, u32[]{:S(2)}, u32[]{:S(2)}) %collective-permute-start.15) | collective-permute-done | bytes 114720 | tf_op jit(solution)/shard_map/ppermute | solution.py:63
  85.4 1.1 select.41
  86.5 27.8 %all_to_all.15.x_ref.own_hbm = bf16[16,64,896]{2,1,0:T(8,128)(2,1)S(1)} all-to-all(bf16[16,64,896]{2,1,0:T(8,128)(2,1)S(1)} %select.41), channel_id=1, replica_groups={{0,8,16,24,32,40,48,56,64,72,80,88,96,104,112,120},{4,12,20,28,36,44,52..., dimensions={0} | all-to-all | bytes 3670016 | tf_op jit(solution)/shard_map/all_to_all | solution.py:73
  114.3 2.8 %up.2.acc_ref = f32[256,512]{1,0:T(8,128)S(1)} custom-call(bf16[16,64,896]{2,1,0:T(8,128)(2,1)S(1)} %all_to_all.15.x_ref.own_hbm, bf16[16,2,224,256]{3,2,1,0:T(8,128)(2,1)} %bitcast.44, bf16[16,2,224,256]{3,2,1,0:T(8,128)(2,1)} %bitcast.46), custom_call_target="tpu_custom_call" | custom-call | flops 939524096 | bytes 6000000 | tf_op jit(solution)/shard_map/up/pallas_call | solution.py:473
  118.1 3.5 %up.3.a0 = bf16[256,256]{1,0:T(8,128)(2,1)S(1)} custom-call(f32[256,512]{1,0:T(8,128)S(1)} %up.2.acc_ref, bf16[16,64,896]{2,1,0:T(8,128)(2,1)S(1)} %collective-permute-done.18.x_ref.other_hbm, bf16[16,2,224,256]{3,2,1,0:T(8,128)(2,1)} %bitcast.45, bf16[16,2,224,256]{3,2,1,0:T(8,128)(2,1)} %bitcast.47), custom_call_target="tpu_custom_call" | custom-call | flops 939524096 | bytes 6000000 | tf_op jit(solution)/shard_map/up/pallas_call | solution.py:473
  122.0 2.9 %collective-permute-start.20 = (bf16[256,256]{1,0:T(8,128)(2,1)S(1)}, bf16[256,256]{1,0:T(8,128)(2,1)S(1)}, u32[]{:S(2)}, u32[]{:S(2)}) collective-permute-start(bf16[256,256]{1,0:T(8,128)(2,1)S(1)} %up.3.a0), channel_id=1, source_target_pairs={{0,3},{1,0},{2,1},{3,2},{4,7},{5,4},{6,5},{7,6},{8,11},{9,8},{10,9... | collective-permute-start | bytes 393224 | tf_op jit(solution)/shard_map/ppermute | solution.py:57
  125.0 3.5 %collective-permute-done.19.a1 = bf16[256,256]{1,0:T(8,128)(2,1)S(1)} collective-permute-done((bf16[256,256]{1,0:T(8,128)(2,1)S(1)}, bf16[256,256]{1,0:T(8,128)(2,1)S(1)}, u32[]{:S(2)}, u32[]{:S(2)}) %collective-permute-start.19) | collective-permute-done | bytes 131104 | tf_op jit(solution)/shard_map/ppermute | solution.py:57
  128.4 2.1 %collective-permute-done.20.a2 = bf16[256,256]{1,0:T(8,128)(2,1)S(1)} collective-permute-done((bf16[256,256]{1,0:T(8,128)(2,1)S(1)}, bf16[256,256]{1,0:T(8,128)(2,1)S(1)}, u32[]{:S(2)}, u32[]{:S(2)}) %collective-permute-start.20) | collective-permute-done | bytes 131104 | tf_op jit(solution)/shard_map/ppermute | solution.py:57
  131.4 3.3 %down.1.y_ref = bf16[256,1792]{1,0:T(8,128)(2,1)S(1)} custom-call(bf16[256,256]{1,0:T(8,128)(2,1)S(1)} %up.3.a0, bf16[256,256]{1,0:T(8,128)(2,1)S(1)} %collective-permute-done.19.a1, bf16[256,256]{1,0:T(8,128)(2,1)S(1)} %collective-permute-done.20.a2, bf16[256,256]{1,0:T(8,128)(2,1)S(1)} %collective-permute-done.21.a3, bf16[256,7168]{1,0:T(8,128)(2,1)} %bitcast.43, ...), custom_call_target="tpu_custom_call" | custom-call | flops 939524096 | bytes 6000000 | tf_op jit(solution)/shard_map/down/pallas_call | solution.py:558
  134.9 1.8 %collective-permute-done.22.received_ref = bf16[128,1792]{1,0:T(8,128)(2,1)S(1)} collective-permute-done((bf16[128,1792]{1,0:T(8,128)(2,1)S(1)}, bf16[128,1792]{1,0:T(8,128)(2,1)S(1)}, u32[]{:S(2)}, u32[]{:S(2)}) %collective-permute-start.22) | collective-permute-done | bytes 458784 | tf_op jit(solution)/shard_map/ppermute | solution.py:46
  137.2 14.7 %all_to_all.16 = bf16[16,8,1792]{2,1,0:T(8,128)(2,1)S(1)} all-to-all(bf16[16,8,1792]{2,1,0:T(8,128)(2,1)S(1)} %bitcast.37), channel_id=1, replica_groups={{0,8,16,24,32,40,48,56,64,72,80,88,96,104,112,120},{4,12,20,28,36,44,52..., dimensions={0} | all-to-all | bytes 917504 | tf_op jit(solution)/shard_map/all_to_all | solution.py:73
  152.6 3.0 %collective-permute-start.24 = (bf16[16,1792]{1,0:T(8,128)(2,1)S(1)}, bf16[16,1792]{1,0:T(8,128)(2,1)S(1)}, u32[]{:S(2)}, u32[]{:S(2)}) collective-permute-start(bf16[16,1792]{1,0:T(8,128)(2,1)S(1)} %convolution_convert_fusion), channel_id=1, source_target_pairs={{0,3},{1,0},{2,1},{3,2},{4,7},{5,4},{6,5},{7,6},{8,11},{9,8},{10,9... | collective-permute-start | bytes 172040 | tf_op jit(solution)/shard_map/ppermute | solution.py:57
  (86 shorter events, 18.7 us)
Async XLA Ops:
  0.0 7.1 %copy-start.11 = (s32[16,8]{0,1:T(8,128)S(1)}, s32[16,8]{0,1:T(8,128)}, u32[]{:S(2)}) copy-start(s32[16,8]{0,1:T(8,128)} %param.27) | copy-start | bytes 1540
  0.0 7.1 %copy-start.12 = (s32[16,4]{0,1:T(4,128)S(1)}, s32[16,4]{0,1:T(4,128)}, u32[]{:S(2)}) copy-start(s32[16,4]{0,1:T(4,128)} %param.25) | copy-start | bytes 772
  0.0 7.1 %copy-start.13 = (s32[16]{0:T(128)S(1)}, s32[16]{0:T(128)}, u32[]{:S(2)}) copy-start(s32[16]{0:T(128)} %lengths.1) | copy-start | bytes 196
  2.8 34.6 %collective-permute-start.4 = (bf16[256,1792]{1,0:T(8,128)(2,1)S(1)}, bf16[256,1792]{1,0:T(8,128)(2,1)S(1)}, u32[]{:S(2)}, u32[]{:S(2)}) collective-permute-start(bf16[256,1792]{1,0:T(8,128)(2,1)S(1)} %get-tuple-element.28), channel_id=1, source_target_pairs={{0,1},{1,2},{2,3},{3,0},{4,5},{5,6},{6,7},{7,4},{8,9},{9,10},{10,1... | collective-permute-start | bytes 2752520 | tf_op jit(solution)/shard_map/ppermute | solution.py:57
  4.9 32.5 %collective-permute-start.5 = (bf16[256,1792]{1,0:T(8,128)(2,1)S(1)}, bf16[256,1792]{1,0:T(8,128)(2,1)}, u32[]{:S(2)}, u32[]{:S(2)}) collective-permute-start(bf16[256,1792]{1,0:T(8,128)(2,1)S(1)} %get-tuple-element.29), channel_id=1, source_target_pairs={{0,3},{1,0},{2,1},{3,2},{4,7},{5,4},{6,5},{7,6},{8,11},{9,8},{10,9... | collective-permute-start | bytes 2752520 | tf_op jit(solution)/shard_map/ppermute | solution.py:57
  7.2 27.4 %copy-start.15 = (bf16[16,7168]{1,0:T(8,128)(2,1)S(1)}, bf16[16,7168]{1,0:T(8,128)(2,1)}, u32[]{:S(2)}) copy-start(bf16[16,7168]{1,0:T(8,128)(2,1)} %param.14) | copy-start | bytes 688132
  23.9 2.4 %collective-permute-start = (bf16[16,2176]{1,0:T(8,128)(2,1)S(1)}, bf16[16,2176]{1,0:T(8,128)(2,1)S(1)}, u32[]{:S(2)}, u32[]{:S(2)}) collective-permute-start(bf16[16,2176]{1,0:T(8,128)(2,1)S(1)} %get-tuple-element.27), channel_id=1, source_target_pairs={{0,4},{4,0},{8,12},{12,8},{16,20},{20,16},{24,28},{28,24},{32,36},... | collective-permute-start | bytes 208904 | tf_op jit(solution)/shard_map/ppermute | solution.py:46
  26.3 6.7 %collective-permute-start.3 = (bf16[32,2176]{1,0:T(8,128)(2,1)S(1)}, bf16[32,2176]{1,0:T(8,128)(2,1)}, u32[]{:S(2)}, u32[]{:S(2)}) collective-permute-start(bf16[32,2176]{1,0:T(8,128)(2,1)S(1)} %maximum_select_fusion), channel_id=1, source_target_pairs={{0,64},{4,20},{8,72},{12,28},{16,80},{20,4},{24,88},{28,12},{32,96... | collective-permute-start | bytes 417800 | tf_op jit(solution)/shard_map/ppermute | solution.py:53
  28.8 7.0 %collective-permute-start.2 = (bf16[32,2176]{1,0:T(8,128)(2,1)S(1)}, bf16[32,2176]{1,0:T(8,128)(2,1)}, u32[]{:S(2)}, u32[]{:S(2)}) collective-permute-start(bf16[32,2176]{1,0:T(8,128)(2,1)S(1)} %maximum_select_fusion), channel_id=1, source_target_pairs={{0,96},{4,28},{8,104},{12,4},{16,112},{20,12},{24,120},{28,20},{32... | collective-permute-start | bytes 417800 | tf_op jit(solution)/shard_map/ppermute | solution.py:53
  29.9 6.4 %collective-permute-start.1 = (bf16[32,2176]{1,0:T(8,128)(2,1)S(1)}, bf16[32,2176]{1,0:T(8,128)(2,1)}, u32[]{:S(2)}, u32[]{:S(2)}) collective-permute-start(bf16[32,2176]{1,0:T(8,128)(2,1)S(1)} %maximum_select_fusion), channel_id=1, source_target_pairs={{0,32},{4,12},{8,40},{12,20},{16,48},{20,28},{24,56},{28,4},{32,64... | collective-permute-start | bytes 417800 | tf_op jit(solution)/shard_map/ppermute | solution.py:53
  33.0 23.6 %collective-permute-start.9 = (bf16[256,1792]{1,0:T(8,128)(2,1)}, bf16[256,1792]{1,0:T(8,128)(2,1)}, u32[]{:S(2)}, u32[]{:S(2)}) collective-permute-start(bf16[256,1792]{1,0:T(8,128)(2,1)} %get-tuple-element.31), channel_id=1, source_target_pairs={{0,2},{1,3},{2,0},{3,1},{4,6},{5,7},{6,4},{7,5},{8,10},{9,11},{10,... | collective-permute-start | bytes 2752520 | tf_op jit(solution)/shard_map/ppermute | solution.py:57
  37.4 21.9 %collective-permute-start.8 = (bf16[128,2176]{1,0:T(8,128)(2,1)S(1)}, bf16[128,2176]{1,0:T(8,128)(2,1)S(1)}, u32[]{:S(2)}, u32[]{:S(2)}) collective-permute-start(bf16[128,2176]{1,0:T(8,128)(2,1)S(1)} %pad_maximum_fusion.refs_0_), channel_id=1, source_target_pairs={{0,16},{4,68},{8,24},{12,76},{16,0},{20,84},{24,8},{28,92},{32,48}... | collective-permute-start | bytes 1671176 | tf_op jit(solution)/shard_map/ppermute | solution.py:53
  39.7 19.6 %collective-permute-start.6 = (bf16[128,2176]{1,0:T(8,128)(2,1)S(1)}, bf16[128,2176]{1,0:T(8,128)(2,1)S(1)}, u32[]{:S(2)}, u32[]{:S(2)}) collective-permute-start(bf16[128,2176]{1,0:T(8,128)(2,1)S(1)} %pad_maximum_fusion.refs_0_), channel_id=1, source_target_pairs={{0,8},{4,36},{8,16},{12,44},{16,24},{20,52},{24,0},{28,60},{32,40}... | collective-permute-start | bytes 1671176 | tf_op jit(solution)/shard_map/ppermute | solution.py:53
  42.5 17.0 %collective-permute-start.7 = (bf16[128,2176]{1,0:T(8,128)(2,1)S(1)}, bf16[128,2176]{1,0:T(8,128)(2,1)S(1)}, u32[]{:S(2)}, u32[]{:S(2)}) collective-permute-start(bf16[128,2176]{1,0:T(8,128)(2,1)S(1)} %pad_maximum_fusion.refs_0_), channel_id=1, source_target_pairs={{0,24},{4,100},{8,0},{12,108},{16,8},{20,116},{24,16},{28,124},{32... | collective-permute-start | bytes 1671176 | tf_op jit(solution)/shard_map/ppermute | solution.py:53
  42.9 15.7 %all-to-all-start = ((bf16[32,16,224]{2,1,0:T(8,128)(2,1)}), bf16[32,16,224]{2,1,0:T(8,128)(2,1)S(1)}, u32[]{:S(2)}, u32[]{:S(2)}) async-start(bf16[32,16,224]{2,1,0:T(8,128)(2,1)} %bitcast.35), calls=%async_computation | async-start | bytes 524288 | tf_op jit(solution)/shard_map/all_to_all | solution.py:682
  47.5 12.5 %collective-permute-start.10 = (bf16[128,2176]{1,0:T(8,128)(2,1)S(1)}, bf16[128,2176]{1,0:T(8,128)(2,1)S(1)}, u32[]{:S(2)}, u32[]{:S(2)}) collective-permute-start(bf16[128,2176]{1,0:T(8,128)(2,1)S(1)} %pad_maximum_fusion.refs_0_), channel_id=1, source_target_pairs={{0,4},{4,0},{8,12},{12,8},{16,20},{20,16},{24,28},{28,24},{32,36},... | collective-permute-start | bytes 1671176 | tf_op jit(solution)/shard_map/ppermute | solution.py:46
  59.3 2.0 %collective-permute-start.11 = (bf16[128,2176]{1,0:T(8,128)(2,1)S(1)}, bf16[128,2176]{1,0:T(8,128)(2,1)S(1)}, u32[]{:S(2)}, u32[]{:S(2)}) collective-permute-start(bf16[128,2176]{1,0:T(8,128)(2,1)S(1)} %collective-permute-done.6.refs_1_), channel_id=1, source_target_pairs={{0,4},{4,0},{8,12},{12,8},{16,20},{20,16},{24,28},{28,24},{32,36},... | collective-permute-start | bytes 1671176 | tf_op jit(solution)/shard_map/ppermute | solution.py:46
  59.4 2.8 %collective-permute-start.12 = (bf16[128,2176]{1,0:T(8,128)(2,1)S(1)}, bf16[128,2176]{1,0:T(8,128)(2,1)}, u32[]{:S(2)}, u32[]{:S(2)}) collective-permute-start(bf16[128,2176]{1,0:T(8,128)(2,1)S(1)} %collective-permute-done.7.refs_2_), channel_id=1, source_target_pairs={{0,4},{4,0},{8,12},{12,8},{16,20},{20,16},{24,28},{28,24},{32,36},... | collective-permute-start | bytes 1671176 | tf_op jit(solution)/shard_map/ppermute | solution.py:46
  59.8 3.2 %collective-permute-start.13 = (bf16[128,2176]{1,0:T(8,128)(2,1)S(1)}, bf16[128,2176]{1,0:T(8,128)(2,1)}, u32[]{:S(2)}, u32[]{:S(2)}) collective-permute-start(bf16[128,2176]{1,0:T(8,128)(2,1)S(1)} %collective-permute-done.8.refs_3_), channel_id=1, source_target_pairs={{0,4},{4,0},{8,12},{12,8},{16,20},{20,16},{24,28},{28,24},{32,36},... | collective-permute-start | bytes 1671176 | tf_op jit(solution)/shard_map/ppermute | solution.py:46
  71.4 14.0 %copy-start.4 = (bf16[32,16,224]{2,1,0:T(8,128)(2,1)S(1)}, bf16[32,16,224]{2,1,0:T(8,128)(2,1)}, u32[]{:S(2)}) copy-start(bf16[32,16,224]{2,1,0:T(8,128)(2,1)} %copy-done.3) | copy-start | bytes 688132
  71.4 5.7 %collective-permute-start.14 = (bf16[8,32,224]{2,1,0:T(8,128)(2,1)}, bf16[8,32,224]{2,1,0:T(8,128)(2,1)S(1)}, u32[]{:S(2)}, u32[]{:S(2)}) collective-permute-start(bf16[8,32,224]{2,1,0:T(8,128)(2,1)} %get-tuple-element.34), channel_id=1, source_target_pairs={{0,1},{1,0},{2,3},{3,2},{4,5},{5,4},{6,7},{7,6},{8,9},{9,8},{10,11... | collective-permute-start | bytes 344072 | tf_op jit(solution)/shard_map/ppermute | solution.py:63
  71.5 8.5 %collective-permute-start.16 = (bf16[8,32,224]{2,1,0:T(8,128)(2,1)S(1)}, bf16[8,32,224]{2,1,0:T(8,128)(2,1)S(1)}, u32[]{:S(2)}, u32[]{:S(2)}) collective-permute-start(bf16[8,32,224]{2,1,0:T(8,128)(2,1)S(1)} %get-tuple-element.35), channel_id=1, source_target_pairs={{0,3},{1,2},{2,1},{3,0},{4,7},{5,6},{6,5},{7,4},{8,11},{9,10},{10,... | collective-permute-start | bytes 344072 | tf_op jit(solution)/shard_map/ppermute | solution.py:63
  78.1 6.3 %collective-permute-start.15 = (bf16[8,32,224]{2,1,0:T(8,128)(2,1)S(1)}, bf16[8,32,224]{2,1,0:T(8,128)(2,1)S(1)}, u32[]{:S(2)}, u32[]{:S(2)}) collective-permute-start(bf16[8,32,224]{2,1,0:T(8,128)(2,1)S(1)} %add_convert_fusion.3), channel_id=1, source_target_pairs={{0,3},{1,2},{2,1},{3,0},{4,7},{5,6},{6,5},{7,4},{8,11},{9,10},{10,... | collective-permute-start | bytes 344072 | tf_op jit(solution)/shard_map/ppermute | solution.py:63
  80.1 5.2 %collective-permute-start.17 = (bf16[8,32,224]{2,1,0:T(8,128)(2,1)S(1)}, bf16[8,32,224]{2,1,0:T(8,128)(2,1)S(1)}, u32[]{:S(2)}, u32[]{:S(2)}) collective-permute-start(bf16[8,32,224]{2,1,0:T(8,128)(2,1)S(1)} %add_convert_fusion.1), channel_id=1, source_target_pairs={{0,1},{1,0},{2,3},{3,2},{4,5},{5,4},{6,7},{7,6},{8,9},{9,8},{10,11... | collective-permute-start | bytes 344072 | tf_op jit(solution)/shard_map/ppermute | solution.py:63
  114.3 3.8 %collective-permute-start.18 = (bf16[16,64,896]{2,1,0:T(8,128)(2,1)S(1)}, bf16[16,64,896]{2,1,0:T(8,128)(2,1)S(1)}, u32[]{:S(2)}, u32[]{:S(2)}) collective-permute-start(bf16[16,64,896]{2,1,0:T(8,128)(2,1)S(1)} %all_to_all.15.x_ref.own_hbm), channel_id=1, source_target_pairs={{0,4},{4,0},{8,12},{12,8},{16,20},{20,16},{24,28},{28,24},{32,36},... | collective-permute-start | bytes 5505032 | tf_op jit(solution)/shard_map/ppermute | solution.py:46
  121.6 6.8 %collective-permute-start.19 = (bf16[256,256]{1,0:T(8,128)(2,1)S(1)}, bf16[256,256]{1,0:T(8,128)(2,1)S(1)}, u32[]{:S(2)}, u32[]{:S(2)}) collective-permute-start(bf16[256,256]{1,0:T(8,128)(2,1)S(1)} %up.3.a0), channel_id=1, source_target_pairs={{0,1},{1,2},{2,3},{3,0},{4,5},{5,6},{6,7},{7,4},{8,9},{9,10},{10,1... | collective-permute-start | bytes 393224 | tf_op jit(solution)/shard_map/ppermute | solution.py:57
  122.0 8.5 %collective-permute-start.20 = (bf16[256,256]{1,0:T(8,128)(2,1)S(1)}, bf16[256,256]{1,0:T(8,128)(2,1)S(1)}, u32[]{:S(2)}, u32[]{:S(2)}) collective-permute-start(bf16[256,256]{1,0:T(8,128)(2,1)S(1)} %up.3.a0), channel_id=1, source_target_pairs={{0,3},{1,0},{2,1},{3,2},{4,7},{5,4},{6,5},{7,6},{8,11},{9,8},{10,9... | collective-permute-start | bytes 393224 | tf_op jit(solution)/shard_map/ppermute | solution.py:57
  124.9 6.5 %collective-permute-start.21 = (bf16[256,256]{1,0:T(8,128)(2,1)S(1)}, bf16[256,256]{1,0:T(8,128)(2,1)S(1)}, u32[]{:S(2)}, u32[]{:S(2)}) collective-permute-start(bf16[256,256]{1,0:T(8,128)(2,1)S(1)} %up.3.a0), channel_id=1, source_target_pairs={{0,2},{1,3},{2,0},{3,1},{4,6},{5,7},{6,4},{7,5},{8,10},{9,11},{10,... | collective-permute-start | bytes 393224 | tf_op jit(solution)/shard_map/ppermute | solution.py:57
  134.8 1.9 %collective-permute-start.22 = (bf16[128,1792]{1,0:T(8,128)(2,1)S(1)}, bf16[128,1792]{1,0:T(8,128)(2,1)S(1)}, u32[]{:S(2)}, u32[]{:S(2)}) collective-permute-start(bf16[128,1792]{1,0:T(8,128)(2,1)S(1)} %bitcast.49), channel_id=1, source_target_pairs={{0,4},{4,0},{8,12},{12,8},{16,20},{20,16},{24,28},{28,24},{32,36},... | collective-permute-start | bytes 1376264 | tf_op jit(solution)/shard_map/ppermute | solution.py:46
  152.1 12.0 %collective-permute-start.25 = (bf16[16,1792]{1,0:T(8,128)(2,1)S(1)}, bf16[16,1792]{1,0:T(8,128)(2,1)S(1)}, u32[]{:S(2)}, u32[]{:S(2)}) collective-permute-start(bf16[16,1792]{1,0:T(8,128)(2,1)S(1)} %convolution_convert_fusion), channel_id=1, source_target_pairs={{0,2},{1,3},{2,0},{3,1},{4,6},{5,7},{6,4},{7,5},{8,10},{9,11},{10,... | collective-permute-start | bytes 172040 | tf_op jit(solution)/shard_map/ppermute | solution.py:57
  152.6 11.5 %collective-permute-start.24 = (bf16[16,1792]{1,0:T(8,128)(2,1)S(1)}, bf16[16,1792]{1,0:T(8,128)(2,1)S(1)}, u32[]{:S(2)}, u32[]{:S(2)}) collective-permute-start(bf16[16,1792]{1,0:T(8,128)(2,1)S(1)} %convolution_convert_fusion), channel_id=1, source_target_pairs={{0,3},{1,0},{2,1},{3,2},{4,7},{5,4},{6,5},{7,6},{8,11},{9,8},{10,9... | collective-permute-start | bytes 172040 | tf_op jit(solution)/shard_map/ppermute | solution.py:57
  155.6 8.5 %collective-permute-start.23 = (bf16[16,1792]{1,0:T(8,128)(2,1)S(1)}, bf16[16,1792]{1,0:T(8,128)(2,1)S(1)}, u32[]{:S(2)}, u32[]{:S(2)}) collective-permute-start(bf16[16,1792]{1,0:T(8,128)(2,1)S(1)} %convolution_convert_fusion), channel_id=1, source_target_pairs={{0,1},{1,2},{2,3},{3,0},{4,5},{5,6},{6,7},{7,4},{8,9},{9,10},{10,1... | collective-permute-start | bytes 172040 | tf_op jit(solution)/shard_map/ppermute | solution.py:57
  (11 other events, 39.5 us)

commit v3 on v2

--- a/solution.py
+++ b/solution.py
@@ -57,6 +57,11 @@
     return lax.ppermute(value, "tensor", [(z, (z + by) % PLANES) for z in range(PLANES)])
 
 
+def spread_z(value):
+    copies = jnp.broadcast_to(value[None], (PLANES,) + value.shape)
+    return lax.all_to_all(copies, "tensor", split_axis=0, concat_axis=0, tiled=True)
+
+
 def sum_z(low, high):
     def add(block, mask):
         pairs = [(z, z ^ mask) for z in range(PLANES)]
@@ -75,12 +80,16 @@
     )
 
 
-CHUNK = 256
 DEPTH = 6
 
 
 def this_core():
     return lax.axis_index("dp") % CORES
+
+
+def quarter_lanes(by, width):
+    z = lax.axis_index("tensor")
+    return pl.ds(pl.multiple_of((z + by) % PLANES * width, width), width)
 
 
 def upright(ref):
@@ -123,42 +132,37 @@
 
 
 def attend_kernel(
-    lengths, q_ref, qr_ref, k_hbm, r_hbm, vu_hbm, groups_ref, picks_ref, levels_ref,
-    kept_ref, given_ref, places_ref, k_ref, r_ref, mix_ref, vu_ref, k_sems, r_sems, vu_sem,
+    lengths, q_ref, qr_ref, k_hbm, r_hbm, vu_hbm, dw_hbm, res_ref, groups_ref, picks_ref, levels_ref,
+    kept_ref, given_ref, places_ref, spread_ref, cut_1, cut_3,
+    k_ref, r_ref, mix_ref, vu_ref, cut_ref, sems, cut_sems, vu_sem,
 ):
     rows, heads, lat = q_ref.shape
-    positions = k_hbm.shape[1]
-    chunks = positions // CHUNK
     width = vu_ref.shape[2]
+    cuts = (cut_1, cut_3)
     core = this_core()
     vu_copy = pltpu.make_async_copy(vu_hbm, vu_ref, vu_sem)
 
-    def held(row):
-        return (lengths[row] + CHUNK - 1) // CHUNK
-
-    def copies(row, slot, chunk):
-        at = pl.ds(chunk * CHUNK, CHUNK)
+    def copies(row, slot):
         return (
-            pltpu.make_async_copy(
-                k_hbm.at[row, at, :], k_ref.at[slot, at, :], k_sems.at[slot, chunk]
-            ),
-            pltpu.make_async_copy(
-                r_hbm.at[row, :, at], r_ref.at[slot, :, at], r_sems.at[slot, chunk]
-            ),
+            pltpu.make_async_copy(k_hbm.at[row], k_ref.at[slot], sems.at[0, slot]),
+            pltpu.make_async_copy(r_hbm.at[row], r_ref.at[slot], sems.at[1, slot]),
         )
 
-    def each(row, slot, act):
-        for chunk in range(chunks):
-
-            @pl.when(chunk < held(row))
-            def _():
-                for copy in copies(row, slot, chunk):
-                    act(copy)
-
+    entering, leaving = [], []
+    for n, by in enumerate((1, 3)):
+        lanes = quarter_lanes(by, cut_ref.shape[2])
+        entering.append(pltpu.make_async_copy(dw_hbm.at[:, lanes], cut_ref.at[n], cut_sems.at[0, n]))
+        leaving.append(pltpu.make_async_copy(cut_ref.at[n], cuts[n], cut_sems.at[1, n]))
     for row in range(DEPTH):
-        each(row, row, lambda copy: copy.start())
+        for copy in copies(row, row):
+            copy.start()
+    for copy in entering:
+        copy.start()
     vu_copy.start()
 
+    columns = spread_ref.shape[2]
+    for j in range(spread_ref.shape[0]):
+        spread_ref[j] = res_ref[:, j * columns : (j + 1) * columns]
     places, levels = route_tables(upright(groups_ref), upright(picks_ref), upright(levels_ref))
     places_ref[...] = places
     half = heads * width // 2
@@ -166,39 +170,50 @@
     kept_ref[:, half:] = jnp.where(first, places.astype(f32), levels.astype(f32)).astype(bf16)
     given_ref[:, half:] = jnp.where(first, levels.astype(f32), places.astype(f32)).astype(bf16)
 
-    def step(row, carry):
-        slot = lax.rem(row, DEPTH)
-        each(row, slot, lambda copy: copy.wait())
-        for count in range(1, chunks + 1):
-
-            @pl.when(held(row) == count)
-            def _():
-                seen = count * CHUNK
-                keys = k_ref[slot, :seen, :]
-                scores = lax.dot_general(
-                    q_ref[row], keys, (((1,), (1,)), ((), ())), preferred_element_type=f32
-                )
-                scores = scores + jnp.dot(
-                    qr_ref[row], r_ref[slot, :, :seen], preferred_element_type=f32
-                )
-                scores = scores * score_scale
-                place = lax.broadcasted_iota(jnp.int32, scores.shape, 1)
-                scores = jnp.where(place < lengths[row], scores, far_below)
-                highest = jnp.max(scores, axis=1, keepdims=True)
-                raised = jnp.exp(scores - highest)
-                weights = (raised / jnp.sum(raised, axis=1, keepdims=True)).astype(bf16)
-                mix = jnp.dot(weights, keys, preferred_element_type=f32)
-                at = pl.ds(pl.multiple_of(row * heads, heads), heads)
-                for j in range(mix_ref.shape[0]):
-                    mix_ref[j, at, :] = mix[:, j * 128 : (j + 1) * 128]
-
-        @pl.when(row + DEPTH < rows)
-        def _():
-            each(row + DEPTH, slot, lambda copy: copy.start())
-
-        return carry
-
-    lax.fori_loop(0, rows, step, 0)
+    def scores_of(row, slot):
+        scores = lax.dot_general(
+            q_ref[row], k_ref[slot], (((1,), (1,)), ((), ())), preferred_element_type=f32
+        )
+        return scores + jnp.dot(qr_ref[row], r_ref[slot], preferred_element_type=f32)
+
+    def weights_of(scores, row):
+        scores = scores * score_scale
+        place = lax.broadcasted_iota(jnp.int32, scores.shape, 1)
+        scores = jnp.where(place < lengths[row], scores, far_below)
+        highest = jnp.max(scores, axis=1, keepdims=True)
+        raised = jnp.exp(scores - highest)
+        return (raised * (1.0 / jnp.sum(raised, axis=1, keepdims=True))).astype(bf16)
+
+    def finish(scores, row, slot):
+        mix = jnp.dot(weights_of(scores, row), k_ref[slot], preferred_element_type=f32)
+        at = pl.ds(row * heads, heads)
+        for j in range(mix_ref.shape[0]):
+            mix_ref[j, at, :] = mix[:, j * 128 : (j + 1) * 128]
+
+    def wait(row, slot):
+        for copy in copies(row, slot):
+            copy.wait()
+
+    scored, weighed = {}, {}
+    for row in range(rows + 2):
+        if row < rows:
+            wait(row, row % DEPTH)
+            scored[row] = scores_of(row, row % DEPTH)
+        if 0 <= row - 1 < rows:
+            weighed[row - 1] = weights_of(scored.pop(row - 1), row - 1)
+        if row >= 2:
+            done = row - 2
+            mix = jnp.dot(weighed.pop(done), k_ref[done % DEPTH], preferred_element_type=f32)
+            at = pl.ds(done * heads, heads)
+            for j in range(mix_ref.shape[0]):
+                mix_ref[j, at, :] = mix[:, j * 128 : (j + 1) * 128]
+            if done + DEPTH < rows:
+                for copy in copies(done + DEPTH, done % DEPTH):
+                    copy.start()
+        if row == DEPTH:
+            for n, copy in enumerate(entering):
+                copy.wait()
+                leaving[n].start()
     vu_copy.wait()
     for side, ref in ((core, kept_ref), (1 - core, given_ref)):
         for i in range(heads // 2):
@@ -208,32 +223,40 @@
             ref[:, i * width : (i + 1) * width] = jnp.dot(
                 left, vu_ref[h], preferred_element_type=f32
             ).astype(bf16)
-
-
-def attend(query_latent, query_rope, cache_latent, cache_rope, lengths, value_up, routing):
+    for copy in leaving:
+        copy.wait()
+
+
+def attend(
+    query_latent, query_rope, cache_latent, cache_rope, lengths, value_up, down_weight, residual, columns, routing
+):
     rows, heads, lat = query_latent.shape
     rope = query_rope.shape[2]
     positions = cache_latent.shape[1]
     width = value_up.shape[2]
+    units, model = down_weight.shape
     whole = pl.BlockSpec(memory_space=pltpu.VMEM)
     small = pl.BlockSpec(memory_space=pltpu.SMEM)
     far = pl.BlockSpec(memory_space=pltpu.HBM)
     return pl.pallas_call(
         attend_kernel,
-        in_specs=[small, whole, whole, far, far, far, whole, whole, whole],
-        out_specs=(whole,) * 3,
+        in_specs=[small, whole, whole] + [far] * 4 + [whole] * 4,
+        out_specs=(whole,) * 4 + (far,) * 2,
         out_shape=(
             jax.ShapeDtypeStruct((rows, heads * width // 2 + 128), bf16),
             jax.ShapeDtypeStruct((rows, heads * width // 2 + 128), bf16),
             jax.ShapeDtypeStruct((rows, 128), bf16),
-        ),
+            jax.ShapeDtypeStruct((residual.shape[1] // columns, rows, columns), bf16),
+        )
+        + (jax.ShapeDtypeStruct((units, model // PLANES), bf16),) * 2,
         scratch_shapes=[
             pltpu.VMEM((DEPTH, positions, lat), bf16),
             pltpu.VMEM((DEPTH, rope, positions), bf16),
             pltpu.VMEM((lat // 128, rows * heads, 128), f32),
             pltpu.VMEM((heads, lat, width), bf16),
-            pltpu.SemaphoreType.DMA((DEPTH, positions // CHUNK)),
-            pltpu.SemaphoreType.DMA((DEPTH, positions // CHUNK)),
+            pltpu.VMEM((2, units, model // PLANES), bf16),
+            pltpu.SemaphoreType.DMA((2, DEPTH)),
+            pltpu.SemaphoreType.DMA((2, 2)),
             pltpu.SemaphoreType.DMA,
         ],
         compiler_params=pltpu.CompilerParams(vmem_limit_bytes=VMEM),
@@ -245,77 +268,78 @@
         name="attend",
     )(
         lengths, query_latent, query_rope, distant(cache_latent), distant(cache_rope), distant(value_up),
-        *routing,
-    )
-
-
-def project_kernel(*refs):
-    count = 2 * SIDE
-    blocks_hbm, w_hbm = refs[:count], refs[count]
-    low_ref, high_ref, places_ref, levels_ref = refs[count + 1 : count + 5]
-    b_ref, w_ref, b_sems, w_sems = refs[count + 5 :]
+        distant(down_weight), residual, *routing,
+    )
+
+
+def half_product(blocks, w_hbm, w_ref, sem, side):
+    half = w_ref.shape[1]
+    copy = pltpu.make_async_copy(
+        w_hbm.at[:, pl.ds(pl.multiple_of(side * half, half), half)], w_ref, sem
+    )
+    copy.start()
+    left = jnp.concatenate([block[:, :half] for block in blocks])
+    copy.wait()
+    terms = lax.dot_general(left, w_ref[...], (((1,), (1,)), ((), ())), preferred_element_type=f32)
+    span = terms.shape[0] // SIDE
+    return [terms[i * span : (i + 1) * span] for i in range(SIDE)]
+
+
+def first_half_kernel(*refs):
+    blocks, w_hbm, out_ref, table_ref, w_ref, sem = refs[:SIDE], *refs[SIDE:]
+    for i, terms in enumerate(half_product(blocks, w_hbm, w_ref, sem, this_core())):
+        out_ref[i] = terms
+        table_ref[i] = blocks[i][:, w_ref.shape[1] :]
+
+
+def second_half_kernel(*refs):
+    blocks, w_hbm, made_ref, own_ref = refs[:SIDE], *refs[SIDE : SIDE + 3]
+    low_ref, high_ref, places_ref, levels_ref, w_ref, sem = refs[SIDE + 3 :]
     core = this_core()
-    half = w_ref.shape[2]
-    lanes = [pl.ds(pl.multiple_of(side * half, half), half) for side in (core, 1 - core)]
-    w_copies = [
-        pltpu.make_async_copy(w_hbm.at[:, lanes[n]], w_ref.at[n], w_sems.at[n]) for n in range(2)
-    ]
-    copies = [
-        pltpu.make_async_copy(blocks_hbm[n], b_ref.at[n], b_sems.at[n]) for n in range(count)
-    ]
-    w_copies[0].start()
-    for copy in copies[:SIDE]:
-        copy.start()
-    w_copies[1].start()
-    for copy in copies[SIDE:]:
-        copy.start()
-    made = []
-    for n in range(count):
-        if n % SIDE == 0:
-            w_copies[n // SIDE].wait()
-        copies[n].wait()
-        made.append(
-            lax.dot_general(
-                b_ref[n, :, :half], w_ref[n // SIDE], (((1,), (1,)), ((), ())),
-                preferred_element_type=f32,
-            )
-        )
+    half = w_ref.shape[1]
+    made = half_product(blocks, w_hbm, w_ref, sem, 1 - core)
     rows = made[0].shape[0] // SIDE
     first = core == 0
     for i in range(SIDE):
         for j in range(SIDE):
             at, across = slice(j * rows, (j + 1) * rows), slice(i * rows, (i + 1) * rows)
-            total = (made[i][at] + made[SIDE + j][across]).astype(bf16)
+            total = (made_ref[i, at] + made[j][across]).astype(bf16)
             (low_ref if i < 2 else high_ref)[i % 2 * SIDE + j] = total
-            mine = b_ref[i, at, half:].astype(f32)
-            theirs = b_ref[SIDE + j, across, half:].astype(f32)
+            mine = own_ref[i, at].astype(f32)
+            theirs = blocks[j][across, half:].astype(f32)
             places_ref[i * SIDE + j] = jnp.where(first, mine, theirs).astype(bf16)
             levels_ref[i * SIDE + j] = jnp.where(first, theirs, mine).astype(bf16)
 
 
-def project(blocks, swapped, out_proj):
-    wide = blocks[0].shape[1]
-    rows = blocks[0].shape[0] // SIDE
+def project(blocks, out_proj, before=None):
     columns = out_proj.shape[1]
+    tall = blocks[0].shape[0]
+    rows = tall // SIDE
     whole = pl.BlockSpec(memory_space=pltpu.VMEM)
     far = pl.BlockSpec(memory_space=pltpu.HBM)
-    sums = jax.ShapeDtypeStruct((CHIPS // 2, rows, columns), bf16)
-    table = jax.ShapeDtypeStruct((CHIPS, rows, 128), bf16)
+    if before is None:
+        out_shape = (
+            jax.ShapeDtypeStruct((SIDE, tall, columns), f32),
+            jax.ShapeDtypeStruct((SIDE, tall, 128), bf16),
+        )
+    else:
+        sums = jax.ShapeDtypeStruct((CHIPS // 2, rows, columns), bf16)
+        table = pltpu.HBM((CHIPS, rows, 128), bf16)
+        out_shape = (sums, sums, table, table)
+    before = before or ()
     return pl.pallas_call(
-        project_kernel,
-        in_specs=[far] * (2 * SIDE + 1),
-        out_specs=(whole,) * 4,
-        out_shape=(sums, sums, table, table),
+        second_half_kernel if before else first_half_kernel,
+        in_specs=[whole] * SIDE + [far] + [whole] * len(before),
+        out_specs=(whole,) * len(out_shape),
+        out_shape=out_shape,
         scratch_shapes=[
-            pltpu.VMEM((2 * SIDE, SIDE * rows, wide), bf16),
-            pltpu.VMEM((2, columns, out_proj.shape[0] // 2), bf16),
-            pltpu.SemaphoreType.DMA((2 * SIDE,)),
-            pltpu.SemaphoreType.DMA((2,)),
+            pltpu.VMEM((columns, out_proj.shape[0] // 2), bf16),
+            pltpu.SemaphoreType.DMA,
         ],
         compiler_params=pltpu.CompilerParams(vmem_limit_bytes=VMEM),
-        cost_estimate=pl.CostEstimate(flops=10**9, bytes_accessed=7 * 10**6, transcendentals=0),
+        cost_estimate=pl.CostEstimate(flops=5 * 10**8, bytes_accessed=4 * 10**6, transcendentals=0),
         name="project",
-    )(*blocks, *swapped, distant(out_proj.T))
+    )(*blocks, distant(out_proj.T), *before)
 
 
 def slot_masks(mark, rows):
@@ -368,7 +392,7 @@
         compiler_params=pltpu.CompilerParams(vmem_limit_bytes=VMEM),
         cost_estimate=pl.CostEstimate(flops=10**8, bytes_accessed=10**6, transcendentals=0),
         name="gate_table",
-    )(table, places, levels)
+    )(table, distant(places), distant(levels))
 
 
 def select_kernel(table, low_ref, high_ref, res_ref, places_ref, out_ref):
@@ -421,7 +445,7 @@
         compiler_params=pltpu.CompilerParams(vmem_limit_bytes=VMEM),
         cost_estimate=pl.CostEstimate(flops=10**9, bytes_accessed=6 * 10**6, transcendentals=0),
         name="select",
-    )(table, *parts, residual, places)
+    )(table, *parts, distant(residual), distant(places))
 
 
 def unpacked(block, columns):
@@ -491,39 +515,19 @@
     )(*operands, distant(gate_weight), distant(up_weight))
 
 
-def cut_kernel(w_hbm, *refs):
-    outs, held, sems = refs[:3], refs[3], refs[4]
-    z = lax.axis_index("tensor")
-    width = outs[0].shape[1]
-    copies = []
-    for n, by in enumerate((1, 3, 2)):
-        lanes = pl.ds(pl.multiple_of((z + by) % PLANES * width, width), width)
-        copies.append(pltpu.make_async_copy(w_hbm.at[:, lanes], held.at[n], sems.at[0, n]))
-    for copy in copies:
-        copy.start()
-    leaving = []
-    for n, copy in enumerate(copies):
-        copy.wait()
-        leaving.append(pltpu.make_async_copy(held.at[n], outs[n], sems.at[1, n]))
-        leaving[n].start()
-    for copy in leaving:
-        copy.wait()
+def cut_kernel(w_hbm, out_ref):
+    pltpu.sync_copy(w_hbm.at[:, quarter_lanes(2, out_ref.shape[1])], out_ref)
 
 
 def cut(down_weight):
     units, width = down_weight.shape
-    far = pl.BlockSpec(memory_space=pltpu.HBM)
     return pl.pallas_call(
         cut_kernel,
-        in_specs=[far],
-        out_specs=(far,) * 3,
-        out_shape=(jax.ShapeDtypeStruct((units, width // PLANES), bf16),) * 3,
-        scratch_shapes=[
-            pltpu.VMEM((3, units, width // PLANES), bf16),
-            pltpu.SemaphoreType.DMA((2, 3)),
-        ],
+        in_specs=[pl.BlockSpec(memory_space=pltpu.HBM)],
+        out_specs=pl.BlockSpec(memory_space=pltpu.VMEM),
+        out_shape=jax.ShapeDtypeStruct((units, width // PLANES), bf16),
         compiler_params=pltpu.CompilerParams(vmem_limit_bytes=VMEM),
-        cost_estimate=pl.CostEstimate(flops=0, bytes_accessed=6 * 10**6, transcendentals=0),
+        cost_estimate=pl.CostEstimate(flops=0, bytes_accessed=2 * 10**6, transcendentals=0),
         name="cut",
     )(distant(down_weight))
 
@@ -661,11 +665,10 @@
     here_x, here_y = chip // SIDE, chip % SIDE
 
     quarter = model // PLANES
-    sent = cut(down_proj[0])
-    downs = [move_z(part, by) for part, by in zip(sent, (1, 3, 2))]
-
-    kept, given, places_here = attend(
-        query_latent, query_rope, cache_latent, cache_rope, lengths, value_up,
+    opposite = move_z(cut(down_proj[0]), 2)
+
+    kept, given, places_here, spread, *sent = attend(
+        query_latent, query_rope, cache_latent, cache_rope, lengths, value_up, down_proj[0], residual, columns,
         (groups.T, expert_picks.T, gate_levels.T),
     )
     weighting = places_here == (jnp.arange(128) % CAP + 1).astype(bf16)
@@ -677,17 +680,17 @@
     )
     blocks = jnp.concatenate(around(flat, 0), axis=0)
 
-    spread = residual.reshape(rows, CHIPS * CORES, columns).transpose(1, 0, 2)
-    spread, blocks, downs[:2] = lax.optimization_barrier((spread, blocks, downs[:2]))
+    spread, blocks, opposite = lax.optimization_barrier((spread, blocks, opposite))
     residual_columns = lax.all_to_all(spread, "dp", split_axis=0, concat_axis=0, tiled=True)
+    downs = [move_z(part, by) for part, by in zip(sent, (1, 3))] + [opposite]
     residual_columns = residual_columns.reshape(CHIPS, CORES, rows, columns)
 
     blocks = around(blocks, 1)
-    blocks[3], downs[2], residual_columns = lax.optimization_barrier(
-        (blocks[3], downs[2], residual_columns)
+    blocks[3], downs[:2], residual_columns = lax.optimization_barrier(
+        (blocks[3], downs[:2], residual_columns)
     )
     swapped = [move_core(block) for block in blocks]
-    low, high, places_all, levels_all = project(blocks, swapped, out_proj)
+    low, high, places_all, levels_all = project(swapped, out_proj, project(blocks, out_proj))
     low, high = sum_z(low, high)
 
     far = jnp.arange(SIDE, dtype=jnp.int32)
@@ -718,12 +721,7 @@
 
     returned = chip_exchange(returning).reshape(CHIPS * CAP, quarter)
     mixed = jnp.dot(weighting, returned, preferred_element_type=f32).astype(bf16)
-    turned = jnp.stack([mixed] + [move_z(mixed, by) for by in (1, 3, 2)])
-    back = (z - jnp.arange(PLANES)) % PLANES
-    spot = back ^ (back >> 1)
-    return jnp.concatenate(
-        [lax.dynamic_index_in_dim(turned, spot[k], 0, keepdims=False) for k in range(PLANES)], axis=1
-    )
+    return spread_z(mixed).transpose(1, 0, 2).reshape(rows, model)
 
 
 def solution(mesh):

time: 166 us -> 151 us (0.910)
  blocking collectives: 42.5 us -> 51.7 us
  between operations: 7.9 us -> 0.31 us
  starting transfers between devices: 34.6 us -> 27.1 us
  Pallas kernels: 38.9 us -> 35.4 us
  local copies, waits for them, and re-layouts: 5.88 us -> 2.51 us
  other arithmetic: 3.03 us -> 0.33 us
    all_to_all x0 -> x1, blocking collectives: none -> 8.88 us  [spread_z(): lax.all_to_all(copies, 'tensor', split_axis=0, concat_axis=0, tiled=True)]
    pallas_call x3 -> x4, Pallas kernels: 26.6 us -> 22.1 us  [the longest x1 14.9 us: attend(): pl.pallas_call(attend_kernel, in_specs=[small, whole, whole] + [far] * 4...]
    ppermute x4, waiting for transfers between devices: 5.22 us -> 9.2 us  [add(): moved = lax.ppermute(block, 'tensor', pairs)]
    ppermute x9 -> x6, starting transfers between devices: 12.8 us -> 9.96 us  [move_z(): lax.ppermute(value, 'tensor', [(z, (z + by) % PLANES) for z in range(PLAN...]
    ppermute x7, waiting for transfers between devices: 6.66 us -> 4 us  [move_core(): return lax.ppermute(value, 'dp', place_pairs(lambda x, y, c: (x, y, 1 - c)))]
    ppermute x4, starting transfers between devices: 4.64 us -> 2.01 us  [add(): moved = lax.ppermute(block, 'tensor', pairs)]
    unnamed x32 -> x22, local copies, waits for them, and re-layouts: 3.84 us -> 1.66 us
    ppermute x7, starting transfers between devices: 2.54 us -> 0.8 us  [move_core(): return lax.ppermute(value, 'dp', place_pairs(lambda x, y, c: (x, y, 1 - c)))]
  transfers between devices with their start and end apart: 27 -> 24, of which waited for: 16 -> 14; matrix products, arithmetic and copies ran while one was open for 3% -> 0% of each run, Pallas kernels for 12% -> 15%
where the time goes in v3:
time: 151 us
  blocking collectives  51.7 us (34%)
  Pallas kernels  35.4 us (23%)
  waiting for transfers between devices  33.4 us (22%)
  starting transfers between devices  27.1 us (18%)
  local copies, waits for them, and re-layouts  2.51 us (2%)
    all_to_all x2, blocking collectives, chip_exchange(): lax.all_to_all(value, 'dp', split_axis=0, concat_axis=0, axis_index_group...  42.8 us
    pallas_call x1, Pallas kernels, attend(): pl.pallas_call(attend_kernel, in_specs=[small, whole, whole] + [far] * 4...  14.9 us
    ppermute x6, waiting for transfers between devices, move_z(): lax.ppermute(value, 'tensor', [(z, (z + by) % PLANES) for z in range(PLAN...  14.4 us
    ppermute x6, starting transfers between devices, move_ring(): return lax.ppermute(value, 'dp', place_pairs(place))  10.3 us
    ppermute x6, starting transfers between devices, move_z(): lax.ppermute(value, 'tensor', [(z, (z + by) % PLANES) for z in range(PLAN...  9.96 us
    ppermute x4, waiting for transfers between devices, add(): moved = lax.ppermute(block, 'tensor', pairs)  9.2 us
    all_to_all x1, blocking collectives, spread_z(): lax.all_to_all(copies, 'tensor', split_axis=0, concat_axis=0, tiled=True)  8.88 us
    pallas_call x2, Pallas kernels, up(): pl.pallas_call(up_kernel if before is None else act_kernel, in_specs=[who...  6.28 us
  transfers between devices with their start and end apart: 24, of which 14 were waited for; matrix products, arithmetic and copies ran while one was open for 0% of the time, Pallas kernels for 15%

profile of v3, /device:TPU:0, one launch (start us, length us, event | category | flops | bytes accessed | tf_op | source)
XLA Modules:
  0.0 150.9 jit_solution(11929947211970184669)
XLA Ops:
  0.0 1.3 cut.1
  1.3 4.0 %collective-permute-start.4 = (bf16[256,1792]{1,0:T(8,128)(2,1)S(1)}, bf16[256,1792]{1,0:T(8,128)(2,1)S(1)}, u32[]{:S(2)}, u32[]{:S(2)}) collective-permute-start(bf16[256,1792]{1,0:T(8,128)(2,1)S(1)} %cut.1), channel_id=1, source_target_pairs={{0,2},{1,3},{2,0},{3,1},{4,6},{5,7},{6,4},{7,5},{8,10},{9,11},{10,... | collective-permute-start | bytes 2752520 | tf_op jit(solution)/shard_map/ppermute | solution.py:57
  5.3 14.9 %attend.1 = (bf16[16,2176]{1,0:T(8,128)(2,1)S(1)}, bf16[16,2176]{1,0:T(8,128)(2,1)S(1)}, bf16[16,128]{1,0:T(8,128)(2,1)S(1)}, bf16[32,16,224]{2,1,0:T(8,128)(2,1...) custom-call(s32[16]{0:T(128)S(1)} %copy-done.8, bf16[16,32,512]{2,1,0:T(8,128)(2,1)S(1)} %copy-done.2, ...), custom_call_target="tpu_custom_call" | custom-call | flops 1073741824 | bytes 18874368 | tf_op jit(solution)/shard_map/attend/pallas_call | solution.py:241
  20.4 1.2 collective-permute-done
  21.6 3.1 %collective-permute-start.3 = (bf16[32,2176]{1,0:T(8,128)(2,1)S(1)}, bf16[32,2176]{1,0:T(8,128)(2,1)S(1)}, u32[]{:S(2)}, u32[]{:S(2)}) collective-permute-start(bf16[32,2176]{1,0:T(8,128)(2,1)S(1)} %maximum_select_fusion), channel_id=1, source_target_pairs={{0,64},{4,20},{8,72},{12,28},{16,80},{20,4},{24,88},{28,12},{32,96... | collective-permute-start | bytes 417800 | tf_op jit(solution)/shard_map/ppermute | solution.py:53
  24.7 1.1 collective-permute-start.2
  28.3 1.7 %collective-permute-start.12 = (bf16[256,1792]{1,0:T(8,128)(2,1)S(1)}, bf16[256,1792]{1,0:T(8,128)(2,1)}, u32[]{:S(2)}, u32[]{:S(2)}) collective-permute-start(bf16[256,1792]{1,0:T(8,128)(2,1)S(1)} %get-tuple-element.33), channel_id=1, source_target_pairs={{0,3},{1,0},{2,1},{3,2},{4,7},{5,4},{6,5},{7,6},{8,11},{9,8},{10,9... | collective-permute-start | bytes 2752520 | tf_op jit(solution)/shard_map/ppermute | solution.py:57
  30.0 2.1 %collective-permute-done.1 = bf16[32,2176]{1,0:T(8,128)(2,1)S(1)} collective-permute-done((bf16[32,2176]{1,0:T(8,128)(2,1)S(1)}, bf16[32,2176]{1,0:T(8,128)(2,1)S(1)}, u32[]{:S(2)}, u32[]{:S(2)}) %collective-permute-start.1) | collective-permute-done | bytes 139296 | tf_op jit(solution)/shard_map/ppermute | solution.py:53
  33.1 3.2 %collective-permute-start.10 = (bf16[128,2176]{1,0:T(8,128)(2,1)S(1)}, bf16[128,2176]{1,0:T(8,128)(2,1)S(1)}, u32[]{:S(2)}, u32[]{:S(2)}) collective-permute-start(bf16[128,2176]{1,0:T(8,128)(2,1)S(1)} %pad_maximum_fusion.refs_0_), channel_id=1, source_target_pairs={{0,16},{4,68},{8,24},{12,76},{16,0},{20,84},{24,8},{28,92},{32,48}... | collective-permute-start | bytes 1671176 | tf_op jit(solution)/shard_map/ppermute | solution.py:53
  36.3 1.1 collective-permute-start.8
  38.4 4.0 %all-to-all-start = ((bf16[32,16,224]{2,1,0:T(8,128)(2,1)}), bf16[32,16,224]{2,1,0:T(8,128)(2,1)S(1)}, u32[]{:S(2)}, u32[]{:S(2)}) async-start(bf16[32,16,224]{2,1,0:T(8,128)(2,1)} %get-tuple-element.34), calls=%async_computation | async-start | bytes 524288 | tf_op jit(solution)/shard_map/all_to_all | solution.py:684
  42.4 7.7 %collective-permute-done.11.w1 = bf16[256,1792]{1,0:T(8,128)(2,1)} collective-permute-done((bf16[256,1792]{1,0:T(8,128)(2,1)}, bf16[256,1792]{1,0:T(8,128)(2,1)}, u32[]{:S(2)}, u32[]{:S(2)}) %collective-permute-start.11) | collective-permute-done | bytes 917536 | tf_op jit(solution)/shard_map/ppermute | solution.py:57
  50.0 3.1 %all-to-all-done = bf16[32,16,224]{2,1,0:T(8,128)(2,1)S(1)} async-done(((bf16[32,16,224]{2,1,0:T(8,128)(2,1)}), bf16[32,16,224]{2,1,0:T(8,128)(2,1)S(1)}, u32[]{:S(2)}, u32[]{:S(2)}) %all-to-all-start) | async-done | bytes 229408 | tf_op jit(solution)/shard_map/all_to_all | solution.py:684
  54.5 3.3 %project.2 = (f32[4,128,224]{2,1,0:T(8,128)S(1)}, bf16[4,128,128]{2,1,0:T(8,128)(2,1)S(1)}) custom-call(bf16[128,2176]{1,0:T(8,128)(2,1)S(1)} %pad_maximum_fusion.refs_0_, bf16[128,2176]{1,0:T(8,128)(2,1)} %collective-permute-done.6.refs_1_, bf16[128,2176]{1,0:T(8,128)(2,1)} %collective-permute-done.8.refs_2_, ...), custom_call_target="tpu_custom_call" | custom-call | flops 500000000 | bytes 4000000 | tf_op jit(solution)/shard_map/project/pallas_call | solution.py:330
  57.9 2.6 %project.3 = (bf16[8,32,224]{2,1,0:T(8,128)(2,1)S(1)}, bf16[8,32,224]{2,1,0:T(8,128)(2,1)S(1)}, bf16[16,32,128]{2,1,0:T(8,128)(2,1)}, bf16[16,32,128]{2,1,0:T(8,128)(2,1)}) custom-call(bf16[128,2176]{1,0:T(8,128)(2,1)S(1)} %collective-permute-done.5.refs_0_, bf16[128,2176]{1,0:T(8,128)(2,1)S(1)} %collective-permute-done.7.refs_1_, ...), custom_call_target="tpu_custom_call" | custom-call | flops 500000000 | bytes 4000000 | tf_op jit(solution)/shard_map/project/pallas_call | solution.py:330
  60.5 1.1 collective-permute-start.14
  61.8 1.6 %gate_table.1.gates_ref = f32[256,128]{1,0:T(8,128)S(1)} custom-call(s32[16]{0:T(128)S(1)} %select_n.84.table, bf16[16,32,128]{2,1,0:T(8,128)(2,1)} %get-tuple-element.41.places_ref, bf16[16,32,128]{2,1,0:T(8,128)(2,1)} %get-tuple-element.42.levels_ref), custom_call_target="tpu_custom_call" | custom-call | flops 100000000 | bytes 1000000 | tf_op jit(solution)/shard_map/gate_table/pallas_call | solution.py:386
  63.4 3.0 %collective-permute-done.14 = bf16[8,32,224]{2,1,0:T(8,128)(2,1)S(1)} collective-permute-done((bf16[8,32,224]{2,1,0:T(8,128)(2,1)S(1)}, bf16[8,32,224]{2,1,0:T(8,128)(2,1)S(1)}, u32[]{:S(2)}, u32[]{:S(2)}) %collective-permute-start.14) | collective-permute-done | bytes 114720 | tf_op jit(solution)/shard_map/ppermute | solution.py:68
  67.2 1.3 collective-permute-done.16
  68.6 4.1 %collective-permute-done.15 = bf16[8,32,224]{2,1,0:T(8,128)(2,1)S(1)} collective-permute-done((bf16[8,32,224]{2,1,0:T(8,128)(2,1)S(1)}, bf16[8,32,224]{2,1,0:T(8,128)(2,1)S(1)}, u32[]{:S(2)}, u32[]{:S(2)}) %collective-permute-start.15) | collective-permute-done | bytes 114720 | tf_op jit(solution)/shard_map/ppermute | solution.py:68
  73.6 1.5 %select.39 = bf16[16,64,896]{2,1,0:T(8,128)(2,1)S(1)} custom-call(s32[16]{0:T(128)S(1)} %select_n.84.table, bf16[8,32,224]{2,1,0:T(8,128)(2,1)S(1)} %add_convert_fusion.2.low_ref, bf16[8,32,224]{2,1,0:T(8,128)(2,1)S(1)} %add_convert_fusion.high_ref, bf16[16,2,16,224]{3,2,1,0:T(8,128)(2,1)} %bitcast.36, bf16[16,32,128]{2,1,0:T(8,128)(2,1)} %get-tuple-element.41.places_ref), custom_call_target="tpu_custom_call" | custom-call | flops 1000000000 | bytes 6000000 | tf_op jit(solution)/shard_map/select/pallas_call | solution.py:438
  75.2 28.2 %all_to_all.20.x_ref.own_hbm = bf16[16,64,896]{2,1,0:T(8,128)(2,1)S(1)} all-to-all(bf16[16,64,896]{2,1,0:T(8,128)(2,1)S(1)} %select.39), channel_id=1, replica_groups={{0,8,16,24,32,40,48,56,64,72,80,88,96,104,112,120},{4,12,20,28,36,44,52..., dimensions={0} | all-to-all | bytes 3670016 | tf_op jit(solution)/shard_map/all_to_all | solution.py:78
  103.3 2.8 %up.2.acc_ref = f32[256,512]{1,0:T(8,128)S(1)} custom-call(bf16[16,64,896]{2,1,0:T(8,128)(2,1)S(1)} %all_to_all.20.x_ref.own_hbm, bf16[16,2,224,256]{3,2,1,0:T(8,128)(2,1)} %bitcast.28, bf16[16,2,224,256]{3,2,1,0:T(8,128)(2,1)} %bitcast.30), custom_call_target="tpu_custom_call" | custom-call | flops 939524096 | bytes 6000000 | tf_op jit(solution)/shard_map/up/pallas_call | solution.py:497
  107.1 3.5 %up.3.a0 = bf16[256,256]{1,0:T(8,128)(2,1)S(1)} custom-call(f32[256,512]{1,0:T(8,128)S(1)} %up.2.acc_ref, bf16[16,64,896]{2,1,0:T(8,128)(2,1)S(1)} %collective-permute-done.18.x_ref.other_hbm, bf16[16,2,224,256]{3,2,1,0:T(8,128)(2,1)} %bitcast.29, bf16[16,2,224,256]{3,2,1,0:T(8,128)(2,1)} %bitcast.31), custom_call_target="tpu_custom_call" | custom-call | flops 939524096 | bytes 6000000 | tf_op jit(solution)/shard_map/up/pallas_call | solution.py:497
  110.6 1.2 collective-permute-start.21
  111.8 1.8 %collective-permute-start.20 = (bf16[256,256]{1,0:T(8,128)(2,1)S(1)}, bf16[256,256]{1,0:T(8,128)(2,1)S(1)}, u32[]{:S(2)}, u32[]{:S(2)}) collective-permute-start(bf16[256,256]{1,0:T(8,128)(2,1)S(1)} %up.3.a0), channel_id=1, source_target_pairs={{0,3},{1,0},{2,1},{3,2},{4,7},{5,4},{6,5},{7,6},{8,11},{9,8},{10,9... | collective-permute-start | bytes 393224 | tf_op jit(solution)/shard_map/ppermute | solution.py:57
  113.9 4.7 %collective-permute-done.21.a3 = bf16[256,256]{1,0:T(8,128)(2,1)S(1)} collective-permute-done((bf16[256,256]{1,0:T(8,128)(2,1)S(1)}, bf16[256,256]{1,0:T(8,128)(2,1)S(1)}, u32[]{:S(2)}, u32[]{:S(2)}) %collective-permute-start.21) | collective-permute-done | bytes 131104 | tf_op jit(solution)/shard_map/ppermute | solution.py:57
  119.2 1.4 collective-permute-done.19.a1
  120.6 3.3 %down.1.y_ref = bf16[256,1792]{1,0:T(8,128)(2,1)S(1)} custom-call(bf16[256,256]{1,0:T(8,128)(2,1)S(1)} %up.3.a0, bf16[256,256]{1,0:T(8,128)(2,1)S(1)} %collective-permute-done.19.a1, bf16[256,256]{1,0:T(8,128)(2,1)S(1)} %collective-permute-done.20.a2, bf16[256,256]{1,0:T(8,128)(2,1)S(1)} %collective-permute-done.21.a3, bf16[256,7168]{1,0:T(8,128)(2,1)} %bitcast.27, ...), custom_call_target="tpu_custom_call" | custom-call | flops 939524096 | bytes 6000000 | tf_op jit(solution)/shard_map/down/pallas_call | solution.py:562
  124.1 1.8 %collective-permute-done.22.received_ref = bf16[128,1792]{1,0:T(8,128)(2,1)S(1)} collective-permute-done((bf16[128,1792]{1,0:T(8,128)(2,1)S(1)}, bf16[128,1792]{1,0:T(8,128)(2,1)S(1)}, u32[]{:S(2)}, u32[]{:S(2)}) %collective-permute-start.22) | collective-permute-done | bytes 458784 | tf_op jit(solution)/shard_map/ppermute | solution.py:46
  126.4 14.7 %all_to_all.21 = bf16[16,8,1792]{2,1,0:T(8,128)(2,1)S(1)} all-to-all(bf16[16,8,1792]{2,1,0:T(8,128)(2,1)S(1)} %bitcast.21), channel_id=1, replica_groups={{0,8,16,24,32,40,48,56,64,72,80,88,96,104,112,120},{4,12,20,28,36,44,52..., dimensions={0} | all-to-all | bytes 917504 | tf_op jit(solution)/shard_map/all_to_all | solution.py:78
  141.3 8.9 %all_to_all.22 = bf16[4,16,1792]{2,1,0:T(8,128)(2,1)S(1)} all-to-all(bf16[4,16,1792]{2,1,0:T(8,128)(2,1)S(1)} %broadcast_in_dim.2), channel_id=1, replica_groups=mesh['dp'=32,'tensor'=4] {'tensor'}, dimensions={0} | all-to-all | bytes 458752 | tf_op jit(solution)/shard_map/all_to_all | solution.py:62
  (67 shorter events, 11.3 us)
Async XLA Ops:
  0.0 5.3 %copy-start.2 = (bf16[16,32,512]{2,1,0:T(8,128)(2,1)S(1)}, bf16[16,32,512]{2,1,0:T(8,128)(2,1)}, u32[]{:S(2)}) copy-start(bf16[16,32,512]{2,1,0:T(8,128)(2,1)} %q_ref.1) | copy-start | bytes 1572868
  0.0 5.3 %copy-start.3 = (bf16[16,7168]{1,0:T(8,128)(2,1)S(1)}, bf16[16,7168]{1,0:T(8,128)(2,1)}, u32[]{:S(2)}) copy-start(bf16[16,7168]{1,0:T(8,128)(2,1)} %res_ref.1) | copy-start | bytes 688132
  0.0 5.3 %copy-start.4 = (bf16[16,32,64]{2,1,0:T(8,128)(2,1)S(1)}, bf16[16,32,64]{2,1,0:T(8,128)(2,1)}, u32[]{:S(2)}) copy-start(bf16[16,32,64]{2,1,0:T(8,128)(2,1)} %qr_ref.1) | copy-start | bytes 196612
  0.0 5.3 %copy-start.5 = (s32[16,8]{0,1:T(8,128)S(1)}, s32[16,8]{0,1:T(8,128)}, u32[]{:S(2)}) copy-start(s32[16,8]{0,1:T(8,128)} %param.26) | copy-start | bytes 1540
  0.0 5.3 %copy-start.6 = (s32[16,8]{0,1:T(8,128)S(1)}, s32[16,8]{0,1:T(8,128)}, u32[]{:S(2)}) copy-start(s32[16,8]{0,1:T(8,128)} %param.27) | copy-start | bytes 1540
  0.0 5.3 %copy-start.7 = (s32[16,4]{0,1:T(4,128)S(1)}, s32[16,4]{0,1:T(4,128)}, u32[]{:S(2)}) copy-start(s32[16,4]{0,1:T(4,128)} %param.25) | copy-start | bytes 772
  0.0 5.3 %copy-start.8 = (s32[16]{0:T(128)S(1)}, s32[16]{0:T(128)}, u32[]{:S(2)}) copy-start(s32[16]{0:T(128)} %lengths.1) | copy-start | bytes 196
  1.3 30.9 %collective-permute-start.4 = (bf16[256,1792]{1,0:T(8,128)(2,1)S(1)}, bf16[256,1792]{1,0:T(8,128)(2,1)S(1)}, u32[]{:S(2)}, u32[]{:S(2)}) collective-permute-start(bf16[256,1792]{1,0:T(8,128)(2,1)S(1)} %cut.1), channel_id=1, source_target_pairs={{0,2},{1,3},{2,0},{3,1},{4,6},{5,7},{6,4},{7,5},{8,10},{9,11},{10,... | collective-permute-start | bytes 2752520 | tf_op jit(solution)/shard_map/ppermute | solution.py:57
  20.3 1.3 collective-permute-start
  21.6 6.6 %collective-permute-start.3 = (bf16[32,2176]{1,0:T(8,128)(2,1)S(1)}, bf16[32,2176]{1,0:T(8,128)(2,1)S(1)}, u32[]{:S(2)}, u32[]{:S(2)}) collective-permute-start(bf16[32,2176]{1,0:T(8,128)(2,1)S(1)} %maximum_select_fusion), channel_id=1, source_target_pairs={{0,64},{4,20},{8,72},{12,28},{16,80},{20,4},{24,88},{28,12},{32,96... | collective-permute-start | bytes 417800 | tf_op jit(solution)/shard_map/ppermute | solution.py:53
  24.7 5.3 %collective-permute-start.2 = (bf16[32,2176]{1,0:T(8,128)(2,1)S(1)}, bf16[32,2176]{1,0:T(8,128)(2,1)S(1)}, u32[]{:S(2)}, u32[]{:S(2)}) collective-permute-start(bf16[32,2176]{1,0:T(8,128)(2,1)S(1)} %maximum_select_fusion), channel_id=1, source_target_pairs={{0,96},{4,28},{8,104},{12,4},{16,112},{20,12},{24,120},{28,20},{32... | collective-permute-start | bytes 417800 | tf_op jit(solution)/shard_map/ppermute | solution.py:53
  25.9 6.3 %collective-permute-start.1 = (bf16[32,2176]{1,0:T(8,128)(2,1)S(1)}, bf16[32,2176]{1,0:T(8,128)(2,1)S(1)}, u32[]{:S(2)}, u32[]{:S(2)}) collective-permute-start(bf16[32,2176]{1,0:T(8,128)(2,1)S(1)} %maximum_select_fusion), channel_id=1, source_target_pairs={{0,32},{4,12},{8,40},{12,20},{16,48},{20,28},{24,56},{28,4},{32,64... | collective-permute-start | bytes 417800 | tf_op jit(solution)/shard_map/ppermute | solution.py:53
  26.8 23.3 %collective-permute-start.11 = (bf16[256,1792]{1,0:T(8,128)(2,1)}, bf16[256,1792]{1,0:T(8,128)(2,1)}, u32[]{:S(2)}, u32[]{:S(2)}) collective-permute-start(bf16[256,1792]{1,0:T(8,128)(2,1)} %get-tuple-element.32), channel_id=1, source_target_pairs={{0,1},{1,2},{2,3},{3,0},{4,5},{5,6},{6,7},{7,4},{8,9},{9,10},{10,1... | collective-permute-start | bytes 2752520 | tf_op jit(solution)/shard_map/ppermute | solution.py:57
  28.3 21.8 %collective-permute-start.12 = (bf16[256,1792]{1,0:T(8,128)(2,1)S(1)}, bf16[256,1792]{1,0:T(8,128)(2,1)}, u32[]{:S(2)}, u32[]{:S(2)}) collective-permute-start(bf16[256,1792]{1,0:T(8,128)(2,1)S(1)} %get-tuple-element.33), channel_id=1, source_target_pairs={{0,3},{1,0},{2,1},{3,2},{4,7},{5,4},{6,5},{7,6},{8,11},{9,8},{10,9... | collective-permute-start | bytes 2752520 | tf_op jit(solution)/shard_map/ppermute | solution.py:57
  33.1 20.0 %collective-permute-start.10 = (bf16[128,2176]{1,0:T(8,128)(2,1)S(1)}, bf16[128,2176]{1,0:T(8,128)(2,1)S(1)}, u32[]{:S(2)}, u32[]{:S(2)}) collective-permute-start(bf16[128,2176]{1,0:T(8,128)(2,1)S(1)} %pad_maximum_fusion.refs_0_), channel_id=1, source_target_pairs={{0,16},{4,68},{8,24},{12,76},{16,0},{20,84},{24,8},{28,92},{32,48}... | collective-permute-start | bytes 1671176 | tf_op jit(solution)/shard_map/ppermute | solution.py:53
  36.3 17.5 %collective-permute-start.8 = (bf16[128,2176]{1,0:T(8,128)(2,1)S(1)}, bf16[128,2176]{1,0:T(8,128)(2,1)}, u32[]{:S(2)}, u32[]{:S(2)}) collective-permute-start(bf16[128,2176]{1,0:T(8,128)(2,1)S(1)} %pad_maximum_fusion.refs_0_), channel_id=1, source_target_pairs={{0,24},{4,100},{8,0},{12,108},{16,8},{20,116},{24,16},{28,124},{32... | collective-permute-start | bytes 1671176 | tf_op jit(solution)/shard_map/ppermute | solution.py:53
  37.4 16.6 %collective-permute-start.6 = (bf16[128,2176]{1,0:T(8,128)(2,1)S(1)}, bf16[128,2176]{1,0:T(8,128)(2,1)}, u32[]{:S(2)}, u32[]{:S(2)}) collective-permute-start(bf16[128,2176]{1,0:T(8,128)(2,1)S(1)} %pad_maximum_fusion.refs_0_), channel_id=1, source_target_pairs={{0,8},{4,36},{8,16},{12,44},{16,24},{20,52},{24,0},{28,60},{32,40}... | collective-permute-start | bytes 1671176 | tf_op jit(solution)/shard_map/ppermute | solution.py:53
  38.4 14.8 %all-to-all-start = ((bf16[32,16,224]{2,1,0:T(8,128)(2,1)}), bf16[32,16,224]{2,1,0:T(8,128)(2,1)S(1)}, u32[]{:S(2)}, u32[]{:S(2)}) async-start(bf16[32,16,224]{2,1,0:T(8,128)(2,1)} %get-tuple-element.34), calls=%async_computation | async-start | bytes 524288 | tf_op jit(solution)/shard_map/all_to_all | solution.py:684
  50.0 7.8 %collective-permute-start.5 = (bf16[128,2176]{1,0:T(8,128)(2,1)S(1)}, bf16[128,2176]{1,0:T(8,128)(2,1)S(1)}, u32[]{:S(2)}, u32[]{:S(2)}) collective-permute-start(bf16[128,2176]{1,0:T(8,128)(2,1)S(1)} %pad_maximum_fusion.refs_0_), channel_id=1, source_target_pairs={{0,4},{4,0},{8,12},{12,8},{16,20},{20,16},{24,28},{28,24},{32,36},... | collective-permute-start | bytes 1671176 | tf_op jit(solution)/shard_map/ppermute | solution.py:46
  53.9 4.0 %collective-permute-start.9 = (bf16[128,2176]{1,0:T(8,128)(2,1)}, bf16[128,2176]{1,0:T(8,128)(2,1)S(1)}, u32[]{:S(2)}, u32[]{:S(2)}) collective-permute-start(bf16[128,2176]{1,0:T(8,128)(2,1)} %collective-permute-done.8.refs_2_), channel_id=1, source_target_pairs={{0,4},{4,0},{8,12},{12,8},{16,20},{20,16},{24,28},{28,24},{32,36},... | collective-permute-start | bytes 1671176 | tf_op jit(solution)/shard_map/ppermute | solution.py:46
  54.0 3.9 %collective-permute-start.7 = (bf16[128,2176]{1,0:T(8,128)(2,1)}, bf16[128,2176]{1,0:T(8,128)(2,1)S(1)}, u32[]{:S(2)}, u32[]{:S(2)}) collective-permute-start(bf16[128,2176]{1,0:T(8,128)(2,1)} %collective-permute-done.6.refs_1_), channel_id=1, source_target_pairs={{0,4},{4,0},{8,12},{12,8},{16,20},{20,16},{24,28},{28,24},{32,36},... | collective-permute-start | bytes 1671176 | tf_op jit(solution)/shard_map/ppermute | solution.py:46
  54.4 3.5 %collective-permute-start.13 = (bf16[128,2176]{1,0:T(8,128)(2,1)S(1)}, bf16[128,2176]{1,0:T(8,128)(2,1)S(1)}, u32[]{:S(2)}, u32[]{:S(2)}) collective-permute-start(bf16[128,2176]{1,0:T(8,128)(2,1)S(1)} %collective-permute-done.10.refs_3_), channel_id=1, source_target_pairs={{0,4},{4,0},{8,12},{12,8},{16,20},{20,16},{24,28},{28,24},{32,36},... | collective-permute-start | bytes 1671176 | tf_op jit(solution)/shard_map/ppermute | solution.py:46
  60.5 5.9 %collective-permute-start.14 = (bf16[8,32,224]{2,1,0:T(8,128)(2,1)S(1)}, bf16[8,32,224]{2,1,0:T(8,128)(2,1)S(1)}, u32[]{:S(2)}, u32[]{:S(2)}) collective-permute-start(bf16[8,32,224]{2,1,0:T(8,128)(2,1)S(1)} %get-tuple-element.38), channel_id=1, source_target_pairs={{0,1},{1,0},{2,3},{3,2},{4,5},{5,4},{6,7},{7,6},{8,9},{9,8},{10,11... | collective-permute-start | bytes 344072 | tf_op jit(solution)/shard_map/ppermute | solution.py:68
  61.8 6.7 %collective-permute-start.16 = (bf16[8,32,224]{2,1,0:T(8,128)(2,1)S(1)}, bf16[8,32,224]{2,1,0:T(8,128)(2,1)S(1)}, u32[]{:S(2)}, u32[]{:S(2)}) collective-permute-start(bf16[8,32,224]{2,1,0:T(8,128)(2,1)S(1)} %get-tuple-element.39), channel_id=1, source_target_pairs={{0,3},{1,2},{2,1},{3,0},{4,7},{5,6},{6,5},{7,4},{8,11},{9,10},{10,... | collective-permute-start | bytes 344072 | tf_op jit(solution)/shard_map/ppermute | solution.py:68
  66.4 6.3 %collective-permute-start.15 = (bf16[8,32,224]{2,1,0:T(8,128)(2,1)S(1)}, bf16[8,32,224]{2,1,0:T(8,128)(2,1)S(1)}, u32[]{:S(2)}, u32[]{:S(2)}) collective-permute-start(bf16[8,32,224]{2,1,0:T(8,128)(2,1)S(1)} %add_convert_fusion.3), channel_id=1, source_target_pairs={{0,3},{1,2},{2,1},{3,0},{4,7},{5,6},{6,5},{7,4},{8,11},{9,10},{10,... | collective-permute-start | bytes 344072 | tf_op jit(solution)/shard_map/ppermute | solution.py:68
  68.5 5.0 %collective-permute-start.17 = (bf16[8,32,224]{2,1,0:T(8,128)(2,1)S(1)}, bf16[8,32,224]{2,1,0:T(8,128)(2,1)S(1)}, u32[]{:S(2)}, u32[]{:S(2)}) collective-permute-start(bf16[8,32,224]{2,1,0:T(8,128)(2,1)S(1)} %add_convert_fusion.1), channel_id=1, source_target_pairs={{0,1},{1,0},{2,3},{3,2},{4,5},{5,4},{6,7},{7,6},{8,9},{9,8},{10,11... | collective-permute-start | bytes 344072 | tf_op jit(solution)/shard_map/ppermute | solution.py:68
  103.3 3.8 %collective-permute-start.18 = (bf16[16,64,896]{2,1,0:T(8,128)(2,1)S(1)}, bf16[16,64,896]{2,1,0:T(8,128)(2,1)S(1)}, u32[]{:S(2)}, u32[]{:S(2)}) collective-permute-start(bf16[16,64,896]{2,1,0:T(8,128)(2,1)S(1)} %all_to_all.20.x_ref.own_hbm), channel_id=1, source_target_pairs={{0,4},{4,0},{8,12},{12,8},{16,20},{20,16},{24,28},{28,24},{32,36},... | collective-permute-start | bytes 5505032 | tf_op jit(solution)/shard_map/ppermute | solution.py:46
  110.6 7.9 %collective-permute-start.21 = (bf16[256,256]{1,0:T(8,128)(2,1)S(1)}, bf16[256,256]{1,0:T(8,128)(2,1)S(1)}, u32[]{:S(2)}, u32[]{:S(2)}) collective-permute-start(bf16[256,256]{1,0:T(8,128)(2,1)S(1)} %up.3.a0), channel_id=1, source_target_pairs={{0,2},{1,3},{2,0},{3,1},{4,6},{5,7},{6,4},{7,5},{8,10},{9,11},{10,... | collective-permute-start | bytes 393224 | tf_op jit(solution)/shard_map/ppermute | solution.py:57
  111.8 7.3 %collective-permute-start.20 = (bf16[256,256]{1,0:T(8,128)(2,1)S(1)}, bf16[256,256]{1,0:T(8,128)(2,1)S(1)}, u32[]{:S(2)}, u32[]{:S(2)}) collective-permute-start(bf16[256,256]{1,0:T(8,128)(2,1)S(1)} %up.3.a0), channel_id=1, source_target_pairs={{0,3},{1,0},{2,1},{3,2},{4,7},{5,4},{6,5},{7,6},{8,11},{9,8},{10,9... | collective-permute-start | bytes 393224 | tf_op jit(solution)/shard_map/ppermute | solution.py:57
  113.7 6.9 %collective-permute-start.19 = (bf16[256,256]{1,0:T(8,128)(2,1)S(1)}, bf16[256,256]{1,0:T(8,128)(2,1)S(1)}, u32[]{:S(2)}, u32[]{:S(2)}) collective-permute-start(bf16[256,256]{1,0:T(8,128)(2,1)S(1)} %up.3.a0), channel_id=1, source_target_pairs={{0,1},{1,2},{2,3},{3,0},{4,5},{5,6},{6,7},{7,4},{8,9},{9,10},{10,1... | collective-permute-start | bytes 393224 | tf_op jit(solution)/shard_map/ppermute | solution.py:57
  120.6 5.3 %copy-start.1 = (bf16[16,64,896]{2,1,0:T(8,128)(2,1)S(1)}, bf16[16,64,896]{2,1,0:T(8,128)(2,1)}, u32[]{:S(2)}) copy-start(bf16[16,64,896]{2,1,0:T(8,128)(2,1)} %copy-done) | copy-start | bytes 5505028
  124.0 1.9 %collective-permute-start.22 = (bf16[128,1792]{1,0:T(8,128)(2,1)S(1)}, bf16[128,1792]{1,0:T(8,128)(2,1)S(1)}, u32[]{:S(2)}, u32[]{:S(2)}) collective-permute-start(bf16[128,1792]{1,0:T(8,128)(2,1)S(1)} %bitcast.35), channel_id=1, source_target_pairs={{0,4},{4,0},{8,12},{12,8},{16,20},{20,16},{24,28},{28,24},{32,36},... | collective-permute-start | bytes 1376264 | tf_op jit(solution)/shard_map/ppermute | solution.py:46
  (3 other events, 5.1 us)

commit v4 on v3

--- a/solution.py
+++ b/solution.py
@@ -133,13 +133,12 @@
 
 def attend_kernel(
     lengths, q_ref, qr_ref, k_hbm, r_hbm, vu_hbm, dw_hbm, res_ref, groups_ref, picks_ref, levels_ref,
-    kept_ref, given_ref, places_ref, spread_ref, cut_1, cut_3,
+    out_ref, places_ref, spread_ref, cut_1, cut_3,
     k_ref, r_ref, mix_ref, vu_ref, cut_ref, sems, cut_sems, vu_sem,
 ):
     rows, heads, lat = q_ref.shape
     width = vu_ref.shape[2]
     cuts = (cut_1, cut_3)
-    core = this_core()
     vu_copy = pltpu.make_async_copy(vu_hbm, vu_ref, vu_sem)
 
     def copies(row, slot):
@@ -165,10 +164,8 @@
         spread_ref[j] = res_ref[:, j * columns : (j + 1) * columns]
     places, levels = route_tables(upright(groups_ref), upright(picks_ref), upright(levels_ref))
     places_ref[...] = places
-    half = heads * width // 2
-    first = core == 0
-    kept_ref[:, half:] = jnp.where(first, places.astype(f32), levels.astype(f32)).astype(bf16)
-    given_ref[:, half:] = jnp.where(first, levels.astype(f32), places.astype(f32)).astype(bf16)
+    out_ref[:, heads * width : heads * width + 128] = places
+    out_ref[:, heads * width + 128 :] = levels
 
     def scores_of(row, slot):
         scores = lax.dot_general(
@@ -215,14 +212,12 @@
                 copy.wait()
                 leaving[n].start()
     vu_copy.wait()
-    for side, ref in ((core, kept_ref), (1 - core, given_ref)):
-        for i in range(heads // 2):
-            h = side * (heads // 2) + i
-            left = [mix_ref[j, pl.ds(h, rows, stride=heads), :] for j in range(mix_ref.shape[0])]
-            left = jnp.concatenate(left, axis=1).astype(bf16)
-            ref[:, i * width : (i + 1) * width] = jnp.dot(
-                left, vu_ref[h], preferred_element_type=f32
-            ).astype(bf16)
+    for h in range(heads):
+        left = [mix_ref[j, pl.ds(h, rows, stride=heads), :] for j in range(mix_ref.shape[0])]
+        left = jnp.concatenate(left, axis=1).astype(bf16)
+        out_ref[:, h * width : (h + 1) * width] = jnp.dot(
+            left, vu_ref[h], preferred_element_type=f32
+        ).astype(bf16)
     for copy in leaving:
         copy.wait()
 
@@ -241,10 +236,9 @@
     return pl.pallas_call(
         attend_kernel,
         in_specs=[small, whole, whole] + [far] * 4 + [whole] * 4,
-        out_specs=(whole,) * 4 + (far,) * 2,
+        out_specs=(whole,) * 3 + (far,) * 2,
         out_shape=(
-            jax.ShapeDtypeStruct((rows, heads * width // 2 + 128), bf16),
-            jax.ShapeDtypeStruct((rows, heads * width // 2 + 128), bf16),
+            jax.ShapeDtypeStruct((rows, heads * width + 2 * 128), bf16),
             jax.ShapeDtypeStruct((rows, 128), bf16),
             jax.ShapeDtypeStruct((residual.shape[1] // columns, rows, columns), bf16),
         )
@@ -272,74 +266,48 @@
     )
 
 
-def half_product(blocks, w_hbm, w_ref, sem, side):
-    half = w_ref.shape[1]
-    copy = pltpu.make_async_copy(
-        w_hbm.at[:, pl.ds(pl.multiple_of(side * half, half), half)], w_ref, sem
-    )
+def project_kernel(*refs):
+    blocks, w_hbm = refs[:SIDE], refs[SIDE]
+    out_ref, places_ref, levels_ref, w_ref, sem = refs[SIDE + 1 :]
+    depth = w_ref.shape[1]
+    copy = pltpu.make_async_copy(w_hbm, w_ref, sem)
     copy.start()
-    left = jnp.concatenate([block[:, :half] for block in blocks])
+    left = jnp.concatenate([block[:, :depth] for block in blocks])
+    rows = out_ref.shape[1]
+    for i, block in enumerate(blocks):
+        for j in range(SIDE):
+            at = slice(j * rows, (j + 1) * rows)
+            places_ref[i * SIDE + j] = block[at, depth : depth + 128]
+            levels_ref[i * SIDE + j] = block[at, depth + 128 :]
     copy.wait()
-    terms = lax.dot_general(left, w_ref[...], (((1,), (1,)), ((), ())), preferred_element_type=f32)
-    span = terms.shape[0] // SIDE
-    return [terms[i * span : (i + 1) * span] for i in range(SIDE)]
-
-
-def first_half_kernel(*refs):
-    blocks, w_hbm, out_ref, table_ref, w_ref, sem = refs[:SIDE], *refs[SIDE:]
-    for i, terms in enumerate(half_product(blocks, w_hbm, w_ref, sem, this_core())):
-        out_ref[i] = terms
-        table_ref[i] = blocks[i][:, w_ref.shape[1] :]
-
-
-def second_half_kernel(*refs):
-    blocks, w_hbm, made_ref, own_ref = refs[:SIDE], *refs[SIDE : SIDE + 3]
-    low_ref, high_ref, places_ref, levels_ref, w_ref, sem = refs[SIDE + 3 :]
-    core = this_core()
-    half = w_ref.shape[1]
-    made = half_product(blocks, w_hbm, w_ref, sem, 1 - core)
-    rows = made[0].shape[0] // SIDE
-    first = core == 0
-    for i in range(SIDE):
-        for j in range(SIDE):
-            at, across = slice(j * rows, (j + 1) * rows), slice(i * rows, (i + 1) * rows)
-            total = (made_ref[i, at] + made[j][across]).astype(bf16)
-            (low_ref if i < 2 else high_ref)[i % 2 * SIDE + j] = total
-            mine = own_ref[i, at].astype(f32)
-            theirs = blocks[j][across, half:].astype(f32)
-            places_ref[i * SIDE + j] = jnp.where(first, mine, theirs).astype(bf16)
-            levels_ref[i * SIDE + j] = jnp.where(first, theirs, mine).astype(bf16)
-
-
-def project(blocks, out_proj, before=None):
-    columns = out_proj.shape[1]
-    tall = blocks[0].shape[0]
-    rows = tall // SIDE
+    made = lax.dot_general(left, w_ref[...], (((1,), (1,)), ((), ())), preferred_element_type=f32)
+    made = made.astype(bf16)
+    for n in range(CHIPS):
+        out_ref[n] = made[n * rows : (n + 1) * rows]
+
+
+def project(blocks, out_proj):
+    depth, columns = out_proj.shape
+    rows = blocks[0].shape[0] // SIDE
     whole = pl.BlockSpec(memory_space=pltpu.VMEM)
     far = pl.BlockSpec(memory_space=pltpu.HBM)
-    if before is None:
-        out_shape = (
-            jax.ShapeDtypeStruct((SIDE, tall, columns), f32),
-            jax.ShapeDtypeStruct((SIDE, tall, 128), bf16),
-        )
-    else:
-        sums = jax.ShapeDtypeStruct((CHIPS // 2, rows, columns), bf16)
-        table = pltpu.HBM((CHIPS, rows, 128), bf16)
-        out_shape = (sums, sums, table, table)
-    before = before or ()
-    return pl.pallas_call(
-        second_half_kernel if before else first_half_kernel,
-        in_specs=[whole] * SIDE + [far] + [whole] * len(before),
-        out_specs=(whole,) * len(out_shape),
-        out_shape=out_shape,
-        scratch_shapes=[
-            pltpu.VMEM((columns, out_proj.shape[0] // 2), bf16),
-            pltpu.SemaphoreType.DMA,
-        ],
+    table = pltpu.HBM((CHIPS, rows, 128), bf16)
+    return pl.pallas_call(
+        project_kernel,
+        in_specs=[whole] * SIDE + [far],
+        out_specs=(whole,) * 3,
+        out_shape=(jax.ShapeDtypeStruct((CHIPS, rows, columns), bf16), table, table),
+        scratch_shapes=[pltpu.VMEM((columns, depth), bf16), pltpu.SemaphoreType.DMA],
         compiler_params=pltpu.CompilerParams(vmem_limit_bytes=VMEM),
         cost_estimate=pl.CostEstimate(flops=5 * 10**8, bytes_accessed=4 * 10**6, transcendentals=0),
         name="project",
-    )(*blocks, distant(out_proj.T), *before)
+    )(*blocks, distant(out_proj.T))
+
+
+def of_core(parity, table, chip, mine_ref, other_ref):
+    mine = mine_ref[table[chip]].astype(f32)
+    other = other_ref[table[CHIPS + chip]].astype(f32)
+    return jnp.where(this_core() == parity, mine, other)
 
 
 def slot_masks(mark, rows):
@@ -350,18 +318,21 @@
     return jnp.where((mark == wanted) & right_half, 1.0, 0.0).astype(bf16)
 
 
-def gate_kernel(table, places_ref, levels_ref, out_ref, made_ref):
+def gate_kernel(table, places_ref, places_other, levels_ref, levels_other, out_ref, made_ref):
     dp = lax.axis_index("dp")
     group = dp // EPG
-    rows = places_ref.shape[1] // CORES
+    rows = places_ref.shape[1]
     lane = lax.broadcasted_iota(jnp.int32, (2 * rows, 128), 1)
     for quarter in range(CHIPS // QUARTER):
         for parity in range(CORES):
             for pair in range(QUARTER // 2):
                 chips = (quarter * QUARTER + 2 * pair, quarter * QUARTER + 2 * pair + 1)
-                at = slice(parity * rows, (parity + 1) * rows)
-                mark = jnp.concatenate([places_ref[table[chip], at].astype(f32) for chip in chips])
-                level = jnp.concatenate([levels_ref[table[chip], at].astype(f32) for chip in chips])
+                mark = jnp.concatenate(
+                    [of_core(parity, table, chip, places_ref, places_other) for chip in chips]
+                )
+                level = jnp.concatenate(
+                    [of_core(parity, table, chip, levels_ref, levels_other) for chip in chips]
+                )
                 total = jnp.sum(jnp.where(lane < GROUPS * EPG, level, 0.0), axis=1, keepdims=True)
                 mine = jnp.sum(jnp.where(lane == dp, level, 0.0), axis=1, keepdims=True)
                 home = jnp.sum(
@@ -385,25 +356,18 @@
     whole = pl.BlockSpec(memory_space=pltpu.VMEM)
     return pl.pallas_call(
         gate_kernel,
-        in_specs=[pl.BlockSpec(memory_space=pltpu.SMEM), whole, whole],
+        in_specs=[pl.BlockSpec(memory_space=pltpu.SMEM)] + [whole] * 4,
         out_specs=whole,
         out_shape=jax.ShapeDtypeStruct((CHIPS * CORES * CAP, 128), f32),
         scratch_shapes=[pltpu.VMEM((128, 128), f32)],
         compiler_params=pltpu.CompilerParams(vmem_limit_bytes=VMEM),
         cost_estimate=pl.CostEstimate(flops=10**8, bytes_accessed=10**6, transcendentals=0),
         name="gate_table",
-    )(table, distant(places), distant(levels))
-
-
-def select_kernel(table, low_ref, high_ref, res_ref, places_ref, out_ref):
+    )(table, *[distant(value) for value in (*places, *levels)])
+
+
+def select_kernel(table, sums_ref, sums_other, res_ref, places_ref, places_other, out_ref):
     rows = res_ref.shape[2]
-
-    def attention_of(parity, chip):
-        place = table[chip]
-        side = CHIPS // 2
-        inside = place % side
-        at = slice(parity * rows, (parity + 1) * rows)
-        return jnp.where(place < side, low_ref[inside, at].astype(f32), high_ref[inside, at].astype(f32))
 
     for parity in range(CORES):
         for pair in range(QUARTER // 2):
@@ -412,10 +376,9 @@
                 parts = []
                 marks = []
                 for chip in (quarter * QUARTER + 2 * pair, quarter * QUARTER + 2 * pair + 1):
-                    attention = attention_of(parity, chip)
+                    attention = of_core(parity, table, chip, sums_ref, sums_other)
                     parts.append((res_ref[chip, parity].astype(f32) + attention).astype(bf16))
-                    at = slice(parity * rows, (parity + 1) * rows)
-                    marks.append(places_ref[table[chip], at].astype(f32))
+                    marks.append(of_core(parity, table, chip, places_ref, places_other))
                 hidden = jnp.concatenate(parts, axis=0)
                 mark = jnp.concatenate(marks, axis=0)
                 pick = slot_masks(mark, rows)
@@ -437,7 +400,7 @@
     whole = pl.BlockSpec(memory_space=pltpu.VMEM)
     return pl.pallas_call(
         select_kernel,
-        in_specs=[pl.BlockSpec(memory_space=pltpu.SMEM)] + [whole] * 4,
+        in_specs=[pl.BlockSpec(memory_space=pltpu.SMEM)] + [whole] * 5,
         out_specs=whole,
         out_shape=jax.ShapeDtypeStruct(
             (CHIPS, CORES * PART, CHIPS // QUARTER * columns), bf16
@@ -445,7 +408,7 @@
         compiler_params=pltpu.CompilerParams(vmem_limit_bytes=VMEM),
         cost_estimate=pl.CostEstimate(flops=10**9, bytes_accessed=6 * 10**6, transcendentals=0),
         name="select",
-    )(table, *parts, distant(residual), distant(places))
+    )(table, *parts, distant(residual), *[distant(value) for value in places])
 
 
 def unpacked(block, columns):
@@ -453,8 +416,8 @@
     return jnp.concatenate(parts, axis=0)
 
 
-def raise_up(x_ref, gw_hbm, uw_hbm, w_ref, sems, core, acc):
-    columns, units = gw_hbm.shape[2:]
+def weight_copies(gw_hbm, uw_hbm, w_ref, sems, core):
+    units = gw_hbm.shape[-1]
     span = CHIPS // QUARTER
     copies = []
     for part in range(QUARTER):
@@ -466,53 +429,82 @@
                     source.at[chips, core], w_ref.at[chips, :, lanes], sems.at[part, n]
                 )
             )
-    for copy in copies:
-        copy.start()
+    return copies
+
+
+def raise_up(x_ref, w_ref, acc, copies=None):
+    span = CHIPS // QUARTER
     for chip in range(CHIPS):
-        if chip % span == 0:
+        if copies is not None and chip % span == 0:
             copies[chip // span * 2].wait()
             copies[chip // span * 2 + 1].wait()
-        acc = acc + jnp.dot(unpacked(x_ref[chip], columns), w_ref[chip], preferred_element_type=f32)
+        acc = acc + jnp.dot(
+            unpacked(x_ref[chip], w_ref.shape[1]), w_ref[chip], preferred_element_type=f32
+        )
     return acc
 
 
-def up_kernel(x_ref, gw_hbm, uw_hbm, acc_ref, w_ref, sems):
-    zero = jnp.zeros(acc_ref.shape, f32)
-    acc_ref[...] = raise_up(x_ref, gw_hbm, uw_hbm, w_ref, sems, this_core(), zero)
-
-
-def act_kernel(acc_ref, x_ref, gw_hbm, uw_hbm, act_ref, w_ref, sems):
-    acc = raise_up(x_ref, gw_hbm, uw_hbm, w_ref, sems, 1 - this_core(), acc_ref[...])
-    units = acc.shape[1] // 2
-    gated = acc[:, :units]
-    act_ref[...] = (gated / (1.0 + jnp.exp(-gated)) * acc[:, units:]).astype(bf16)
-
-
-def up(x, gate_weight, up_weight, before=None):
+def up_kernel(x_ref, gw_hbm, uw_hbm, acc_ref, next_ref, w_ref, sems, next_sems):
+    core = this_core()
+    copies = weight_copies(gw_hbm, uw_hbm, w_ref, sems, core)
+    following = weight_copies(gw_hbm, uw_hbm, next_ref, next_sems, 1 - core)
+    for copy in copies + following:
+        copy.start()
+    acc_ref[...] = raise_up(x_ref, w_ref, jnp.zeros(acc_ref.shape, f32), copies)
+    for copy in following:
+        copy.wait()
+
+
+def up(x, gate_weight, up_weight):
     columns, units = gate_weight.shape[2:]
     slots = x.shape[1] * CHIPS // QUARTER
     whole = pl.BlockSpec(memory_space=pltpu.VMEM)
     far = pl.BlockSpec(memory_space=pltpu.HBM)
-    operands = (x,) if before is None else (before, x)
-    return pl.pallas_call(
-        up_kernel if before is None else act_kernel,
-        in_specs=[whole] * len(operands) + [far, far],
-        out_specs=whole,
+    return pl.pallas_call(
+        up_kernel,
+        in_specs=[whole, far, far],
+        out_specs=(whole, whole),
         out_shape=(
-            jax.ShapeDtypeStruct((slots, 2 * units), f32)
-            if before is None
-            else jax.ShapeDtypeStruct((slots, units), bf16)
+            jax.ShapeDtypeStruct((slots, 2 * units), f32),
+            pltpu.VMEM((CHIPS, columns, 2 * units), bf16),
         ),
         scratch_shapes=[
             pltpu.VMEM((CHIPS, columns, 2 * units), bf16),
             pltpu.SemaphoreType.DMA((QUARTER, 2)),
+            pltpu.SemaphoreType.DMA((QUARTER, 2)),
         ],
         compiler_params=pltpu.CompilerParams(vmem_limit_bytes=VMEM),
         cost_estimate=pl.CostEstimate(
-            flops=4 * CHIPS * slots * columns * units, bytes_accessed=6 * 10**6, transcendentals=0
+            flops=4 * CHIPS * slots * columns * units, bytes_accessed=9 * 10**6, transcendentals=0
         ),
         name="up",
-    )(*operands, distant(gate_weight), distant(up_weight))
+    )(x, distant(gate_weight), distant(up_weight))
+
+
+def act_kernel(acc_ref, x_ref, w_ref, act_ref):
+    acc = raise_up(x_ref, w_ref, acc_ref[...])
+    units = act_ref.shape[1]
+    gated = acc[:, :units]
+    act_ref[...] = (gated / (1.0 + jnp.exp(-gated)) * acc[:, units:]).astype(bf16)
+
+
+def activate(acc, x, weight):
+    slots = acc.shape[0]
+    units = weight.shape[-1] // 2
+    whole = pl.BlockSpec(memory_space=pltpu.VMEM)
+    return pl.pallas_call(
+        act_kernel,
+        in_specs=[whole] * 3,
+        out_specs=whole,
+        out_shape=jax.ShapeDtypeStruct((slots, units), bf16),
+        compiler_params=pltpu.CompilerParams(vmem_limit_bytes=VMEM),
+        cost_estimate=pl.CostEstimate(
+            flops=4 * slots * units * weight.shape[0] * weight.shape[1],
+            bytes_accessed=6 * 10**6,
+            transcendentals=slots * units,
+        ),
+        name="activate",
+    )(acc, x, weight)
 
 
 def cut_kernel(w_hbm, out_ref):
@@ -667,17 +659,13 @@
     quarter = model // PLANES
     opposite = move_z(cut(down_proj[0]), 2)
 
-    kept, given, places_here, spread, *sent = attend(
+    flat, places_here, spread, *sent = attend(
         query_latent, query_rope, cache_latent, cache_rope, lengths, value_up, down_proj[0], residual, columns,
         (groups.T, expert_picks.T, gate_levels.T),
     )
     weighting = places_here == (jnp.arange(128) % CAP + 1).astype(bf16)
     weighting = weighting.astype(bf16)
 
-    given = move_core(given)
-    flat = jnp.where(
-        core == 0, jnp.concatenate([kept, given], axis=0), jnp.concatenate([given, kept], axis=0)
-    )
     blocks = jnp.concatenate(around(flat, 0), axis=0)
 
     spread, blocks, opposite = lax.optimization_barrier((spread, blocks, opposite))
@@ -690,26 +678,31 @@
         (blocks[3], downs[:2], residual_columns)
     )
     swapped = [move_core(block) for block in blocks]
-    low, high, places_all, levels_all = project(swapped, out_proj, project(blocks, out_proj))
-    low, high = sum_z(low, high)
+    mine, places_mine, levels_mine = project(blocks, out_proj)
+    theirs, places_theirs, levels_theirs = project(swapped, out_proj)
+    mine, theirs = sum_z(mine, theirs)
+    places, levels = (places_mine, places_theirs), (levels_mine, levels_theirs)
 
     far = jnp.arange(SIDE, dtype=jnp.int32)
     x_far = (here_x - far) % SIDE
     y_far = (here_y - far) % SIDE
     x_spot = (x_far ^ (x_far >> 1))[:, None]
     y_spot = (y_far ^ (y_far >> 1))[None, :]
-    table = jnp.where(core == 0, y_spot * SIDE + x_spot, x_spot * SIDE + y_spot)
-    table = table.reshape(CHIPS).astype(jnp.int32)
-    gates = gate_table(table, places_all, levels_all)
-    outgoing = select(table, (low, high), residual_columns, places_all)
+    x_first = (y_spot * SIDE + x_spot).reshape(CHIPS)
+    y_first = (x_spot * SIDE + y_spot).reshape(CHIPS)
+    table = jnp.where(
+        core == 0, jnp.concatenate([x_first, y_first]), jnp.concatenate([y_first, x_first])
+    ).astype(jnp.int32)
+    gates = gate_table(table, places, levels)
+    outgoing = select(table, (mine, theirs), residual_columns, places)
     outgoing, gates = lax.optimization_barrier((outgoing, gates))
 
     own = chip_exchange(outgoing)
     other = move_core(own)
     gate_weight = gate_proj.reshape(CHIPS, CORES, columns, -1)
     up_weight = up_proj.reshape(CHIPS, CORES, columns, -1)
-    acc = up(own, gate_weight, up_weight)
-    act = up(other, gate_weight, up_weight, acc)
+    acc, weight = up(own, gate_weight, up_weight)
+    act = activate(acc, other, weight)
     acts = [act] + [move_z(act, by) for by in (1, 3, 2)]
     made = down(acts, down_proj[0], downs, gates)
     pieces = made.reshape(CHIPS // QUARTER, CORES, PART, quarter)

time: 151 us -> 147 us (0.974)
  waiting for transfers between devices: 33.4 us -> 30.6 us
  starting transfers between devices: 27.1 us -> 29.3 us
  Pallas kernels: 35.4 us -> 33.5 us
  local copies, waits for them, and re-layouts: 2.51 us -> 0.98 us
    pallas_call x4, Pallas kernels: 12.2 us -> 10.4 us  [the longest x2 5.85 us: project(): pl.pallas_call(project_kernel, in_specs=[whole] * SIDE + [far], out_specs...]
    ppermute x4, starting transfers between devices: 2.01 us -> 3.78 us  [add(): moved = lax.ppermute(block, 'tensor', pairs)]
    ppermute x7 -> x6, waiting for transfers between devices: 4 us -> 2.34 us  [move_core(): return lax.ppermute(value, 'dp', place_pairs(lambda x, y, c: (x, y, 1 - c)))]
    unnamed x22 -> x20, local copies, waits for them, and re-layouts: 1.66 us -> 0.04 us
  transfers between devices with their start and end apart: 24 -> 23, of which waited for: 14 -> 14; matrix products, arithmetic and copies ran while one was open for 0% -> 0% of each run, Pallas kernels for 15% -> 17%
where the time goes in v4:
time: 147 us; the launch traced here: 146 us
  blocking collectives  50.9 us (35%)
  Pallas kernels  33.5 us (23%)
  waiting for transfers between devices  30.6 us (21%)
  starting transfers between devices  29.3 us (20%)
    all_to_all x2, blocking collectives, chip_exchange(): lax.all_to_all(value, 'dp', split_axis=0, concat_axis=0, axis_index_group...  42 us
    pallas_call x1, Pallas kernels, attend(): pl.pallas_call(attend_kernel, in_specs=[small, whole, whole] + [far] * 4...  14.9 us
    ppermute x6, waiting for transfers between devices, move_z(): lax.ppermute(value, 'tensor', [(z, (z + by) % PLANES) for z in range(PLAN...  14.2 us
    ppermute x6, starting transfers between devices, move_ring(): return lax.ppermute(value, 'dp', place_pairs(place))  10.4 us
    ppermute x6, starting transfers between devices, move_z(): lax.ppermute(value, 'tensor', [(z, (z + by) % PLANES) for z in range(PLAN...  9.83 us
    all_to_all x1, blocking collectives, spread_z(): lax.all_to_all(copies, 'tensor', split_axis=0, concat_axis=0, tiled=True)  8.88 us
    ppermute x4, waiting for transfers between devices, add(): moved = lax.ppermute(block, 'tensor', pairs)  8.54 us
    pallas_call x2, Pallas kernels, project(): pl.pallas_call(project_kernel, in_specs=[whole] * SIDE + [far], out_specs...  5.85 us
  transfers between devices with their start and end apart: 23, of which 14 were waited for; matrix products, arithmetic and copies ran while one was open for 0% of the time, Pallas kernels for 17%

profile of v4, /device:TPU:0, one launch (start us, length us, event | category | flops | bytes accessed | tf_op | source)
XLA Modules:
  0.0 146.2 jit_solution(13949501849692120909)
XLA Ops:
  0.0 1.3 cut.1
  1.3 4.0 %collective-permute-start.3 = (bf16[256,1792]{1,0:T(8,128)(2,1)S(1)}, bf16[256,1792]{1,0:T(8,128)(2,1)S(1)}, u32[]{:S(2)}, u32[]{:S(2)}) collective-permute-start(bf16[256,1792]{1,0:T(8,128)(2,1)S(1)} %cut.1), channel_id=1, source_target_pairs={{0,2},{1,3},{2,0},{3,1},{4,6},{5,7},{6,4},{7,5},{8,10},{9,11},{10,... | collective-permute-start | bytes 2752520 | tf_op jit(solution)/shard_map/ppermute | solution.py:57
  5.3 14.9 %attend.1 = (bf16[16,4352]{1,0:T(8,128)(2,1)S(1)}, bf16[16,128]{1,0:T(8,128)(2,1)S(1)}, bf16[32,16,224]{2,1,0:T(8,128)(2,1)}, bf16[256,1792]{1,0:T(8,128)(2,1)S(1)}, bf16[256,1792]{1,0:T(8,128)(2,1)}) custom-call(s32[16]{0:T(128)S(1)} %copy-done.8, bf16[16,32,512]{2,1,0:T(8,128)(2,1)S(1)} %copy-done.2, bf16[16,32,64]{2,1,0:T(8,128)(2,1)S(1)} %copy-done.4, ...), custom_call_target="tpu_custom_call" | custom-call | flops 1073741824 | bytes 18874368 | tf_op jit(solution)/shard_map/attend/pallas_call | solution.py:236
  20.2 3.1 %collective-permute-start.2 = (bf16[16,4352]{1,0:T(8,128)(2,1)S(1)}, bf16[16,4352]{1,0:T(8,128)(2,1)S(1)}, u32[]{:S(2)}, u32[]{:S(2)}) collective-permute-start(bf16[16,4352]{1,0:T(8,128)(2,1)S(1)} %get-tuple-element.30), channel_id=1, source_target_pairs={{0,64},{4,20},{8,72},{12,28},{16,80},{20,4},{24,88},{28,12},{32,96... | collective-permute-start | bytes 417800 | tf_op jit(solution)/shard_map/ppermute | solution.py:53
  23.3 1.1 collective-permute-start.1
  26.9 1.7 %collective-permute-start.8 = (bf16[256,1792]{1,0:T(8,128)(2,1)}, bf16[256,1792]{1,0:T(8,128)(2,1)}, u32[]{:S(2)}, u32[]{:S(2)}) collective-permute-start(bf16[256,1792]{1,0:T(8,128)(2,1)} %get-tuple-element.33), channel_id=1, source_target_pairs={{0,3},{1,0},{2,1},{3,2},{4,7},{5,4},{6,5},{7,6},{8,11},{9,8},{10,9... | collective-permute-start | bytes 2752520 | tf_op jit(solution)/shard_map/ppermute | solution.py:57
  28.6 2.1 %collective-permute-done = bf16[16,4352]{1,0:T(8,128)(2,1)S(1)} collective-permute-done((bf16[16,4352]{1,0:T(8,128)(2,1)S(1)}, bf16[16,4352]{1,0:T(8,128)(2,1)S(1)}, u32[]{:S(2)}, u32[]{:S(2)}) %collective-permute-start) | collective-permute-done | bytes 139296 | tf_op jit(solution)/shard_map/ppermute | solution.py:53
  30.8 3.3 %collective-permute-start.6 = (bf16[64,4352]{1,0:T(8,128)(2,1)S(1)}, bf16[64,4352]{1,0:T(8,128)(2,1)S(1)}, u32[]{:S(2)}, u32[]{:S(2)}) collective-permute-start(bf16[64,4352]{1,0:T(8,128)(2,1)S(1)} %pad_maximum_fusion.refs_0_), channel_id=1, source_target_pairs={{0,16},{4,68},{8,24},{12,76},{16,0},{20,84},{24,8},{28,92},{32,48}... | collective-permute-start | bytes 1671176 | tf_op jit(solution)/shard_map/ppermute | solution.py:53
  34.1 1.1 collective-permute-start.5
  36.1 4.6 %all-to-all-start = ((bf16[32,16,224]{2,1,0:T(8,128)(2,1)}), bf16[32,16,224]{2,1,0:T(8,128)(2,1)}, u32[]{:S(2)}, u32[]{:S(2)}) async-start(bf16[32,16,224]{2,1,0:T(8,128)(2,1)} %get-tuple-element.34), calls=%async_computation | async-start | bytes 524288 | tf_op jit(solution)/shard_map/all_to_all | solution.py:672
  40.7 7.1 %collective-permute-done.7.w1 = bf16[256,1792]{1,0:T(8,128)(2,1)} collective-permute-done((bf16[256,1792]{1,0:T(8,128)(2,1)S(1)}, bf16[256,1792]{1,0:T(8,128)(2,1)}, u32[]{:S(2)}, u32[]{:S(2)}) %collective-permute-start.7) | collective-permute-done | bytes 917536 | tf_op jit(solution)/shard_map/ppermute | solution.py:57
  48.1 2.9 %all-to-all-done = bf16[32,16,224]{2,1,0:T(8,128)(2,1)} async-done(((bf16[32,16,224]{2,1,0:T(8,128)(2,1)}), bf16[32,16,224]{2,1,0:T(8,128)(2,1)}, u32[]{:S(2)}, u32[]{:S(2)}) %all-to-all-start) | async-done | bytes 229408 | tf_op jit(solution)/shard_map/all_to_all | solution.py:672
  52.0 2.2 %project.2 = (bf16[16,16,224]{2,1,0:T(8,128)(2,1)S(1)}, bf16[16,16,128]{2,1,0:T(8,128)(2,1)}, bf16[16,16,128]{2,1,0:T(8,128)(2,1)}) custom-call(bf16[64,4352]{1,0:T(8,128)(2,1)S(1)} %pad_maximum_fusion.refs_0_, bf16[64,4352]{1,0:T(8,128)(2,1)S(1)} %collective-permute-done.4.refs_1_, bf16[64,4352]{1,0:T(8,128)(2,1)S(1)} %collective-permute-done.5.refs_2_, ...), custom_call_target="tpu_custom_call" | custom-call | flops 500000000 | bytes 4000000 | tf_op jit(solution)/shard_map/project/pallas_call | solution.py:295
  54.2 1.3 collective-permute-start.9
  55.6 3.6 %project.3 = (bf16[16,16,224]{2,1,0:T(8,128)(2,1)S(1)}, bf16[16,16,128]{2,1,0:T(8,128)(2,1)}, bf16[16,16,128]{2,1,0:T(8,128)(2,1)}) custom-call(bf16[64,4352]{1,0:T(8,128)(2,1)S(1)} %collective-permute-done.11.refs_0_, bf16[64,4352]{1,0:T(8,128)(2,1)} %collective-permute-done.12.refs_1_, bf16[64,4352]{1,0:T(8,128)(2,1)} %collective-permute-done.13.refs_2_, ...), custom_call_target="tpu_custom_call" | custom-call | flops 500000000 | bytes 4000000 | tf_op jit(solution)/shard_map/project/pallas_call | solution.py:295
  60.3 2.3 %collective-permute-start.10 = (bf16[16,16,224]{2,1,0:T(8,128)(2,1)S(1)}, bf16[16,16,224]{2,1,0:T(8,128)(2,1)S(1)}, u32[]{:S(2)}, u32[]{:S(2)}) collective-permute-start(bf16[16,16,224]{2,1,0:T(8,128)(2,1)S(1)} %add_convert_fusion.3), channel_id=1, source_target_pairs={{0,3},{1,2},{2,1},{3,0},{4,7},{5,6},{6,5},{7,4},{8,11},{9,10},{10,... | collective-permute-start | bytes 344072 | tf_op jit(solution)/shard_map/ppermute | solution.py:68
  62.6 4.2 %collective-permute-done.15 = bf16[16,16,224]{2,1,0:T(8,128)(2,1)S(1)} collective-permute-done((bf16[16,16,224]{2,1,0:T(8,128)(2,1)S(1)}, bf16[16,16,224]{2,1,0:T(8,128)(2,1)S(1)}, u32[]{:S(2)}, u32[]{:S(2)}) %collective-permute-start.15) | collective-permute-done | bytes 114720 | tf_op jit(solution)/shard_map/ppermute | solution.py:68
  67.0 1.9 %collective-permute-done.10 = bf16[16,16,224]{2,1,0:T(8,128)(2,1)S(1)} collective-permute-done((bf16[16,16,224]{2,1,0:T(8,128)(2,1)S(1)}, bf16[16,16,224]{2,1,0:T(8,128)(2,1)S(1)}, u32[]{:S(2)}, u32[]{:S(2)}) %collective-permute-start.10) | collective-permute-done | bytes 114720 | tf_op jit(solution)/shard_map/ppermute | solution.py:68
  68.9 1.5 %gate_table.1.gates_ref = f32[256,128]{1,0:T(8,128)S(1)} custom-call(s32[32]{0:T(128)S(1)} %broadcast_select_fusion.table, bf16[16,16,128]{2,1,0:T(8,128)(2,1)} %get-tuple-element.39.places_ref, bf16[16,16,128]{2,1,0:T(8,128)(2,1)} %get-tuple-element.40.places_other, bf16[16,16,128]{2,1,0:T(8,128)(2,1)} %get-tuple-element.41.levels_ref, ...), custom_call_target="tpu_custom_call" | custom-call | flops 100000000 | bytes 1000000 | tf_op jit(solution)/shard_map/gate_table/pallas_call | solution.py:357
  70.4 1.5 %collective-permute-done.16 = bf16[16,16,224]{2,1,0:T(8,128)(2,1)S(1)} collective-permute-done((bf16[16,16,224]{2,1,0:T(8,128)(2,1)S(1)}, bf16[16,16,224]{2,1,0:T(8,128)(2,1)S(1)}, u32[]{:S(2)}, u32[]{:S(2)}) %collective-permute-start.16) | collective-permute-done | bytes 114720 | tf_op jit(solution)/shard_map/ppermute | solution.py:68
  72.0 1.6 %select.39 = bf16[16,64,896]{2,1,0:T(8,128)(2,1)S(1)} custom-call(s32[32]{0:T(128)S(1)} %broadcast_select_fusion.table, bf16[16,16,224]{2,1,0:T(8,128)(2,1)S(1)} %add_convert_fusion.2.sums_ref, bf16[16,16,224]{2,1,0:T(8,128)(2,1)S(1)} %add_convert_fusion.sums_other, bf16[16,2,16,224]{3,2,1,0:T(8,128)(2,1)} %bitcast.4.res_ref, ...), custom_call_target="tpu_custom_call" | custom-call | flops 1000000000 | bytes 6000000 | tf_op jit(solution)/shard_map/select/pallas_call | solution.py:401
  73.5 27.5 %all_to_all.20.x_ref.own_hbm = bf16[16,64,896]{2,1,0:T(8,128)(2,1)S(1)} all-to-all(bf16[16,64,896]{2,1,0:T(8,128)(2,1)S(1)} %select.39), channel_id=1, replica_groups={{0,8,16,24,32,40,48,56,64,72,80,88,96,104,112,120},{4,12,20,28,36,44,52..., dimensions={0} | all-to-all | bytes 3670016 | tf_op jit(solution)/shard_map/all_to_all | solution.py:78
  101.0 3.2 %up.1 = (f32[256,512]{1,0:T(8,128)S(1)}, bf16[16,224,512]{2,1,0:T(8,128)(2,1)S(1)}) custom-call(bf16[16,64,896]{2,1,0:T(8,128)(2,1)S(1)} %all_to_all.20.x_ref.own_hbm, bf16[16,2,224,256]{3,2,1,0:T(8,128)(2,1)} %bitcast.30, bf16[16,2,224,256]{3,2,1,0:T(8,128)(2,1)} %bitcast.31), custom_call_target="tpu_custom_call" | custom-call | flops 939524096 | bytes 9000000 | tf_op jit(solution)/shard_map/up/pallas_call | solution.py:463
  104.8 1.3 activate.1.a0
  106.1 1.1 collective-permute-start.20
  107.2 1.5 %collective-permute-start.19 = (bf16[256,256]{1,0:T(8,128)(2,1)S(1)}, bf16[256,256]{1,0:T(8,128)(2,1)S(1)}, u32[]{:S(2)}, u32[]{:S(2)}) collective-permute-start(bf16[256,256]{1,0:T(8,128)(2,1)S(1)} %activate.1.a0), channel_id=1, source_target_pairs={{0,3},{1,0},{2,1},{3,2},{4,7},{5,4},{6,5},{7,6},{8,11},{9,8},{10,9... | collective-permute-start | bytes 393224 | tf_op jit(solution)/shard_map/ppermute | solution.py:57
  109.2 4.8 %collective-permute-done.20.a3 = bf16[256,256]{1,0:T(8,128)(2,1)S(1)} collective-permute-done((bf16[256,256]{1,0:T(8,128)(2,1)S(1)}, bf16[256,256]{1,0:T(8,128)(2,1)S(1)}, u32[]{:S(2)}, u32[]{:S(2)}) %collective-permute-start.20) | collective-permute-done | bytes 131104 | tf_op jit(solution)/shard_map/ppermute | solution.py:57
  114.6 1.5 %collective-permute-done.18.a1 = bf16[256,256]{1,0:T(8,128)(2,1)S(1)} collective-permute-done((bf16[256,256]{1,0:T(8,128)(2,1)S(1)}, bf16[256,256]{1,0:T(8,128)(2,1)S(1)}, u32[]{:S(2)}, u32[]{:S(2)}) %collective-permute-start.18) | collective-permute-done | bytes 131104 | tf_op jit(solution)/shard_map/ppermute | solution.py:57
  116.1 3.3 %down.1.y_ref = bf16[256,1792]{1,0:T(8,128)(2,1)S(1)} custom-call(bf16[256,256]{1,0:T(8,128)(2,1)S(1)} %activate.1.a0, bf16[256,256]{1,0:T(8,128)(2,1)S(1)} %collective-permute-done.18.a1, bf16[256,256]{1,0:T(8,128)(2,1)S(1)} %collective-permute-done.19.a2, bf16[256,256]{1,0:T(8,128)(2,1)S(1)} %collective-permute-done.20.a3, bf16[256,7168]{1,0:T(8,128)(2,1)} %bitcast.27, ...), custom_call_target="tpu_custom_call" | custom-call | flops 939524096 | bytes 6000000 | tf_op jit(solution)/shard_map/down/pallas_call | solution.py:554
  119.6 1.8 %collective-permute-done.21.received_ref = bf16[128,1792]{1,0:T(8,128)(2,1)S(1)} collective-permute-done((bf16[128,1792]{1,0:T(8,128)(2,1)S(1)}, bf16[128,1792]{1,0:T(8,128)(2,1)S(1)}, u32[]{:S(2)}, u32[]{:S(2)}) %collective-permute-start.21) | collective-permute-done | bytes 458784 | tf_op jit(solution)/shard_map/ppermute | solution.py:46
  121.9 14.5 %all_to_all.21 = bf16[16,8,1792]{2,1,0:T(8,128)(2,1)S(1)} all-to-all(bf16[16,8,1792]{2,1,0:T(8,128)(2,1)S(1)} %bitcast.21), channel_id=1, replica_groups={{0,8,16,24,32,40,48,56,64,72,80,88,96,104,112,120},{4,12,20,28,36,44,52..., dimensions={0} | all-to-all | bytes 917504 | tf_op jit(solution)/shard_map/all_to_all | solution.py:78
  136.6 8.9 %all_to_all.22 = bf16[4,16,1792]{2,1,0:T(8,128)(2,1)S(1)} all-to-all(bf16[4,16,1792]{2,1,0:T(8,128)(2,1)S(1)} %broadcast_in_dim.2), channel_id=1, replica_groups=mesh['dp'=32,'tensor'=4] {'tensor'}, dimensions={0} | all-to-all | bytes 458752 | tf_op jit(solution)/shard_map/all_to_all | solution.py:62
  (65 shorter events, 9.3 us)
Async XLA Ops:
  0.0 5.3 %copy-start.2 = (bf16[16,32,512]{2,1,0:T(8,128)(2,1)S(1)}, bf16[16,32,512]{2,1,0:T(8,128)(2,1)}, u32[]{:S(2)}) copy-start(bf16[16,32,512]{2,1,0:T(8,128)(2,1)} %q_ref.1) | copy-start | bytes 1572868
  0.0 5.3 %copy-start.3 = (bf16[16,7168]{1,0:T(8,128)(2,1)S(1)}, bf16[16,7168]{1,0:T(8,128)(2,1)}, u32[]{:S(2)}) copy-start(bf16[16,7168]{1,0:T(8,128)(2,1)} %res_ref.1) | copy-start | bytes 688132
  0.0 5.3 %copy-start.4 = (bf16[16,32,64]{2,1,0:T(8,128)(2,1)S(1)}, bf16[16,32,64]{2,1,0:T(8,128)(2,1)}, u32[]{:S(2)}) copy-start(bf16[16,32,64]{2,1,0:T(8,128)(2,1)} %qr_ref.1) | copy-start | bytes 196612
  0.0 5.3 %copy-start.5 = (s32[16,8]{0,1:T(8,128)S(1)}, s32[16,8]{0,1:T(8,128)}, u32[]{:S(2)}) copy-start(s32[16,8]{0,1:T(8,128)} %param.26) | copy-start | bytes 1540
  0.0 5.3 %copy-start.6 = (s32[16,8]{0,1:T(8,128)S(1)}, s32[16,8]{0,1:T(8,128)}, u32[]{:S(2)}) copy-start(s32[16,8]{0,1:T(8,128)} %param.27) | copy-start | bytes 1540
  0.0 5.3 %copy-start.7 = (s32[16,4]{0,1:T(4,128)S(1)}, s32[16,4]{0,1:T(4,128)}, u32[]{:S(2)}) copy-start(s32[16,4]{0,1:T(4,128)} %param.25) | copy-start | bytes 772
  0.0 5.3 %copy-start.8 = (s32[16]{0:T(128)S(1)}, s32[16]{0:T(128)}, u32[]{:S(2)}) copy-start(s32[16]{0:T(128)} %lengths.1) | copy-start | bytes 196
  1.3 29.5 %collective-permute-start.3 = (bf16[256,1792]{1,0:T(8,128)(2,1)S(1)}, bf16[256,1792]{1,0:T(8,128)(2,1)S(1)}, u32[]{:S(2)}, u32[]{:S(2)}) collective-permute-start(bf16[256,1792]{1,0:T(8,128)(2,1)S(1)} %cut.1), channel_id=1, source_target_pairs={{0,2},{1,3},{2,0},{3,1},{4,6},{5,7},{6,4},{7,5},{8,10},{9,11},{10,... | collective-permute-start | bytes 2752520 | tf_op jit(solution)/shard_map/ppermute | solution.py:57
  20.2 6.6 %collective-permute-start.2 = (bf16[16,4352]{1,0:T(8,128)(2,1)S(1)}, bf16[16,4352]{1,0:T(8,128)(2,1)S(1)}, u32[]{:S(2)}, u32[]{:S(2)}) collective-permute-start(bf16[16,4352]{1,0:T(8,128)(2,1)S(1)} %get-tuple-element.30), channel_id=1, source_target_pairs={{0,64},{4,20},{8,72},{12,28},{16,80},{20,4},{24,88},{28,12},{32,96... | collective-permute-start | bytes 417800 | tf_op jit(solution)/shard_map/ppermute | solution.py:53
  23.3 5.3 %collective-permute-start.1 = (bf16[16,4352]{1,0:T(8,128)(2,1)S(1)}, bf16[16,4352]{1,0:T(8,128)(2,1)S(1)}, u32[]{:S(2)}, u32[]{:S(2)}) collective-permute-start(bf16[16,4352]{1,0:T(8,128)(2,1)S(1)} %get-tuple-element.30), channel_id=1, source_target_pairs={{0,96},{4,28},{8,104},{12,4},{16,112},{20,12},{24,120},{28,20},{32... | collective-permute-start | bytes 417800 | tf_op jit(solution)/shard_map/ppermute | solution.py:53
  24.5 6.3 %collective-permute-start = (bf16[16,4352]{1,0:T(8,128)(2,1)S(1)}, bf16[16,4352]{1,0:T(8,128)(2,1)S(1)}, u32[]{:S(2)}, u32[]{:S(2)}) collective-permute-start(bf16[16,4352]{1,0:T(8,128)(2,1)S(1)} %get-tuple-element.30), channel_id=1, source_target_pairs={{0,32},{4,12},{8,40},{12,20},{16,48},{20,28},{24,56},{28,4},{32,64... | collective-permute-start | bytes 417800 | tf_op jit(solution)/shard_map/ppermute | solution.py:53
  25.3 22.5 %collective-permute-start.7 = (bf16[256,1792]{1,0:T(8,128)(2,1)S(1)}, bf16[256,1792]{1,0:T(8,128)(2,1)}, u32[]{:S(2)}, u32[]{:S(2)}) collective-permute-start(bf16[256,1792]{1,0:T(8,128)(2,1)S(1)} %get-tuple-element.32), channel_id=1, source_target_pairs={{0,1},{1,2},{2,3},{3,0},{4,5},{5,6},{6,7},{7,4},{8,9},{9,10},{10,1... | collective-permute-start | bytes 2752520 | tf_op jit(solution)/shard_map/ppermute | solution.py:57
  26.9 21.3 %collective-permute-start.8 = (bf16[256,1792]{1,0:T(8,128)(2,1)}, bf16[256,1792]{1,0:T(8,128)(2,1)}, u32[]{:S(2)}, u32[]{:S(2)}) collective-permute-start(bf16[256,1792]{1,0:T(8,128)(2,1)} %get-tuple-element.33), channel_id=1, source_target_pairs={{0,3},{1,0},{2,1},{3,2},{4,7},{5,4},{6,5},{7,6},{8,11},{9,8},{10,9... | collective-permute-start | bytes 2752520 | tf_op jit(solution)/shard_map/ppermute | solution.py:57
  30.8 3.3 %copy-start.9 = (bf16[256,1792]{1,0:T(8,128)(2,1)}, bf16[256,1792]{1,0:T(8,128)(2,1)S(1)}, u32[]{:S(2)}) copy-start(bf16[256,1792]{1,0:T(8,128)(2,1)S(1)} %collective-permute-done.3.w3) | copy-start | bytes 2752516
  30.8 20.2 %collective-permute-start.6 = (bf16[64,4352]{1,0:T(8,128)(2,1)S(1)}, bf16[64,4352]{1,0:T(8,128)(2,1)S(1)}, u32[]{:S(2)}, u32[]{:S(2)}) collective-permute-start(bf16[64,4352]{1,0:T(8,128)(2,1)S(1)} %pad_maximum_fusion.refs_0_), channel_id=1, source_target_pairs={{0,16},{4,68},{8,24},{12,76},{16,0},{20,84},{24,8},{28,92},{32,48}... | collective-permute-start | bytes 1671176 | tf_op jit(solution)/shard_map/ppermute | solution.py:53
  34.1 17.1 %collective-permute-start.5 = (bf16[64,4352]{1,0:T(8,128)(2,1)S(1)}, bf16[64,4352]{1,0:T(8,128)(2,1)S(1)}, u32[]{:S(2)}, u32[]{:S(2)}) collective-permute-start(bf16[64,4352]{1,0:T(8,128)(2,1)S(1)} %pad_maximum_fusion.refs_0_), channel_id=1, source_target_pairs={{0,24},{4,100},{8,0},{12,108},{16,8},{20,116},{24,16},{28,124},{32... | collective-permute-start | bytes 1671176 | tf_op jit(solution)/shard_map/ppermute | solution.py:53
  35.1 16.4 %collective-permute-start.4 = (bf16[64,4352]{1,0:T(8,128)(2,1)S(1)}, bf16[64,4352]{1,0:T(8,128)(2,1)S(1)}, u32[]{:S(2)}, u32[]{:S(2)}) collective-permute-start(bf16[64,4352]{1,0:T(8,128)(2,1)S(1)} %pad_maximum_fusion.refs_0_), channel_id=1, source_target_pairs={{0,8},{4,36},{8,16},{12,44},{16,24},{20,52},{24,0},{28,60},{32,40}... | collective-permute-start | bytes 1671176 | tf_op jit(solution)/shard_map/ppermute | solution.py:53
  36.1 14.9 %all-to-all-start = ((bf16[32,16,224]{2,1,0:T(8,128)(2,1)}), bf16[32,16,224]{2,1,0:T(8,128)(2,1)}, u32[]{:S(2)}, u32[]{:S(2)}) async-start(bf16[32,16,224]{2,1,0:T(8,128)(2,1)} %get-tuple-element.34), calls=%async_computation | async-start | bytes 524288 | tf_op jit(solution)/shard_map/all_to_all | solution.py:672
  47.8 7.8 %collective-permute-start.11 = (bf16[64,4352]{1,0:T(8,128)(2,1)S(1)}, bf16[64,4352]{1,0:T(8,128)(2,1)S(1)}, u32[]{:S(2)}, u32[]{:S(2)}) collective-permute-start(bf16[64,4352]{1,0:T(8,128)(2,1)S(1)} %pad_maximum_fusion.refs_0_), channel_id=1, source_target_pairs={{0,4},{4,0},{8,12},{12,8},{16,20},{20,16},{24,28},{28,24},{32,36},... | collective-permute-start | bytes 1671176 | tf_op jit(solution)/shard_map/ppermute | solution.py:46
  51.0 4.6 %collective-permute-start.14 = (bf16[64,4352]{1,0:T(8,128)(2,1)S(1)}, bf16[64,4352]{1,0:T(8,128)(2,1)S(1)}, u32[]{:S(2)}, u32[]{:S(2)}) collective-permute-start(bf16[64,4352]{1,0:T(8,128)(2,1)S(1)} %collective-permute-done.6.refs_3_), channel_id=1, source_target_pairs={{0,4},{4,0},{8,12},{12,8},{16,20},{20,16},{24,28},{28,24},{32,36},... | collective-permute-start | bytes 1671176 | tf_op jit(solution)/shard_map/ppermute | solution.py:46
  51.1 4.4 %collective-permute-start.13 = (bf16[64,4352]{1,0:T(8,128)(2,1)S(1)}, bf16[64,4352]{1,0:T(8,128)(2,1)}, u32[]{:S(2)}, u32[]{:S(2)}) collective-permute-start(bf16[64,4352]{1,0:T(8,128)(2,1)S(1)} %collective-permute-done.5.refs_2_), channel_id=1, source_target_pairs={{0,4},{4,0},{8,12},{12,8},{16,20},{20,16},{24,28},{28,24},{32,36},... | collective-permute-start | bytes 1671176 | tf_op jit(solution)/shard_map/ppermute | solution.py:46
  51.5 4.0 %collective-permute-start.12 = (bf16[64,4352]{1,0:T(8,128)(2,1)S(1)}, bf16[64,4352]{1,0:T(8,128)(2,1)}, u32[]{:S(2)}, u32[]{:S(2)}) collective-permute-start(bf16[64,4352]{1,0:T(8,128)(2,1)S(1)} %collective-permute-done.4.refs_1_), channel_id=1, source_target_pairs={{0,4},{4,0},{8,12},{12,8},{16,20},{20,16},{24,28},{28,24},{32,36},... | collective-permute-start | bytes 1671176 | tf_op jit(solution)/shard_map/ppermute | solution.py:46
  54.2 6.1 %collective-permute-start.9 = (bf16[16,16,224]{2,1,0:T(8,128)(2,1)S(1)}, bf16[16,16,224]{2,1,0:T(8,128)(2,1)S(1)}, u32[]{:S(2)}, u32[]{:S(2)}) collective-permute-start(bf16[16,16,224]{2,1,0:T(8,128)(2,1)S(1)} %get-tuple-element.36), channel_id=1, source_target_pairs={{0,1},{1,0},{2,3},{3,2},{4,5},{5,4},{6,7},{7,6},{8,9},{9,8},{10,11... | collective-permute-start | bytes 344072 | tf_op jit(solution)/shard_map/ppermute | solution.py:68
  59.2 7.6 %collective-permute-start.15 = (bf16[16,16,224]{2,1,0:T(8,128)(2,1)S(1)}, bf16[16,16,224]{2,1,0:T(8,128)(2,1)S(1)}, u32[]{:S(2)}, u32[]{:S(2)}) collective-permute-start(bf16[16,16,224]{2,1,0:T(8,128)(2,1)S(1)} %get-tuple-element.37), channel_id=1, source_target_pairs={{0,3},{1,2},{2,1},{3,0},{4,7},{5,6},{6,5},{7,4},{8,11},{9,10},{10,... | collective-permute-start | bytes 344072 | tf_op jit(solution)/shard_map/ppermute | solution.py:68
  60.3 8.5 %collective-permute-start.10 = (bf16[16,16,224]{2,1,0:T(8,128)(2,1)S(1)}, bf16[16,16,224]{2,1,0:T(8,128)(2,1)S(1)}, u32[]{:S(2)}, u32[]{:S(2)}) collective-permute-start(bf16[16,16,224]{2,1,0:T(8,128)(2,1)S(1)} %add_convert_fusion.3), channel_id=1, source_target_pairs={{0,3},{1,2},{2,1},{3,0},{4,7},{5,6},{6,5},{7,4},{8,11},{9,10},{10,... | collective-permute-start | bytes 344072 | tf_op jit(solution)/shard_map/ppermute | solution.py:68
  66.9 5.0 %collective-permute-start.16 = (bf16[16,16,224]{2,1,0:T(8,128)(2,1)S(1)}, bf16[16,16,224]{2,1,0:T(8,128)(2,1)S(1)}, u32[]{:S(2)}, u32[]{:S(2)}) collective-permute-start(bf16[16,16,224]{2,1,0:T(8,128)(2,1)S(1)} %add_convert_fusion.1), channel_id=1, source_target_pairs={{0,1},{1,0},{2,3},{3,2},{4,5},{5,4},{6,7},{7,6},{8,9},{9,8},{10,11... | collective-permute-start | bytes 344072 | tf_op jit(solution)/shard_map/ppermute | solution.py:68
  101.0 3.8 %collective-permute-start.17 = (bf16[16,64,896]{2,1,0:T(8,128)(2,1)S(1)}, bf16[16,64,896]{2,1,0:T(8,128)(2,1)S(1)}, u32[]{:S(2)}, u32[]{:S(2)}) collective-permute-start(bf16[16,64,896]{2,1,0:T(8,128)(2,1)S(1)} %all_to_all.20.x_ref.own_hbm), channel_id=1, source_target_pairs={{0,4},{4,0},{8,12},{12,8},{16,20},{20,16},{24,28},{28,24},{32,36},... | collective-permute-start | bytes 5505032 | tf_op jit(solution)/shard_map/ppermute | solution.py:46
  106.1 7.9 %collective-permute-start.20 = (bf16[256,256]{1,0:T(8,128)(2,1)S(1)}, bf16[256,256]{1,0:T(8,128)(2,1)S(1)}, u32[]{:S(2)}, u32[]{:S(2)}) collective-permute-start(bf16[256,256]{1,0:T(8,128)(2,1)S(1)} %activate.1.a0), channel_id=1, source_target_pairs={{0,2},{1,3},{2,0},{3,1},{4,6},{5,7},{6,4},{7,5},{8,10},{9,11},{10,... | collective-permute-start | bytes 393224 | tf_op jit(solution)/shard_map/ppermute | solution.py:57
  107.2 7.4 %collective-permute-start.19 = (bf16[256,256]{1,0:T(8,128)(2,1)S(1)}, bf16[256,256]{1,0:T(8,128)(2,1)S(1)}, u32[]{:S(2)}, u32[]{:S(2)}) collective-permute-start(bf16[256,256]{1,0:T(8,128)(2,1)S(1)} %activate.1.a0), channel_id=1, source_target_pairs={{0,3},{1,0},{2,1},{3,2},{4,7},{5,4},{6,5},{7,6},{8,11},{9,8},{10,9... | collective-permute-start | bytes 393224 | tf_op jit(solution)/shard_map/ppermute | solution.py:57
  108.7 7.4 %collective-permute-start.18 = (bf16[256,256]{1,0:T(8,128)(2,1)S(1)}, bf16[256,256]{1,0:T(8,128)(2,1)S(1)}, u32[]{:S(2)}, u32[]{:S(2)}) collective-permute-start(bf16[256,256]{1,0:T(8,128)(2,1)S(1)} %activate.1.a0), channel_id=1, source_target_pairs={{0,1},{1,2},{2,3},{3,0},{4,5},{5,6},{6,7},{7,4},{8,9},{9,10},{10,1... | collective-permute-start | bytes 393224 | tf_op jit(solution)/shard_map/ppermute | solution.py:57
  116.1 5.3 %copy-start.1 = (bf16[16,64,896]{2,1,0:T(8,128)(2,1)S(1)}, bf16[16,64,896]{2,1,0:T(8,128)(2,1)}, u32[]{:S(2)}) copy-start(bf16[16,64,896]{2,1,0:T(8,128)(2,1)} %copy-done) | copy-start | bytes 5505028
  119.4 1.9 %collective-permute-start.21 = (bf16[128,1792]{1,0:T(8,128)(2,1)S(1)}, bf16[128,1792]{1,0:T(8,128)(2,1)S(1)}, u32[]{:S(2)}, u32[]{:S(2)}) collective-permute-start(bf16[128,1792]{1,0:T(8,128)(2,1)S(1)} %bitcast.33), channel_id=1, source_target_pairs={{0,4},{4,0},{8,12},{12,8},{16,20},{20,16},{24,28},{28,24},{32,36},... | collective-permute-start | bytes 1376264 | tf_op jit(solution)/shard_map/ppermute | solution.py:46
  (1 other events, 1.3 us)

commit v5 on v4

--- a/solution.py
+++ b/solution.py
@@ -246,7 +246,7 @@
         scratch_shapes=[
             pltpu.VMEM((DEPTH, positions, lat), bf16),
             pltpu.VMEM((DEPTH, rope, positions), bf16),
-            pltpu.VMEM((lat // 128, rows * heads, 128), f32),
+            pltpu.VMEM((lat // 128, (rows + 1) * heads, 128), f32),
             pltpu.VMEM((heads, lat, width), bf16),
             pltpu.VMEM((2, units, model // PLANES), bf16),
             pltpu.SemaphoreType.DMA((2, DEPTH)),
@@ -268,10 +268,18 @@
 
 def project_kernel(*refs):
     blocks, w_hbm = refs[:SIDE], refs[SIDE]
-    out_ref, places_ref, levels_ref, w_ref, sem = refs[SIDE + 1 :]
+    out_ref, places_ref, levels_ref, w_ref, b_ref, sems = refs[SIDE + 1 :]
     depth = w_ref.shape[1]
-    copy = pltpu.make_async_copy(w_hbm, w_ref, sem)
+    copy = pltpu.make_async_copy(w_hbm, w_ref, sems.at[SIDE])
+    moves = [
+        pltpu.make_async_copy(block, b_ref.at[n], sems.at[n]) for n, block in enumerate(blocks)
+    ]
+    for move in moves:
+        move.start()
     copy.start()
+    for move in moves:
+        move.wait()
+    blocks = [b_ref.at[n] for n in range(SIDE)]
     left = jnp.concatenate([block[:, :depth] for block in blocks])
     rows = out_ref.shape[1]
     for i, block in enumerate(blocks):
@@ -294,10 +302,14 @@
     table = pltpu.HBM((CHIPS, rows, 128), bf16)
     return pl.pallas_call(
         project_kernel,
-        in_specs=[whole] * SIDE + [far],
+        in_specs=[far] * (SIDE + 1),
         out_specs=(whole,) * 3,
         out_shape=(jax.ShapeDtypeStruct((CHIPS, rows, columns), bf16), table, table),
-        scratch_shapes=[pltpu.VMEM((columns, depth), bf16), pltpu.SemaphoreType.DMA],
+        scratch_shapes=[
+            pltpu.VMEM((columns, depth), bf16),
+            pltpu.VMEM((SIDE,) + blocks[0].shape, bf16),
+            pltpu.SemaphoreType.DMA((SIDE + 1,)),
+        ],
         compiler_params=pltpu.CompilerParams(vmem_limit_bytes=VMEM),
         cost_estimate=pl.CostEstimate(flops=5 * 10**8, bytes_accessed=4 * 10**6, transcendentals=0),
         name="project",

time: 147 us -> 146 us (level)
  no operation moved by 1% of the time
where the time goes in v5:
time: 146 us
  blocking collectives  50.8 us (35%)
  Pallas kernels  33 us (23%)
  waiting for transfers between devices  31.5 us (22%)
  starting transfers between devices  28.5 us (20%)
    all_to_all x2, blocking collectives, chip_exchange(): lax.all_to_all(value, 'dp', split_axis=0, concat_axis=0, axis_index_group...  42 us
    pallas_call x1, Pallas kernels, attend(): pl.pallas_call(attend_kernel, in_specs=[small, whole, whole] + [far] * 4...  14.9 us
    ppermute x6, waiting for transfers between devices, move_z(): lax.ppermute(value, 'tensor', [(z, (z + by) % PLANES) for z in range(PLAN...  14.2 us
    ppermute x6, starting transfers between devices, move_ring(): return lax.ppermute(value, 'dp', place_pairs(place))  10.4 us
    ppermute x6, starting transfers between devices, move_z(): lax.ppermute(value, 'tensor', [(z, (z + by) % PLANES) for z in range(PLAN...  9.81 us
    ppermute x4, waiting for transfers between devices, add(): moved = lax.ppermute(block, 'tensor', pairs)  9.39 us
    all_to_all x1, blocking collectives, spread_z(): lax.all_to_all(copies, 'tensor', split_axis=0, concat_axis=0, tiled=True)  8.88 us
    pallas_call x2, Pallas kernels, project(): pl.pallas_call(project_kernel, in_specs=[far] * (SIDE + 1), out_specs=(wh...  5.32 us
  transfers between devices with their start and end apart: 23, of which 14 were waited for; matrix products, arithmetic and copies ran while one was open for 0% of the time, Pallas kernels for 17%

profile of v5, /device:TPU:0, one launch (start us, length us, event | category | flops | bytes accessed | tf_op | source)
XLA Modules:
  0.0 145.7 jit_solution(8832772444433377598)
XLA Ops:
  0.0 1.3 cut.1
  1.3 4.0 %collective-permute-start.3 = (bf16[256,1792]{1,0:T(8,128)(2,1)S(1)}, bf16[256,1792]{1,0:T(8,128)(2,1)S(1)}, u32[]{:S(2)}, u32[]{:S(2)}) collective-permute-start(bf16[256,1792]{1,0:T(8,128)(2,1)S(1)} %cut.1), channel_id=1, source_target_pairs={{0,2},{1,3},{2,0},{3,1},{4,6},{5,7},{6,4},{7,5},{8,10},{9,11},{10,... | collective-permute-start | bytes 2752520 | tf_op jit(solution)/shard_map/ppermute | solution.py:57
  5.3 14.9 %attend.1 = (bf16[16,4352]{1,0:T(8,128)(2,1)S(1)}, bf16[16,128]{1,0:T(8,128)(2,1)S(1)}, bf16[32,16,224]{2,1,0:T(8,128)(2,1)}, bf16[256,1792]{1,0:T(8,128)(2,1)S(1)}, bf16[256,1792]{1,0:T(8,128)(2,1)}) custom-call(s32[16]{0:T(128)S(1)} %copy-done.8, bf16[16,32,512]{2,1,0:T(8,128)(2,1)S(1)} %copy-done.2, bf16[16,32,64]{2,1,0:T(8,128)(2,1)S(1)} %copy-done.4, ...), custom_call_target="tpu_custom_call" | custom-call | flops 1073741824 | bytes 18874368 | tf_op jit(solution)/shard_map/attend/pallas_call | solution.py:236
  20.2 3.1 %collective-permute-start.2 = (bf16[16,4352]{1,0:T(8,128)(2,1)S(1)}, bf16[16,4352]{1,0:T(8,128)(2,1)S(1)}, u32[]{:S(2)}, u32[]{:S(2)}) collective-permute-start(bf16[16,4352]{1,0:T(8,128)(2,1)S(1)} %get-tuple-element.30), channel_id=1, source_target_pairs={{0,64},{4,20},{8,72},{12,28},{16,80},{20,4},{24,88},{28,12},{32,96... | collective-permute-start | bytes 417800 | tf_op jit(solution)/shard_map/ppermute | solution.py:53
  23.3 1.1 collective-permute-start.1
  26.9 1.7 %collective-permute-start.8 = (bf16[256,1792]{1,0:T(8,128)(2,1)}, bf16[256,1792]{1,0:T(8,128)(2,1)}, u32[]{:S(2)}, u32[]{:S(2)}) collective-permute-start(bf16[256,1792]{1,0:T(8,128)(2,1)} %get-tuple-element.33), channel_id=1, source_target_pairs={{0,3},{1,0},{2,1},{3,2},{4,7},{5,4},{6,5},{7,6},{8,11},{9,8},{10,9... | collective-permute-start | bytes 2752520 | tf_op jit(solution)/shard_map/ppermute | solution.py:57
  28.6 2.1 %collective-permute-done = bf16[16,4352]{1,0:T(8,128)(2,1)S(1)} collective-permute-done((bf16[16,4352]{1,0:T(8,128)(2,1)S(1)}, bf16[16,4352]{1,0:T(8,128)(2,1)S(1)}, u32[]{:S(2)}, u32[]{:S(2)}) %collective-permute-start) | collective-permute-done | bytes 139296 | tf_op jit(solution)/shard_map/ppermute | solution.py:53
  30.8 3.3 %collective-permute-start.6 = (bf16[64,4352]{1,0:T(8,128)(2,1)S(1)}, bf16[64,4352]{1,0:T(8,128)(2,1)S(1)}, u32[]{:S(2)}, u32[]{:S(2)}) collective-permute-start(bf16[64,4352]{1,0:T(8,128)(2,1)S(1)} %pad_maximum_fusion.refs_0_), channel_id=1, source_target_pairs={{0,16},{4,68},{8,24},{12,76},{16,0},{20,84},{24,8},{28,92},{32,48}... | collective-permute-start | bytes 1671176 | tf_op jit(solution)/shard_map/ppermute | solution.py:53
  34.1 1.1 collective-permute-start.5
  36.1 4.6 %all-to-all-start = ((bf16[32,16,224]{2,1,0:T(8,128)(2,1)}), bf16[32,16,224]{2,1,0:T(8,128)(2,1)}, u32[]{:S(2)}, u32[]{:S(2)}) async-start(bf16[32,16,224]{2,1,0:T(8,128)(2,1)} %get-tuple-element.34), calls=%async_computation | async-start | bytes 524288 | tf_op jit(solution)/shard_map/all_to_all | solution.py:684
  40.7 7.1 %collective-permute-done.7.w1 = bf16[256,1792]{1,0:T(8,128)(2,1)} collective-permute-done((bf16[256,1792]{1,0:T(8,128)(2,1)S(1)}, bf16[256,1792]{1,0:T(8,128)(2,1)}, u32[]{:S(2)}, u32[]{:S(2)}) %collective-permute-start.7) | collective-permute-done | bytes 917536 | tf_op jit(solution)/shard_map/ppermute | solution.py:57
  48.1 2.9 %all-to-all-done = bf16[32,16,224]{2,1,0:T(8,128)(2,1)} async-done(((bf16[32,16,224]{2,1,0:T(8,128)(2,1)}), bf16[32,16,224]{2,1,0:T(8,128)(2,1)}, u32[]{:S(2)}, u32[]{:S(2)}) %all-to-all-start) | async-done | bytes 229408 | tf_op jit(solution)/shard_map/all_to_all | solution.py:684
  52.0 2.6 %project.2 = (bf16[16,16,224]{2,1,0:T(8,128)(2,1)S(1)}, bf16[16,16,128]{2,1,0:T(8,128)(2,1)}, bf16[16,16,128]{2,1,0:T(8,128)(2,1)}) custom-call(bf16[64,4352]{1,0:T(8,128)(2,1)S(1)} %pad_maximum_fusion.refs_0_, bf16[64,4352]{1,0:T(8,128)(2,1)S(1)} %collective-permute-done.4.refs_1_, bf16[64,4352]{1,0:T(8,128)(2,1)S(1)} %collective-permute-done.5.refs_2_, ...), custom_call_target="tpu_custom_call" | custom-call | flops 500000000 | bytes 4000000 | tf_op jit(solution)/shard_map/project/pallas_call | solution.py:303
  54.6 1.3 collective-permute-start.9
  56.0 2.7 %project.3 = (bf16[16,16,224]{2,1,0:T(8,128)(2,1)S(1)}, bf16[16,16,128]{2,1,0:T(8,128)(2,1)}, bf16[16,16,128]{2,1,0:T(8,128)(2,1)}) custom-call(bf16[64,4352]{1,0:T(8,128)(2,1)S(1)} %collective-permute-done.11.refs_0_, bf16[64,4352]{1,0:T(8,128)(2,1)} %collective-permute-done.12.refs_1_, bf16[64,4352]{1,0:T(8,128)(2,1)} %collective-permute-done.13.refs_2_, ...), custom_call_target="tpu_custom_call" | custom-call | flops 500000000 | bytes 4000000 | tf_op jit(solution)/shard_map/project/pallas_call | solution.py:303
  58.8 1.8 %collective-permute-done.9 = bf16[16,16,224]{2,1,0:T(8,128)(2,1)S(1)} collective-permute-done((bf16[16,16,224]{2,1,0:T(8,128)(2,1)S(1)}, bf16[16,16,224]{2,1,0:T(8,128)(2,1)S(1)}, u32[]{:S(2)}, u32[]{:S(2)}) %collective-permute-start.9) | collective-permute-done | bytes 114720 | tf_op jit(solution)/shard_map/ppermute | solution.py:68
  60.6 1.5 %collective-permute-start.10 = (bf16[16,16,224]{2,1,0:T(8,128)(2,1)S(1)}, bf16[16,16,224]{2,1,0:T(8,128)(2,1)S(1)}, u32[]{:S(2)}, u32[]{:S(2)}) collective-permute-start(bf16[16,16,224]{2,1,0:T(8,128)(2,1)S(1)} %add_convert_fusion.3), channel_id=1, source_target_pairs={{0,3},{1,2},{2,1},{3,0},{4,7},{5,6},{6,5},{7,4},{8,11},{9,10},{10,... | collective-permute-start | bytes 344072 | tf_op jit(solution)/shard_map/ppermute | solution.py:68
  62.1 4.2 %collective-permute-done.15 = bf16[16,16,224]{2,1,0:T(8,128)(2,1)S(1)} collective-permute-done((bf16[16,16,224]{2,1,0:T(8,128)(2,1)S(1)}, bf16[16,16,224]{2,1,0:T(8,128)(2,1)S(1)}, u32[]{:S(2)}, u32[]{:S(2)}) %collective-permute-start.15) | collective-permute-done | bytes 114720 | tf_op jit(solution)/shard_map/ppermute | solution.py:68
  66.5 1.8 %collective-permute-done.10 = bf16[16,16,224]{2,1,0:T(8,128)(2,1)S(1)} collective-permute-done((bf16[16,16,224]{2,1,0:T(8,128)(2,1)S(1)}, bf16[16,16,224]{2,1,0:T(8,128)(2,1)S(1)}, u32[]{:S(2)}, u32[]{:S(2)}) %collective-permute-start.10) | collective-permute-done | bytes 114720 | tf_op jit(solution)/shard_map/ppermute | solution.py:68
  68.3 1.5 %gate_table.1.gates_ref = f32[256,128]{1,0:T(8,128)S(1)} custom-call(s32[32]{0:T(128)S(1)} %broadcast_select_fusion.table, bf16[16,16,128]{2,1,0:T(8,128)(2,1)} %get-tuple-element.39.places_ref, bf16[16,16,128]{2,1,0:T(8,128)(2,1)} %get-tuple-element.40.places_other, bf16[16,16,128]{2,1,0:T(8,128)(2,1)} %get-tuple-element.41.levels_ref, ...), custom_call_target="tpu_custom_call" | custom-call | flops 100000000 | bytes 1000000 | tf_op jit(solution)/shard_map/gate_table/pallas_call | solution.py:369
  69.9 1.6 %collective-permute-done.16 = bf16[16,16,224]{2,1,0:T(8,128)(2,1)S(1)} collective-permute-done((bf16[16,16,224]{2,1,0:T(8,128)(2,1)S(1)}, bf16[16,16,224]{2,1,0:T(8,128)(2,1)S(1)}, u32[]{:S(2)}, u32[]{:S(2)}) %collective-permute-start.16) | collective-permute-done | bytes 114720 | tf_op jit(solution)/shard_map/ppermute | solution.py:68
  71.5 1.6 %select.39 = bf16[16,64,896]{2,1,0:T(8,128)(2,1)S(1)} custom-call(s32[32]{0:T(128)S(1)} %broadcast_select_fusion.table, bf16[16,16,224]{2,1,0:T(8,128)(2,1)S(1)} %add_convert_fusion.2.sums_ref, bf16[16,16,224]{2,1,0:T(8,128)(2,1)S(1)} %add_convert_fusion.sums_other, bf16[16,2,16,224]{3,2,1,0:T(8,128)(2,1)} %bitcast.4.res_ref, ...), custom_call_target="tpu_custom_call" | custom-call | flops 1000000000 | bytes 6000000 | tf_op jit(solution)/shard_map/select/pallas_call | solution.py:413
  73.1 27.4 %all_to_all.20.x_ref.own_hbm = bf16[16,64,896]{2,1,0:T(8,128)(2,1)S(1)} all-to-all(bf16[16,64,896]{2,1,0:T(8,128)(2,1)S(1)} %select.39), channel_id=1, replica_groups={{0,8,16,24,32,40,48,56,64,72,80,88,96,104,112,120},{4,12,20,28,36,44,52..., dimensions={0} | all-to-all | bytes 3670016 | tf_op jit(solution)/shard_map/all_to_all | solution.py:78
  100.5 3.2 %up.1 = (f32[256,512]{1,0:T(8,128)S(1)}, bf16[16,224,512]{2,1,0:T(8,128)(2,1)S(1)}) custom-call(bf16[16,64,896]{2,1,0:T(8,128)(2,1)S(1)} %all_to_all.20.x_ref.own_hbm, bf16[16,2,224,256]{3,2,1,0:T(8,128)(2,1)} %bitcast.30, bf16[16,2,224,256]{3,2,1,0:T(8,128)(2,1)} %bitcast.31), custom_call_target="tpu_custom_call" | custom-call | flops 939524096 | bytes 9000000 | tf_op jit(solution)/shard_map/up/pallas_call | solution.py:475
  104.3 1.3 activate.1.a0
  106.7 1.5 %collective-permute-start.19 = (bf16[256,256]{1,0:T(8,128)(2,1)S(1)}, bf16[256,256]{1,0:T(8,128)(2,1)S(1)}, u32[]{:S(2)}, u32[]{:S(2)}) collective-permute-start(bf16[256,256]{1,0:T(8,128)(2,1)S(1)} %activate.1.a0), channel_id=1, source_target_pairs={{0,3},{1,0},{2,1},{3,2},{4,7},{5,4},{6,5},{7,6},{8,11},{9,8},{10,9... | collective-permute-start | bytes 393224 | tf_op jit(solution)/shard_map/ppermute | solution.py:57
  108.7 4.8 %collective-permute-done.20.a3 = bf16[256,256]{1,0:T(8,128)(2,1)S(1)} collective-permute-done((bf16[256,256]{1,0:T(8,128)(2,1)S(1)}, bf16[256,256]{1,0:T(8,128)(2,1)S(1)}, u32[]{:S(2)}, u32[]{:S(2)}) %collective-permute-start.20) | collective-permute-done | bytes 131104 | tf_op jit(solution)/shard_map/ppermute | solution.py:57
  114.1 1.4 collective-permute-done.18.a1
  115.5 3.3 %down.1.y_ref = bf16[256,1792]{1,0:T(8,128)(2,1)S(1)} custom-call(bf16[256,256]{1,0:T(8,128)(2,1)S(1)} %activate.1.a0, bf16[256,256]{1,0:T(8,128)(2,1)S(1)} %collective-permute-done.18.a1, bf16[256,256]{1,0:T(8,128)(2,1)S(1)} %collective-permute-done.19.a2, bf16[256,256]{1,0:T(8,128)(2,1)S(1)} %collective-permute-done.20.a3, bf16[256,7168]{1,0:T(8,128)(2,1)} %bitcast.27, ...), custom_call_target="tpu_custom_call" | custom-call | flops 939524096 | bytes 6000000 | tf_op jit(solution)/shard_map/down/pallas_call | solution.py:566
  119.0 1.8 %collective-permute-done.21.received_ref = bf16[128,1792]{1,0:T(8,128)(2,1)S(1)} collective-permute-done((bf16[128,1792]{1,0:T(8,128)(2,1)S(1)}, bf16[128,1792]{1,0:T(8,128)(2,1)S(1)}, u32[]{:S(2)}, u32[]{:S(2)}) %collective-permute-start.21) | collective-permute-done | bytes 458784 | tf_op jit(solution)/shard_map/ppermute | solution.py:46
  121.4 14.5 %all_to_all.21 = bf16[16,8,1792]{2,1,0:T(8,128)(2,1)S(1)} all-to-all(bf16[16,8,1792]{2,1,0:T(8,128)(2,1)S(1)} %bitcast.21), channel_id=1, replica_groups={{0,8,16,24,32,40,48,56,64,72,80,88,96,104,112,120},{4,12,20,28,36,44,52..., dimensions={0} | all-to-all | bytes 917504 | tf_op jit(solution)/shard_map/all_to_all | solution.py:78
  136.1 8.9 %all_to_all.22 = bf16[4,16,1792]{2,1,0:T(8,128)(2,1)S(1)} all-to-all(bf16[4,16,1792]{2,1,0:T(8,128)(2,1)S(1)} %broadcast_in_dim.2), channel_id=1, replica_groups=mesh['dp'=32,'tensor'=4] {'tensor'}, dimensions={0} | all-to-all | bytes 458752 | tf_op jit(solution)/shard_map/all_to_all | solution.py:62
  (65 shorter events, 9.5 us)
Async XLA Ops:
  0.0 5.3 %copy-start.2 = (bf16[16,32,512]{2,1,0:T(8,128)(2,1)S(1)}, bf16[16,32,512]{2,1,0:T(8,128)(2,1)}, u32[]{:S(2)}) copy-start(bf16[16,32,512]{2,1,0:T(8,128)(2,1)} %q_ref.1) | copy-start | bytes 1572868
  0.0 5.3 %copy-start.3 = (bf16[16,7168]{1,0:T(8,128)(2,1)S(1)}, bf16[16,7168]{1,0:T(8,128)(2,1)}, u32[]{:S(2)}) copy-start(bf16[16,7168]{1,0:T(8,128)(2,1)} %res_ref.1) | copy-start | bytes 688132
  0.0 5.3 %copy-start.4 = (bf16[16,32,64]{2,1,0:T(8,128)(2,1)S(1)}, bf16[16,32,64]{2,1,0:T(8,128)(2,1)}, u32[]{:S(2)}) copy-start(bf16[16,32,64]{2,1,0:T(8,128)(2,1)} %qr_ref.1) | copy-start | bytes 196612
  0.0 5.3 %copy-start.5 = (s32[16,8]{0,1:T(8,128)S(1)}, s32[16,8]{0,1:T(8,128)}, u32[]{:S(2)}) copy-start(s32[16,8]{0,1:T(8,128)} %param.26) | copy-start | bytes 1540
  0.0 5.3 %copy-start.6 = (s32[16,8]{0,1:T(8,128)S(1)}, s32[16,8]{0,1:T(8,128)}, u32[]{:S(2)}) copy-start(s32[16,8]{0,1:T(8,128)} %param.27) | copy-start | bytes 1540
  0.0 5.3 %copy-start.7 = (s32[16,4]{0,1:T(4,128)S(1)}, s32[16,4]{0,1:T(4,128)}, u32[]{:S(2)}) copy-start(s32[16,4]{0,1:T(4,128)} %param.25) | copy-start | bytes 772
  0.0 5.3 %copy-start.8 = (s32[16]{0:T(128)S(1)}, s32[16]{0:T(128)}, u32[]{:S(2)}) copy-start(s32[16]{0:T(128)} %lengths.1) | copy-start | bytes 196
  1.3 29.5 %collective-permute-start.3 = (bf16[256,1792]{1,0:T(8,128)(2,1)S(1)}, bf16[256,1792]{1,0:T(8,128)(2,1)S(1)}, u32[]{:S(2)}, u32[]{:S(2)}) collective-permute-start(bf16[256,1792]{1,0:T(8,128)(2,1)S(1)} %cut.1), channel_id=1, source_target_pairs={{0,2},{1,3},{2,0},{3,1},{4,6},{5,7},{6,4},{7,5},{8,10},{9,11},{10,... | collective-permute-start | bytes 2752520 | tf_op jit(solution)/shard_map/ppermute | solution.py:57
  20.2 6.6 %collective-permute-start.2 = (bf16[16,4352]{1,0:T(8,128)(2,1)S(1)}, bf16[16,4352]{1,0:T(8,128)(2,1)S(1)}, u32[]{:S(2)}, u32[]{:S(2)}) collective-permute-start(bf16[16,4352]{1,0:T(8,128)(2,1)S(1)} %get-tuple-element.30), channel_id=1, source_target_pairs={{0,64},{4,20},{8,72},{12,28},{16,80},{20,4},{24,88},{28,12},{32,96... | collective-permute-start | bytes 417800 | tf_op jit(solution)/shard_map/ppermute | solution.py:53
  23.3 5.3 %collective-permute-start.1 = (bf16[16,4352]{1,0:T(8,128)(2,1)S(1)}, bf16[16,4352]{1,0:T(8,128)(2,1)S(1)}, u32[]{:S(2)}, u32[]{:S(2)}) collective-permute-start(bf16[16,4352]{1,0:T(8,128)(2,1)S(1)} %get-tuple-element.30), channel_id=1, source_target_pairs={{0,96},{4,28},{8,104},{12,4},{16,112},{20,12},{24,120},{28,20},{32... | collective-permute-start | bytes 417800 | tf_op jit(solution)/shard_map/ppermute | solution.py:53
  24.5 6.3 %collective-permute-start = (bf16[16,4352]{1,0:T(8,128)(2,1)S(1)}, bf16[16,4352]{1,0:T(8,128)(2,1)S(1)}, u32[]{:S(2)}, u32[]{:S(2)}) collective-permute-start(bf16[16,4352]{1,0:T(8,128)(2,1)S(1)} %get-tuple-element.30), channel_id=1, source_target_pairs={{0,32},{4,12},{8,40},{12,20},{16,48},{20,28},{24,56},{28,4},{32,64... | collective-permute-start | bytes 417800 | tf_op jit(solution)/shard_map/ppermute | solution.py:53
  25.3 22.5 %collective-permute-start.7 = (bf16[256,1792]{1,0:T(8,128)(2,1)S(1)}, bf16[256,1792]{1,0:T(8,128)(2,1)}, u32[]{:S(2)}, u32[]{:S(2)}) collective-permute-start(bf16[256,1792]{1,0:T(8,128)(2,1)S(1)} %get-tuple-element.32), channel_id=1, source_target_pairs={{0,1},{1,2},{2,3},{3,0},{4,5},{5,6},{6,7},{7,4},{8,9},{9,10},{10,1... | collective-permute-start | bytes 2752520 | tf_op jit(solution)/shard_map/ppermute | solution.py:57
  26.9 21.3 %collective-permute-start.8 = (bf16[256,1792]{1,0:T(8,128)(2,1)}, bf16[256,1792]{1,0:T(8,128)(2,1)}, u32[]{:S(2)}, u32[]{:S(2)}) collective-permute-start(bf16[256,1792]{1,0:T(8,128)(2,1)} %get-tuple-element.33), channel_id=1, source_target_pairs={{0,3},{1,0},{2,1},{3,2},{4,7},{5,4},{6,5},{7,6},{8,11},{9,8},{10,9... | collective-permute-start | bytes 2752520 | tf_op jit(solution)/shard_map/ppermute | solution.py:57
  30.8 3.3 %copy-start.9 = (bf16[256,1792]{1,0:T(8,128)(2,1)}, bf16[256,1792]{1,0:T(8,128)(2,1)S(1)}, u32[]{:S(2)}) copy-start(bf16[256,1792]{1,0:T(8,128)(2,1)S(1)} %collective-permute-done.3.w3) | copy-start | bytes 2752516
  30.8 20.2 %collective-permute-start.6 = (bf16[64,4352]{1,0:T(8,128)(2,1)S(1)}, bf16[64,4352]{1,0:T(8,128)(2,1)S(1)}, u32[]{:S(2)}, u32[]{:S(2)}) collective-permute-start(bf16[64,4352]{1,0:T(8,128)(2,1)S(1)} %pad_maximum_fusion.refs_0_), channel_id=1, source_target_pairs={{0,16},{4,68},{8,24},{12,76},{16,0},{20,84},{24,8},{28,92},{32,48}... | collective-permute-start | bytes 1671176 | tf_op jit(solution)/shard_map/ppermute | solution.py:53
  34.1 17.1 %collective-permute-start.5 = (bf16[64,4352]{1,0:T(8,128)(2,1)S(1)}, bf16[64,4352]{1,0:T(8,128)(2,1)S(1)}, u32[]{:S(2)}, u32[]{:S(2)}) collective-permute-start(bf16[64,4352]{1,0:T(8,128)(2,1)S(1)} %pad_maximum_fusion.refs_0_), channel_id=1, source_target_pairs={{0,24},{4,100},{8,0},{12,108},{16,8},{20,116},{24,16},{28,124},{32... | collective-permute-start | bytes 1671176 | tf_op jit(solution)/shard_map/ppermute | solution.py:53
  35.1 16.4 %collective-permute-start.4 = (bf16[64,4352]{1,0:T(8,128)(2,1)S(1)}, bf16[64,4352]{1,0:T(8,128)(2,1)S(1)}, u32[]{:S(2)}, u32[]{:S(2)}) collective-permute-start(bf16[64,4352]{1,0:T(8,128)(2,1)S(1)} %pad_maximum_fusion.refs_0_), channel_id=1, source_target_pairs={{0,8},{4,36},{8,16},{12,44},{16,24},{20,52},{24,0},{28,60},{32,40}... | collective-permute-start | bytes 1671176 | tf_op jit(solution)/shard_map/ppermute | solution.py:53
  36.1 14.9 %all-to-all-start = ((bf16[32,16,224]{2,1,0:T(8,128)(2,1)}), bf16[32,16,224]{2,1,0:T(8,128)(2,1)}, u32[]{:S(2)}, u32[]{:S(2)}) async-start(bf16[32,16,224]{2,1,0:T(8,128)(2,1)} %get-tuple-element.34), calls=%async_computation | async-start | bytes 524288 | tf_op jit(solution)/shard_map/all_to_all | solution.py:684
  47.8 8.1 %collective-permute-start.11 = (bf16[64,4352]{1,0:T(8,128)(2,1)S(1)}, bf16[64,4352]{1,0:T(8,128)(2,1)S(1)}, u32[]{:S(2)}, u32[]{:S(2)}) collective-permute-start(bf16[64,4352]{1,0:T(8,128)(2,1)S(1)} %pad_maximum_fusion.refs_0_), channel_id=1, source_target_pairs={{0,4},{4,0},{8,12},{12,8},{16,20},{20,16},{24,28},{28,24},{32,36},... | collective-permute-start | bytes 1671176 | tf_op jit(solution)/shard_map/ppermute | solution.py:46
  51.0 5.0 %collective-permute-start.14 = (bf16[64,4352]{1,0:T(8,128)(2,1)S(1)}, bf16[64,4352]{1,0:T(8,128)(2,1)S(1)}, u32[]{:S(2)}, u32[]{:S(2)}) collective-permute-start(bf16[64,4352]{1,0:T(8,128)(2,1)S(1)} %collective-permute-done.6.refs_3_), channel_id=1, source_target_pairs={{0,4},{4,0},{8,12},{12,8},{16,20},{20,16},{24,28},{28,24},{32,36},... | collective-permute-start | bytes 1671176 | tf_op jit(solution)/shard_map/ppermute | solution.py:46
  51.1 4.8 %collective-permute-start.13 = (bf16[64,4352]{1,0:T(8,128)(2,1)S(1)}, bf16[64,4352]{1,0:T(8,128)(2,1)}, u32[]{:S(2)}, u32[]{:S(2)}) collective-permute-start(bf16[64,4352]{1,0:T(8,128)(2,1)S(1)} %collective-permute-done.5.refs_2_), channel_id=1, source_target_pairs={{0,4},{4,0},{8,12},{12,8},{16,20},{20,16},{24,28},{28,24},{32,36},... | collective-permute-start | bytes 1671176 | tf_op jit(solution)/shard_map/ppermute | solution.py:46
  51.5 4.4 %collective-permute-start.12 = (bf16[64,4352]{1,0:T(8,128)(2,1)S(1)}, bf16[64,4352]{1,0:T(8,128)(2,1)}, u32[]{:S(2)}, u32[]{:S(2)}) collective-permute-start(bf16[64,4352]{1,0:T(8,128)(2,1)S(1)} %collective-permute-done.4.refs_1_), channel_id=1, source_target_pairs={{0,4},{4,0},{8,12},{12,8},{16,20},{20,16},{24,28},{28,24},{32,36},... | collective-permute-start | bytes 1671176 | tf_op jit(solution)/shard_map/ppermute | solution.py:46
  54.6 6.1 %collective-permute-start.9 = (bf16[16,16,224]{2,1,0:T(8,128)(2,1)S(1)}, bf16[16,16,224]{2,1,0:T(8,128)(2,1)S(1)}, u32[]{:S(2)}, u32[]{:S(2)}) collective-permute-start(bf16[16,16,224]{2,1,0:T(8,128)(2,1)S(1)} %get-tuple-element.36), channel_id=1, source_target_pairs={{0,1},{1,0},{2,3},{3,2},{4,5},{5,4},{6,7},{7,6},{8,9},{9,8},{10,11... | collective-permute-start | bytes 344072 | tf_op jit(solution)/shard_map/ppermute | solution.py:68
  58.7 7.6 %collective-permute-start.15 = (bf16[16,16,224]{2,1,0:T(8,128)(2,1)S(1)}, bf16[16,16,224]{2,1,0:T(8,128)(2,1)S(1)}, u32[]{:S(2)}, u32[]{:S(2)}) collective-permute-start(bf16[16,16,224]{2,1,0:T(8,128)(2,1)S(1)} %get-tuple-element.37), channel_id=1, source_target_pairs={{0,3},{1,2},{2,1},{3,0},{4,7},{5,6},{6,5},{7,4},{8,11},{9,10},{10,... | collective-permute-start | bytes 344072 | tf_op jit(solution)/shard_map/ppermute | solution.py:68
  60.6 7.6 %collective-permute-start.10 = (bf16[16,16,224]{2,1,0:T(8,128)(2,1)S(1)}, bf16[16,16,224]{2,1,0:T(8,128)(2,1)S(1)}, u32[]{:S(2)}, u32[]{:S(2)}) collective-permute-start(bf16[16,16,224]{2,1,0:T(8,128)(2,1)S(1)} %add_convert_fusion.3), channel_id=1, source_target_pairs={{0,3},{1,2},{2,1},{3,0},{4,7},{5,6},{6,5},{7,4},{8,11},{9,10},{10,... | collective-permute-start | bytes 344072 | tf_op jit(solution)/shard_map/ppermute | solution.py:68
  66.4 5.0 %collective-permute-start.16 = (bf16[16,16,224]{2,1,0:T(8,128)(2,1)S(1)}, bf16[16,16,224]{2,1,0:T(8,128)(2,1)S(1)}, u32[]{:S(2)}, u32[]{:S(2)}) collective-permute-start(bf16[16,16,224]{2,1,0:T(8,128)(2,1)S(1)} %add_convert_fusion.1), channel_id=1, source_target_pairs={{0,1},{1,0},{2,3},{3,2},{4,5},{5,4},{6,7},{7,6},{8,9},{9,8},{10,11... | collective-permute-start | bytes 344072 | tf_op jit(solution)/shard_map/ppermute | solution.py:68
  100.5 3.8 %collective-permute-start.17 = (bf16[16,64,896]{2,1,0:T(8,128)(2,1)S(1)}, bf16[16,64,896]{2,1,0:T(8,128)(2,1)S(1)}, u32[]{:S(2)}, u32[]{:S(2)}) collective-permute-start(bf16[16,64,896]{2,1,0:T(8,128)(2,1)S(1)} %all_to_all.20.x_ref.own_hbm), channel_id=1, source_target_pairs={{0,4},{4,0},{8,12},{12,8},{16,20},{20,16},{24,28},{28,24},{32,36},... | collective-permute-start | bytes 5505032 | tf_op jit(solution)/shard_map/ppermute | solution.py:46
  105.6 7.9 %collective-permute-start.20 = (bf16[256,256]{1,0:T(8,128)(2,1)S(1)}, bf16[256,256]{1,0:T(8,128)(2,1)S(1)}, u32[]{:S(2)}, u32[]{:S(2)}) collective-permute-start(bf16[256,256]{1,0:T(8,128)(2,1)S(1)} %activate.1.a0), channel_id=1, source_target_pairs={{0,2},{1,3},{2,0},{3,1},{4,6},{5,7},{6,4},{7,5},{8,10},{9,11},{10,... | collective-permute-start | bytes 393224 | tf_op jit(solution)/shard_map/ppermute | solution.py:57
  106.7 7.5 %collective-permute-start.19 = (bf16[256,256]{1,0:T(8,128)(2,1)S(1)}, bf16[256,256]{1,0:T(8,128)(2,1)S(1)}, u32[]{:S(2)}, u32[]{:S(2)}) collective-permute-start(bf16[256,256]{1,0:T(8,128)(2,1)S(1)} %activate.1.a0), channel_id=1, source_target_pairs={{0,3},{1,0},{2,1},{3,2},{4,7},{5,4},{6,5},{7,6},{8,11},{9,8},{10,9... | collective-permute-start | bytes 393224 | tf_op jit(solution)/shard_map/ppermute | solution.py:57
  108.2 7.4 %collective-permute-start.18 = (bf16[256,256]{1,0:T(8,128)(2,1)S(1)}, bf16[256,256]{1,0:T(8,128)(2,1)S(1)}, u32[]{:S(2)}, u32[]{:S(2)}) collective-permute-start(bf16[256,256]{1,0:T(8,128)(2,1)S(1)} %activate.1.a0), channel_id=1, source_target_pairs={{0,1},{1,2},{2,3},{3,0},{4,5},{5,6},{6,7},{7,4},{8,9},{9,10},{10,1... | collective-permute-start | bytes 393224 | tf_op jit(solution)/shard_map/ppermute | solution.py:57
  115.5 5.3 %copy-start.1 = (bf16[16,64,896]{2,1,0:T(8,128)(2,1)S(1)}, bf16[16,64,896]{2,1,0:T(8,128)(2,1)}, u32[]{:S(2)}) copy-start(bf16[16,64,896]{2,1,0:T(8,128)(2,1)} %copy-done) | copy-start | bytes 5505028
  118.9 1.9 %collective-permute-start.21 = (bf16[128,1792]{1,0:T(8,128)(2,1)S(1)}, bf16[128,1792]{1,0:T(8,128)(2,1)S(1)}, u32[]{:S(2)}, u32[]{:S(2)}) collective-permute-start(bf16[128,1792]{1,0:T(8,128)(2,1)S(1)} %bitcast.33), channel_id=1, source_target_pairs={{0,4},{4,0},{8,12},{12,8},{16,20},{20,16},{24,28},{28,24},{32,36},... | collective-permute-start | bytes 1376264 | tf_op jit(solution)/shard_map/ppermute | solution.py:46
  (1 other events, 1.3 us)

commit v6 on v5

--- a/solution.py
+++ b/solution.py
@@ -267,16 +267,14 @@
 
 
 def project_kernel(*refs):
-    blocks, w_hbm = refs[:SIDE], refs[SIDE]
-    out_ref, places_ref, levels_ref, w_ref, b_ref, sems = refs[SIDE + 1 :]
+    blocks, w_ref = refs[:SIDE], refs[SIDE]
+    out_ref, places_ref, levels_ref, b_ref, sems = refs[SIDE + 1 :]
     depth = w_ref.shape[1]
-    copy = pltpu.make_async_copy(w_hbm, w_ref, sems.at[SIDE])
     moves = [
         pltpu.make_async_copy(block, b_ref.at[n], sems.at[n]) for n, block in enumerate(blocks)
     ]
     for move in moves:
         move.start()
-    copy.start()
     for move in moves:
         move.wait()
     blocks = [b_ref.at[n] for n in range(SIDE)]
@@ -287,7 +285,6 @@
             at = slice(j * rows, (j + 1) * rows)
             places_ref[i * SIDE + j] = block[at, depth : depth + 128]
             levels_ref[i * SIDE + j] = block[at, depth + 128 :]
-    copy.wait()
     made = lax.dot_general(left, w_ref[...], (((1,), (1,)), ((), ())), preferred_element_type=f32)
     made = made.astype(bf16)
     for n in range(CHIPS):
@@ -295,25 +292,24 @@
 
 
 def project(blocks, out_proj):
-    depth, columns = out_proj.shape
+    columns = out_proj.shape[1]
     rows = blocks[0].shape[0] // SIDE
     whole = pl.BlockSpec(memory_space=pltpu.VMEM)
     far = pl.BlockSpec(memory_space=pltpu.HBM)
     table = pltpu.HBM((CHIPS, rows, 128), bf16)
     return pl.pallas_call(
         project_kernel,
-        in_specs=[far] * (SIDE + 1),
+        in_specs=[far] * SIDE + [whole],
         out_specs=(whole,) * 3,
         out_shape=(jax.ShapeDtypeStruct((CHIPS, rows, columns), bf16), table, table),
         scratch_shapes=[
-            pltpu.VMEM((columns, depth), bf16),
             pltpu.VMEM((SIDE,) + blocks[0].shape, bf16),
-            pltpu.SemaphoreType.DMA((SIDE + 1,)),
+            pltpu.SemaphoreType.DMA((SIDE,)),
         ],
         compiler_params=pltpu.CompilerParams(vmem_limit_bytes=VMEM),
         cost_estimate=pl.CostEstimate(flops=5 * 10**8, bytes_accessed=4 * 10**6, transcendentals=0),
         name="project",
-    )(*blocks, distant(out_proj.T))
+    )(*blocks, out_proj.T)
 
 
 def of_core(parity, table, chip, mine_ref, other_ref):

time: 146 us -> 147 us (level)
  transfers between devices with their start and end apart: 23 -> 23, of which waited for: 14 -> 14; matrix products, arithmetic and copies ran while one was open for 0% -> 0% of each run, Pallas kernels for 17% -> 16%
where the time goes in v6:
time: 147 us; the launch traced here: 146 us
  blocking collectives  51.5 us (35%)
  Pallas kernels  32 us (22%)
  waiting for transfers between devices  30.5 us (21%)
  starting transfers between devices  29.4 us (20%)
  local copies, waits for them, and re-layouts  1.9 us (1%)
    all_to_all x2, blocking collectives, chip_exchange(): lax.all_to_all(value, 'dp', split_axis=0, concat_axis=0, axis_index_group...  42 us
    pallas_call x1, Pallas kernels, attend(): pl.pallas_call(attend_kernel, in_specs=[small, whole, whole] + [far] * 4...  13.9 us
    ppermute x6, waiting for transfers between devices, move_z(): lax.ppermute(value, 'tensor', [(z, (z + by) % PLANES) for z in range(PLAN...  13 us
    ppermute x6, starting transfers between devices, move_ring(): return lax.ppermute(value, 'dp', place_pairs(place))  10.4 us
    ppermute x6, starting transfers between devices, move_z(): lax.ppermute(value, 'tensor', [(z, (z + by) % PLANES) for z in range(PLAN...  10.2 us
    all_to_all x1, blocking collectives, spread_z(): lax.all_to_all(copies, 'tensor', split_axis=0, concat_axis=0, tiled=True)  9.5 us
    ppermute x4, waiting for transfers between devices, add(): moved = lax.ppermute(block, 'tensor', pairs)  8.81 us
    pallas_call x2, Pallas kernels, project(): pl.pallas_call(project_kernel, in_specs=[far] * SIDE + [whole], out_specs...  5.34 us
  transfers between devices with their start and end apart: 23, of which 14 were waited for; matrix products, arithmetic and copies ran while one was open for 0% of the time, Pallas kernels for 16%

profile of v6, /device:TPU:0, one launch (start us, length us, event | category | flops | bytes accessed | tf_op | source)
XLA Modules:
  0.0 146.2 jit_solution(2913969933388236593)
XLA Ops:
  0.0 1.3 cut.1
  1.3 4.0 %collective-permute-start.3 = (bf16[256,1792]{1,0:T(8,128)(2,1)S(1)}, bf16[256,1792]{1,0:T(8,128)(2,1)S(1)}, u32[]{:S(2)}, u32[]{:S(2)}) collective-permute-start(bf16[256,1792]{1,0:T(8,128)(2,1)S(1)} %cut.1), channel_id=1, source_target_pairs={{0,2},{1,3},{2,0},{3,1},{4,6},{5,7},{6,4},{7,5},{8,10},{9,11},{10,... | collective-permute-start | bytes 2752520 | tf_op jit(solution)/shard_map/ppermute | solution.py:57
  5.3 13.9 %attend.1 = (bf16[16,4352]{1,0:T(8,128)(2,1)S(1)}, bf16[16,128]{1,0:T(8,128)(2,1)S(1)}, bf16[32,16,224]{2,1,0:T(8,128)(2,1)S(1)}, bf16[256,1792]{1,0:T(8,128)(2,1)}, bf16[256,1792]{1,0:T(8,128)(2,1)}) custom-call(s32[16]{0:T(128)S(1)} %copy-done.10, bf16[16,32,512]{2,1,0:T(8,128)(2,1)S(1)} %copy-done.3, bf16[16,32,64]{2,1,0:T(8,128)(2,1)S(1)} %copy-done.6, ...), custom_call_target="tpu_custom_call" | custom-call | flops 1073741824 | bytes 18874368 | tf_op jit(solution)/shard_map/attend/pallas_call | solution.py:236
  19.3 3.1 %collective-permute-start.2 = (bf16[16,4352]{1,0:T(8,128)(2,1)S(1)}, bf16[16,4352]{1,0:T(8,128)(2,1)S(1)}, u32[]{:S(2)}, u32[]{:S(2)}) collective-permute-start(bf16[16,4352]{1,0:T(8,128)(2,1)S(1)} %get-tuple-element.30), channel_id=1, source_target_pairs={{0,64},{4,20},{8,72},{12,28},{16,80},{20,4},{24,88},{28,12},{32,96... | collective-permute-start | bytes 417800 | tf_op jit(solution)/shard_map/ppermute | solution.py:53
  22.4 1.1 collective-permute-start.1
  25.9 1.7 %collective-permute-start.8 = (bf16[256,1792]{1,0:T(8,128)(2,1)}, bf16[256,1792]{1,0:T(8,128)(2,1)}, u32[]{:S(2)}, u32[]{:S(2)}) collective-permute-start(bf16[256,1792]{1,0:T(8,128)(2,1)} %get-tuple-element.33), channel_id=1, source_target_pairs={{0,3},{1,0},{2,1},{3,2},{4,7},{5,4},{6,5},{7,6},{8,11},{9,8},{10,9... | collective-permute-start | bytes 2752520 | tf_op jit(solution)/shard_map/ppermute | solution.py:57
  27.6 2.1 %collective-permute-done = bf16[16,4352]{1,0:T(8,128)(2,1)S(1)} collective-permute-done((bf16[16,4352]{1,0:T(8,128)(2,1)S(1)}, bf16[16,4352]{1,0:T(8,128)(2,1)S(1)}, u32[]{:S(2)}, u32[]{:S(2)}) %collective-permute-start) | collective-permute-done | bytes 139296 | tf_op jit(solution)/shard_map/ppermute | solution.py:53
  30.8 3.2 %collective-permute-start.6 = (bf16[64,4352]{1,0:T(8,128)(2,1)S(1)}, bf16[64,4352]{1,0:T(8,128)(2,1)S(1)}, u32[]{:S(2)}, u32[]{:S(2)}) collective-permute-start(bf16[64,4352]{1,0:T(8,128)(2,1)S(1)} %pad_maximum_fusion.refs_0_), channel_id=1, source_target_pairs={{0,16},{4,68},{8,24},{12,76},{16,0},{20,84},{24,8},{28,92},{32,48}... | collective-permute-start | bytes 1671176 | tf_op jit(solution)/shard_map/ppermute | solution.py:53
  36.0 4.6 %all-to-all-start = ((bf16[32,16,224]{2,1,0:T(8,128)(2,1)}), bf16[32,16,224]{2,1,0:T(8,128)(2,1)}, u32[]{:S(2)}, u32[]{:S(2)}) async-start(bf16[32,16,224]{2,1,0:T(8,128)(2,1)} %copy-done.4), calls=%async_computation | async-start | bytes 524288 | tf_op jit(solution)/shard_map/all_to_all | solution.py:680
  40.6 6.4 %collective-permute-done.7.w1 = bf16[256,1792]{1,0:T(8,128)(2,1)} collective-permute-done((bf16[256,1792]{1,0:T(8,128)(2,1)}, bf16[256,1792]{1,0:T(8,128)(2,1)}, u32[]{:S(2)}, u32[]{:S(2)}) %collective-permute-start.7) | collective-permute-done | bytes 917536 | tf_op jit(solution)/shard_map/ppermute | solution.py:57
  47.2 3.7 %all-to-all-done = bf16[32,16,224]{2,1,0:T(8,128)(2,1)} async-done(((bf16[32,16,224]{2,1,0:T(8,128)(2,1)}), bf16[32,16,224]{2,1,0:T(8,128)(2,1)}, u32[]{:S(2)}, u32[]{:S(2)}) %all-to-all-start) | async-done | bytes 229408 | tf_op jit(solution)/shard_map/all_to_all | solution.py:680
  51.8 2.5 %project.2 = (bf16[16,16,224]{2,1,0:T(8,128)(2,1)S(1)}, bf16[16,16,128]{2,1,0:T(8,128)(2,1)}, bf16[16,16,128]{2,1,0:T(8,128)(2,1)}) custom-call(bf16[64,4352]{1,0:T(8,128)(2,1)S(1)} %pad_maximum_fusion.refs_0_, bf16[64,4352]{1,0:T(8,128)(2,1)} %collective-permute-done.4.refs_1_, bf16[64,4352]{1,0:T(8,128)(2,1)S(1)} %collective-permute-done.5.refs_2_, ...), custom_call_target="tpu_custom_call" | custom-call | flops 500000000 | bytes 4000000 | tf_op jit(solution)/shard_map/project/pallas_call | solution.py:300
  54.3 1.3 collective-permute-start.9
  55.7 2.9 %project.3 = (bf16[16,16,224]{2,1,0:T(8,128)(2,1)S(1)}, bf16[16,16,128]{2,1,0:T(8,128)(2,1)}, bf16[16,16,128]{2,1,0:T(8,128)(2,1)}) custom-call(bf16[64,4352]{1,0:T(8,128)(2,1)} %collective-permute-done.11.refs_0_, bf16[64,4352]{1,0:T(8,128)(2,1)} %collective-permute-done.12.refs_1_, bf16[64,4352]{1,0:T(8,128)(2,1)} %collective-permute-done.13.refs_2_, ...), custom_call_target="tpu_custom_call" | custom-call | flops 500000000 | bytes 4000000 | tf_op jit(solution)/shard_map/project/pallas_call | solution.py:300
  59.1 1.2 collective-permute-done.9
  60.4 1.6 %collective-permute-start.10 = (bf16[16,16,224]{2,1,0:T(8,128)(2,1)S(1)}, bf16[16,16,224]{2,1,0:T(8,128)(2,1)S(1)}, u32[]{:S(2)}, u32[]{:S(2)}) collective-permute-start(bf16[16,16,224]{2,1,0:T(8,128)(2,1)S(1)} %add_convert_fusion.3), channel_id=1, source_target_pairs={{0,3},{1,2},{2,1},{3,0},{4,7},{5,6},{6,5},{7,4},{8,11},{9,10},{10,... | collective-permute-start | bytes 344072 | tf_op jit(solution)/shard_map/ppermute | solution.py:68
  62.0 4.2 %collective-permute-done.15 = bf16[16,16,224]{2,1,0:T(8,128)(2,1)S(1)} collective-permute-done((bf16[16,16,224]{2,1,0:T(8,128)(2,1)S(1)}, bf16[16,16,224]{2,1,0:T(8,128)(2,1)S(1)}, u32[]{:S(2)}, u32[]{:S(2)}) %collective-permute-start.15) | collective-permute-done | bytes 114720 | tf_op jit(solution)/shard_map/ppermute | solution.py:68
  66.3 1.9 %collective-permute-done.10 = bf16[16,16,224]{2,1,0:T(8,128)(2,1)S(1)} collective-permute-done((bf16[16,16,224]{2,1,0:T(8,128)(2,1)S(1)}, bf16[16,16,224]{2,1,0:T(8,128)(2,1)S(1)}, u32[]{:S(2)}, u32[]{:S(2)}) %collective-permute-start.10) | collective-permute-done | bytes 114720 | tf_op jit(solution)/shard_map/ppermute | solution.py:68
  68.3 1.5 %gate_table.1.gates_ref = f32[256,128]{1,0:T(8,128)S(1)} custom-call(s32[32]{0:T(128)S(1)} %broadcast_select_fusion.table, bf16[16,16,128]{2,1,0:T(8,128)(2,1)} %get-tuple-element.39.places_ref, bf16[16,16,128]{2,1,0:T(8,128)(2,1)} %get-tuple-element.40.places_other, bf16[16,16,128]{2,1,0:T(8,128)(2,1)} %get-tuple-element.41.levels_ref, ...), custom_call_target="tpu_custom_call" | custom-call | flops 100000000 | bytes 1000000 | tf_op jit(solution)/shard_map/gate_table/pallas_call | solution.py:365
  69.8 1.5 %collective-permute-done.16 = bf16[16,16,224]{2,1,0:T(8,128)(2,1)S(1)} collective-permute-done((bf16[16,16,224]{2,1,0:T(8,128)(2,1)S(1)}, bf16[16,16,224]{2,1,0:T(8,128)(2,1)S(1)}, u32[]{:S(2)}, u32[]{:S(2)}) %collective-permute-start.16) | collective-permute-done | bytes 114720 | tf_op jit(solution)/shard_map/ppermute | solution.py:68
  71.3 1.6 %select.39 = bf16[16,64,896]{2,1,0:T(8,128)(2,1)S(1)} custom-call(s32[32]{0:T(128)S(1)} %broadcast_select_fusion.table, bf16[16,16,224]{2,1,0:T(8,128)(2,1)S(1)} %add_convert_fusion.2.sums_ref, bf16[16,16,224]{2,1,0:T(8,128)(2,1)S(1)} %add_convert_fusion.sums_other, bf16[16,2,16,224]{3,2,1,0:T(8,128)(2,1)} %bitcast.4.res_ref, ...), custom_call_target="tpu_custom_call" | custom-call | flops 1000000000 | bytes 6000000 | tf_op jit(solution)/shard_map/select/pallas_call | solution.py:409
  72.9 27.5 %all_to_all.20.x_ref.own_hbm = bf16[16,64,896]{2,1,0:T(8,128)(2,1)S(1)} all-to-all(bf16[16,64,896]{2,1,0:T(8,128)(2,1)S(1)} %select.39), channel_id=1, replica_groups={{0,8,16,24,32,40,48,56,64,72,80,88,96,104,112,120},{4,12,20,28,36,44,52..., dimensions={0} | all-to-all | bytes 3670016 | tf_op jit(solution)/shard_map/all_to_all | solution.py:78
  100.4 3.2 %up.1 = (f32[256,512]{1,0:T(8,128)S(1)}, bf16[16,224,512]{2,1,0:T(8,128)(2,1)S(1)}) custom-call(bf16[16,64,896]{2,1,0:T(8,128)(2,1)S(1)} %all_to_all.20.x_ref.own_hbm, bf16[16,2,224,256]{3,2,1,0:T(8,128)(2,1)} %bitcast.30, bf16[16,2,224,256]{3,2,1,0:T(8,128)(2,1)} %bitcast.31), custom_call_target="tpu_custom_call" | custom-call | flops 939524096 | bytes 9000000 | tf_op jit(solution)/shard_map/up/pallas_call | solution.py:471
  104.2 1.3 activate.1.a0
  105.5 1.5 %collective-permute-start.20 = (bf16[256,256]{1,0:T(8,128)(2,1)S(1)}, bf16[256,256]{1,0:T(8,128)(2,1)S(1)}, u32[]{:S(2)}, u32[]{:S(2)}) collective-permute-start(bf16[256,256]{1,0:T(8,128)(2,1)S(1)} %activate.1.a0), channel_id=1, source_target_pairs={{0,2},{1,3},{2,0},{3,1},{4,6},{5,7},{6,4},{7,5},{8,10},{9,11},{10,... | collective-permute-start | bytes 393224 | tf_op jit(solution)/shard_map/ppermute | solution.py:57
  107.0 1.1 collective-permute-start.19
  109.0 4.4 %collective-permute-done.20.a3 = bf16[256,256]{1,0:T(8,128)(2,1)S(1)} collective-permute-done((bf16[256,256]{1,0:T(8,128)(2,1)S(1)}, bf16[256,256]{1,0:T(8,128)(2,1)S(1)}, u32[]{:S(2)}, u32[]{:S(2)}) %collective-permute-start.20) | collective-permute-done | bytes 131104 | tf_op jit(solution)/shard_map/ppermute | solution.py:57
  113.5 1.5 %collective-permute-done.19.a2 = bf16[256,256]{1,0:T(8,128)(2,1)S(1)} collective-permute-done((bf16[256,256]{1,0:T(8,128)(2,1)S(1)}, bf16[256,256]{1,0:T(8,128)(2,1)S(1)}, u32[]{:S(2)}, u32[]{:S(2)}) %collective-permute-start.19) | collective-permute-done | bytes 131104 | tf_op jit(solution)/shard_map/ppermute | solution.py:57
  115.5 3.3 %down.1.y_ref = bf16[256,1792]{1,0:T(8,128)(2,1)S(1)} custom-call(bf16[256,256]{1,0:T(8,128)(2,1)S(1)} %activate.1.a0, bf16[256,256]{1,0:T(8,128)(2,1)S(1)} %collective-permute-done.18.a1, bf16[256,256]{1,0:T(8,128)(2,1)S(1)} %collective-permute-done.19.a2, bf16[256,256]{1,0:T(8,128)(2,1)S(1)} %collective-permute-done.20.a3, bf16[256,7168]{1,0:T(8,128)(2,1)} %bitcast.29, ...), custom_call_target="tpu_custom_call" | custom-call | flops 939524096 | bytes 6000000 | tf_op jit(solution)/shard_map/down/pallas_call | solution.py:562
  118.9 1.8 %collective-permute-done.21.received_ref = bf16[128,1792]{1,0:T(8,128)(2,1)S(1)} collective-permute-done((bf16[128,1792]{1,0:T(8,128)(2,1)S(1)}, bf16[128,1792]{1,0:T(8,128)(2,1)S(1)}, u32[]{:S(2)}, u32[]{:S(2)}) %collective-permute-start.21) | collective-permute-done | bytes 458784 | tf_op jit(solution)/shard_map/ppermute | solution.py:46
  121.3 14.5 %all_to_all.21 = bf16[16,8,1792]{2,1,0:T(8,128)(2,1)S(1)} all-to-all(bf16[16,8,1792]{2,1,0:T(8,128)(2,1)S(1)} %bitcast.23), channel_id=1, replica_groups={{0,8,16,24,32,40,48,56,64,72,80,88,96,104,112,120},{4,12,20,28,36,44,52..., dimensions={0} | all-to-all | bytes 917504 | tf_op jit(solution)/shard_map/all_to_all | solution.py:78
  136.0 9.5 %all_to_all.22 = bf16[4,16,1792]{2,1,0:T(8,128)(2,1)S(1)} all-to-all(bf16[4,16,1792]{2,1,0:T(8,128)(2,1)S(1)} %broadcast_in_dim.2), channel_id=1, replica_groups=mesh['dp'=32,'tensor'=4] {'tensor'}, dimensions={0} | all-to-all | bytes 458752 | tf_op jit(solution)/shard_map/all_to_all | solution.py:62
  (69 shorter events, 10.9 us)
Async XLA Ops:
  0.0 5.3 %copy-start.3 = (bf16[16,32,512]{2,1,0:T(8,128)(2,1)S(1)}, bf16[16,32,512]{2,1,0:T(8,128)(2,1)}, u32[]{:S(2)}) copy-start(bf16[16,32,512]{2,1,0:T(8,128)(2,1)} %q_ref.1) | copy-start | bytes 1572868
  0.0 5.3 %copy-start.5 = (bf16[16,7168]{1,0:T(8,128)(2,1)S(1)}, bf16[16,7168]{1,0:T(8,128)(2,1)}, u32[]{:S(2)}) copy-start(bf16[16,7168]{1,0:T(8,128)(2,1)} %res_ref.1) | copy-start | bytes 688132
  0.0 5.3 %copy-start.6 = (bf16[16,32,64]{2,1,0:T(8,128)(2,1)S(1)}, bf16[16,32,64]{2,1,0:T(8,128)(2,1)}, u32[]{:S(2)}) copy-start(bf16[16,32,64]{2,1,0:T(8,128)(2,1)} %qr_ref.1) | copy-start | bytes 196612
  0.0 5.3 %copy-start.7 = (s32[16,8]{0,1:T(8,128)S(1)}, s32[16,8]{0,1:T(8,128)}, u32[]{:S(2)}) copy-start(s32[16,8]{0,1:T(8,128)} %param.26) | copy-start | bytes 1540
  0.0 5.3 %copy-start.8 = (s32[16,8]{0,1:T(8,128)S(1)}, s32[16,8]{0,1:T(8,128)}, u32[]{:S(2)}) copy-start(s32[16,8]{0,1:T(8,128)} %param.27) | copy-start | bytes 1540
  0.0 5.3 %copy-start.9 = (s32[16,4]{0,1:T(4,128)S(1)}, s32[16,4]{0,1:T(4,128)}, u32[]{:S(2)}) copy-start(s32[16,4]{0,1:T(4,128)} %param.25) | copy-start | bytes 772
  0.0 5.3 %copy-start.10 = (s32[16]{0:T(128)S(1)}, s32[16]{0:T(128)}, u32[]{:S(2)}) copy-start(s32[16]{0:T(128)} %lengths.1) | copy-start | bytes 196
  1.3 28.5 %collective-permute-start.3 = (bf16[256,1792]{1,0:T(8,128)(2,1)S(1)}, bf16[256,1792]{1,0:T(8,128)(2,1)S(1)}, u32[]{:S(2)}, u32[]{:S(2)}) collective-permute-start(bf16[256,1792]{1,0:T(8,128)(2,1)S(1)} %cut.1), channel_id=1, source_target_pairs={{0,2},{1,3},{2,0},{3,1},{4,6},{5,7},{6,4},{7,5},{8,10},{9,11},{10,... | collective-permute-start | bytes 2752520 | tf_op jit(solution)/shard_map/ppermute | solution.py:57
  5.3 46.5 %copy-start = (bf16[4096,224]{0,1:T(8,128)(2,1)S(1)}, bf16[4096,224]{0,1:T(8,128)(2,1)}, u32[]{:S(2)}) copy-start(bf16[4096,224]{0,1:T(8,128)(2,1)} %param.21) | copy-start | bytes 5505028
  19.3 14.7 %copy-start.4 = (bf16[32,16,224]{2,1,0:T(8,128)(2,1)}, bf16[32,16,224]{2,1,0:T(8,128)(2,1)S(1)}, u32[]{:S(2)}) copy-start(bf16[32,16,224]{2,1,0:T(8,128)(2,1)S(1)} %get-tuple-element.34) | copy-start | bytes 688132
  19.3 6.6 %collective-permute-start.2 = (bf16[16,4352]{1,0:T(8,128)(2,1)S(1)}, bf16[16,4352]{1,0:T(8,128)(2,1)S(1)}, u32[]{:S(2)}, u32[]{:S(2)}) collective-permute-start(bf16[16,4352]{1,0:T(8,128)(2,1)S(1)} %get-tuple-element.30), channel_id=1, source_target_pairs={{0,64},{4,20},{8,72},{12,28},{16,80},{20,4},{24,88},{28,12},{32,96... | collective-permute-start | bytes 417800 | tf_op jit(solution)/shard_map/ppermute | solution.py:53
  22.4 5.3 %collective-permute-start.1 = (bf16[16,4352]{1,0:T(8,128)(2,1)S(1)}, bf16[16,4352]{1,0:T(8,128)(2,1)S(1)}, u32[]{:S(2)}, u32[]{:S(2)}) collective-permute-start(bf16[16,4352]{1,0:T(8,128)(2,1)S(1)} %get-tuple-element.30), channel_id=1, source_target_pairs={{0,96},{4,28},{8,104},{12,4},{16,112},{20,12},{24,120},{28,20},{32... | collective-permute-start | bytes 417800 | tf_op jit(solution)/shard_map/ppermute | solution.py:53
  23.5 6.3 %collective-permute-start = (bf16[16,4352]{1,0:T(8,128)(2,1)S(1)}, bf16[16,4352]{1,0:T(8,128)(2,1)S(1)}, u32[]{:S(2)}, u32[]{:S(2)}) collective-permute-start(bf16[16,4352]{1,0:T(8,128)(2,1)S(1)} %get-tuple-element.30), channel_id=1, source_target_pairs={{0,32},{4,12},{8,40},{12,20},{16,48},{20,28},{24,56},{28,4},{32,64... | collective-permute-start | bytes 417800 | tf_op jit(solution)/shard_map/ppermute | solution.py:53
  24.4 22.7 %collective-permute-start.7 = (bf16[256,1792]{1,0:T(8,128)(2,1)}, bf16[256,1792]{1,0:T(8,128)(2,1)}, u32[]{:S(2)}, u32[]{:S(2)}) collective-permute-start(bf16[256,1792]{1,0:T(8,128)(2,1)} %get-tuple-element.32), channel_id=1, source_target_pairs={{0,1},{1,2},{2,3},{3,0},{4,5},{5,6},{6,7},{7,4},{8,9},{9,10},{10,1... | collective-permute-start | bytes 2752520 | tf_op jit(solution)/shard_map/ppermute | solution.py:57
  25.9 21.3 %collective-permute-start.8 = (bf16[256,1792]{1,0:T(8,128)(2,1)}, bf16[256,1792]{1,0:T(8,128)(2,1)}, u32[]{:S(2)}, u32[]{:S(2)}) collective-permute-start(bf16[256,1792]{1,0:T(8,128)(2,1)} %get-tuple-element.33), channel_id=1, source_target_pairs={{0,3},{1,0},{2,1},{3,2},{4,7},{5,4},{6,5},{7,6},{8,11},{9,8},{10,9... | collective-permute-start | bytes 2752520 | tf_op jit(solution)/shard_map/ppermute | solution.py:57
  30.8 20.1 %collective-permute-start.6 = (bf16[64,4352]{1,0:T(8,128)(2,1)S(1)}, bf16[64,4352]{1,0:T(8,128)(2,1)S(1)}, u32[]{:S(2)}, u32[]{:S(2)}) collective-permute-start(bf16[64,4352]{1,0:T(8,128)(2,1)S(1)} %pad_maximum_fusion.refs_0_), channel_id=1, source_target_pairs={{0,16},{4,68},{8,24},{12,76},{16,0},{20,84},{24,8},{28,92},{32,48}... | collective-permute-start | bytes 1671176 | tf_op jit(solution)/shard_map/ppermute | solution.py:53
  34.0 17.1 %collective-permute-start.5 = (bf16[64,4352]{1,0:T(8,128)(2,1)S(1)}, bf16[64,4352]{1,0:T(8,128)(2,1)S(1)}, u32[]{:S(2)}, u32[]{:S(2)}) collective-permute-start(bf16[64,4352]{1,0:T(8,128)(2,1)S(1)} %pad_maximum_fusion.refs_0_), channel_id=1, source_target_pairs={{0,24},{4,100},{8,0},{12,108},{16,8},{20,116},{24,16},{28,124},{32... | collective-permute-start | bytes 1671176 | tf_op jit(solution)/shard_map/ppermute | solution.py:53
  35.0 16.4 %collective-permute-start.4 = (bf16[64,4352]{1,0:T(8,128)(2,1)S(1)}, bf16[64,4352]{1,0:T(8,128)(2,1)}, u32[]{:S(2)}, u32[]{:S(2)}) collective-permute-start(bf16[64,4352]{1,0:T(8,128)(2,1)S(1)} %pad_maximum_fusion.refs_0_), channel_id=1, source_target_pairs={{0,8},{4,36},{8,16},{12,44},{16,24},{20,52},{24,0},{28,60},{32,40}... | collective-permute-start | bytes 1671176 | tf_op jit(solution)/shard_map/ppermute | solution.py:53
  36.0 14.9 %all-to-all-start = ((bf16[32,16,224]{2,1,0:T(8,128)(2,1)}), bf16[32,16,224]{2,1,0:T(8,128)(2,1)}, u32[]{:S(2)}, u32[]{:S(2)}) async-start(bf16[32,16,224]{2,1,0:T(8,128)(2,1)} %copy-done.4), calls=%async_computation | async-start | bytes 524288 | tf_op jit(solution)/shard_map/all_to_all | solution.py:680
  47.1 8.6 %collective-permute-start.11 = (bf16[64,4352]{1,0:T(8,128)(2,1)S(1)}, bf16[64,4352]{1,0:T(8,128)(2,1)}, u32[]{:S(2)}, u32[]{:S(2)}) collective-permute-start(bf16[64,4352]{1,0:T(8,128)(2,1)S(1)} %pad_maximum_fusion.refs_0_), channel_id=1, source_target_pairs={{0,4},{4,0},{8,12},{12,8},{16,20},{20,16},{24,28},{28,24},{32,36},... | collective-permute-start | bytes 1671176 | tf_op jit(solution)/shard_map/ppermute | solution.py:46
  50.9 4.8 %collective-permute-start.14 = (bf16[64,4352]{1,0:T(8,128)(2,1)S(1)}, bf16[64,4352]{1,0:T(8,128)(2,1)}, u32[]{:S(2)}, u32[]{:S(2)}) collective-permute-start(bf16[64,4352]{1,0:T(8,128)(2,1)S(1)} %collective-permute-done.6.refs_3_), channel_id=1, source_target_pairs={{0,4},{4,0},{8,12},{12,8},{16,20},{20,16},{24,28},{28,24},{32,36},... | collective-permute-start | bytes 1671176 | tf_op jit(solution)/shard_map/ppermute | solution.py:46
  51.0 4.7 %collective-permute-start.13 = (bf16[64,4352]{1,0:T(8,128)(2,1)S(1)}, bf16[64,4352]{1,0:T(8,128)(2,1)}, u32[]{:S(2)}, u32[]{:S(2)}) collective-permute-start(bf16[64,4352]{1,0:T(8,128)(2,1)S(1)} %collective-permute-done.5.refs_2_), channel_id=1, source_target_pairs={{0,4},{4,0},{8,12},{12,8},{16,20},{20,16},{24,28},{28,24},{32,36},... | collective-permute-start | bytes 1671176 | tf_op jit(solution)/shard_map/ppermute | solution.py:46
  51.4 4.3 %collective-permute-start.12 = (bf16[64,4352]{1,0:T(8,128)(2,1)}, bf16[64,4352]{1,0:T(8,128)(2,1)}, u32[]{:S(2)}, u32[]{:S(2)}) collective-permute-start(bf16[64,4352]{1,0:T(8,128)(2,1)} %collective-permute-done.4.refs_1_), channel_id=1, source_target_pairs={{0,4},{4,0},{8,12},{12,8},{16,20},{20,16},{24,28},{28,24},{32,36},... | collective-permute-start | bytes 1671176 | tf_op jit(solution)/shard_map/ppermute | solution.py:46
  54.3 6.1 %collective-permute-start.9 = (bf16[16,16,224]{2,1,0:T(8,128)(2,1)S(1)}, bf16[16,16,224]{2,1,0:T(8,128)(2,1)S(1)}, u32[]{:S(2)}, u32[]{:S(2)}) collective-permute-start(bf16[16,16,224]{2,1,0:T(8,128)(2,1)S(1)} %get-tuple-element.36), channel_id=1, source_target_pairs={{0,1},{1,0},{2,3},{3,2},{4,5},{5,4},{6,7},{7,6},{8,9},{9,8},{10,11... | collective-permute-start | bytes 344072 | tf_op jit(solution)/shard_map/ppermute | solution.py:68
  58.6 7.6 %collective-permute-start.15 = (bf16[16,16,224]{2,1,0:T(8,128)(2,1)S(1)}, bf16[16,16,224]{2,1,0:T(8,128)(2,1)S(1)}, u32[]{:S(2)}, u32[]{:S(2)}) collective-permute-start(bf16[16,16,224]{2,1,0:T(8,128)(2,1)S(1)} %get-tuple-element.37), channel_id=1, source_target_pairs={{0,3},{1,2},{2,1},{3,0},{4,7},{5,6},{6,5},{7,4},{8,11},{9,10},{10,... | collective-permute-start | bytes 344072 | tf_op jit(solution)/shard_map/ppermute | solution.py:68
  60.4 7.8 %collective-permute-start.10 = (bf16[16,16,224]{2,1,0:T(8,128)(2,1)S(1)}, bf16[16,16,224]{2,1,0:T(8,128)(2,1)S(1)}, u32[]{:S(2)}, u32[]{:S(2)}) collective-permute-start(bf16[16,16,224]{2,1,0:T(8,128)(2,1)S(1)} %add_convert_fusion.3), channel_id=1, source_target_pairs={{0,3},{1,2},{2,1},{3,0},{4,7},{5,6},{6,5},{7,4},{8,11},{9,10},{10,... | collective-permute-start | bytes 344072 | tf_op jit(solution)/shard_map/ppermute | solution.py:68
  66.3 5.0 %collective-permute-start.16 = (bf16[16,16,224]{2,1,0:T(8,128)(2,1)S(1)}, bf16[16,16,224]{2,1,0:T(8,128)(2,1)S(1)}, u32[]{:S(2)}, u32[]{:S(2)}) collective-permute-start(bf16[16,16,224]{2,1,0:T(8,128)(2,1)S(1)} %add_convert_fusion.1), channel_id=1, source_target_pairs={{0,1},{1,0},{2,3},{3,2},{4,5},{5,4},{6,7},{7,6},{8,9},{9,8},{10,11... | collective-permute-start | bytes 344072 | tf_op jit(solution)/shard_map/ppermute | solution.py:68
  100.4 3.8 %collective-permute-start.17 = (bf16[16,64,896]{2,1,0:T(8,128)(2,1)S(1)}, bf16[16,64,896]{2,1,0:T(8,128)(2,1)S(1)}, u32[]{:S(2)}, u32[]{:S(2)}) collective-permute-start(bf16[16,64,896]{2,1,0:T(8,128)(2,1)S(1)} %all_to_all.20.x_ref.own_hbm), channel_id=1, source_target_pairs={{0,4},{4,0},{8,12},{12,8},{16,20},{20,16},{24,28},{28,24},{32,36},... | collective-permute-start | bytes 5505032 | tf_op jit(solution)/shard_map/ppermute | solution.py:46
  105.5 7.9 %collective-permute-start.20 = (bf16[256,256]{1,0:T(8,128)(2,1)S(1)}, bf16[256,256]{1,0:T(8,128)(2,1)S(1)}, u32[]{:S(2)}, u32[]{:S(2)}) collective-permute-start(bf16[256,256]{1,0:T(8,128)(2,1)S(1)} %activate.1.a0), channel_id=1, source_target_pairs={{0,2},{1,3},{2,0},{3,1},{4,6},{5,7},{6,4},{7,5},{8,10},{9,11},{10,... | collective-permute-start | bytes 393224 | tf_op jit(solution)/shard_map/ppermute | solution.py:57
  107.0 8.0 %collective-permute-start.19 = (bf16[256,256]{1,0:T(8,128)(2,1)S(1)}, bf16[256,256]{1,0:T(8,128)(2,1)S(1)}, u32[]{:S(2)}, u32[]{:S(2)}) collective-permute-start(bf16[256,256]{1,0:T(8,128)(2,1)S(1)} %activate.1.a0), channel_id=1, source_target_pairs={{0,3},{1,0},{2,1},{3,2},{4,7},{5,4},{6,5},{7,6},{8,11},{9,8},{10,9... | collective-permute-start | bytes 393224 | tf_op jit(solution)/shard_map/ppermute | solution.py:57
  108.1 7.4 %collective-permute-start.18 = (bf16[256,256]{1,0:T(8,128)(2,1)S(1)}, bf16[256,256]{1,0:T(8,128)(2,1)S(1)}, u32[]{:S(2)}, u32[]{:S(2)}) collective-permute-start(bf16[256,256]{1,0:T(8,128)(2,1)S(1)} %activate.1.a0), channel_id=1, source_target_pairs={{0,1},{1,2},{2,3},{3,0},{4,5},{5,6},{6,7},{7,4},{8,9},{9,10},{10,1... | collective-permute-start | bytes 393224 | tf_op jit(solution)/shard_map/ppermute | solution.py:57
  118.8 1.9 %collective-permute-start.21 = (bf16[128,1792]{1,0:T(8,128)(2,1)S(1)}, bf16[128,1792]{1,0:T(8,128)(2,1)S(1)}, u32[]{:S(2)}, u32[]{:S(2)}) collective-permute-start(bf16[128,1792]{1,0:T(8,128)(2,1)S(1)} %bitcast.33), channel_id=1, source_target_pairs={{0,4},{4,0},{8,12},{12,8},{16,20},{20,16},{24,28},{28,24},{32,36},... | collective-permute-start | bytes 1376264 | tf_op jit(solution)/shard_map/ppermute | solution.py:46
  (3 other events, 7.5 us)
